TPU v7x, 32 devices: a whole 2x2x4 slice. The times are simulated.
32 devices in a mesh: groups: 2 (over y), row: 4 (over x, core), col: 4 (over z).
Axes of the slice: x: 2, y: 2, z: 4, core: 2. Of those that a mesh axis runs over, the one named last changes fastest.
Arguments:
- queries: bfloat16 [4096, 512], P(('groups', 'row', 'col')), parts along dimension 0, may hold values from -6 to 6
- keys: bfloat16 [4096, 512], P(('groups', 'col', 'row')), parts along dimension 0, may hold values from -6 to 6
- values: bfloat16 [4096, 512], P(('groups', 'col', 'row')), parts along dimension 0, may hold values from -6 to 6
- outputs: bfloat16 [4096, 512], P(('groups', 'row', 'col')), parts along dimension 0, may hold values from -6 to 6
- out_grad: bfloat16 [4096, 512], P(('groups', 'row', 'col')), parts along dimension 0, may hold values from -192 to 192
- log_norm: float32 [8, 4096], P(None, ('groups', 'row', 'col')), parts along dimension 1, may hold values from 7 to 9
- contacts: int32 [32, 12], P(('groups', 'row')), parts along dimension 0, may hold values from 0 to 15, as said below
Outputs:
- query_grads: bfloat16 [4096, 512], P(('groups', 'row', 'col')), parts along dimension 0
- key_grads: bfloat16 [4096, 512], P(('groups', 'col', 'row')), parts along dimension 0
- value_grads: bfloat16 [4096, 512], P(('groups', 'col', 'row')), parts along dimension 0
There are 2 independent parts, one for each index of `groups`. A program takes and returns all parts, laid end to end along the dimension named above; each array names one. Nothing has to cross between parts.
Inputs may be any that keep to these rules, and one draw needn't show every extreme that they name: `contacts`: each row lists 12 distinct key blocks, among them the row's own index; counting key blocks in aligned groups of 4 consecutive blocks, at most 4 of a row's entries lie in one group, and exactly 4 lie in the group that holds the row's own block.
All inputs are finite; a program needn't handle non-finite values.
Results may differ from a plain program's by a relative error of at most 0.0066.
Values may be sent and summed in bfloat16 or wider, within the bound.
No kernel may reach another device: no remote copies, remote signals or barrier semaphores. Data moves between devices by JAX's collectives and lax.ppermute only.
A program may use at most 128 MiB of HBM per device.

v0:
```python
import math

import jax
import jax.numpy as jnp
from jax import lax
from jax.sharding import PartitionSpec as P

BLOCK = 128
MOST = 4


def block_slots(contacts, first_key, key_count, slot_count):
    within_set_positions = contacts - first_key
    inside = (within_set_positions >= 0) & (within_set_positions < key_count)
    rank_in = jnp.cumsum(inside.astype(jnp.int32), axis=1) - 1
    slot_ids = jnp.arange(slot_count, dtype=jnp.int32)
    hit_mask = inside[:, :, None] & (rank_in[:, :, None] == slot_ids[None, None, :])
    slot_keys = jnp.sum(jnp.where(hit_mask, within_set_positions[:, :, None], 0), axis=1)
    slot_live = jnp.any(hit_mask, axis=1)
    return (slot_keys, slot_live)


def tile_weights(query_portion, key_part, norm_part, live_part, score_scale):
    scores = (
        jnp.einsum("bqhd,bskhd->bshqk", query_portion, key_part, preferred_element_type=jnp.float32)
        * score_scale
    )
    weights = jnp.exp(scores - norm_part[:, None, :, :, None])
    return jnp.where(live_part[:, :, None, None, None], weights, 0.0)


def tile_score_grads(weights, grad_part, payload_slice, delta_part, score_scale):
    prob_grad = jnp.einsum(
        "bqhd,bskhd->bshqk", grad_part, payload_slice, preferred_element_type=jnp.float32
    )
    return (weights * (prob_grad - delta_part[:, None, :, :, None]) * score_scale).astype(
        jnp.bfloat16
    )


def fold_keys(running, partial_value, keys_part, live_part):
    key_count = running.shape[0]
    flattened = partial_value.reshape(keys_part.size, running.shape[1])
    owners = (
        jnp.arange(key_count, dtype=jnp.int32)[:, None] == keys_part.reshape(1, -1)
    ) & live_part.reshape(1, -1)
    placed = jnp.dot(
        owners.astype(jnp.float32),
        flattened,
        precision=lax.Precision.HIGHEST,
        preferred_element_type=jnp.float32,
    )
    return running + placed


def body(queries, keys, values, outputs, out_grad, log_norm, contacts):
    head_count = log_norm.shape[0]
    model_width = queries.shape[1]
    head_dim = model_width // head_count
    score_scale = 1.0 / math.sqrt(head_dim)
    local_rows = queries.shape[0]
    products = out_grad.astype(jnp.float32) * outputs.astype(jnp.float32)
    row_delta = jnp.sum(products.reshape(local_rows, head_count, head_dim), axis=2).T
    row_queries, row_cotangents = (
        lax.all_gather(queries, "col", axis=0, tiled=True),
        lax.all_gather(out_grad, "col", axis=0, tiled=True),
    )
    row_norms, row_deltas = (
        lax.all_gather(log_norm, "col", axis=1, tiled=True),
        lax.all_gather(row_delta, "col", axis=1, tiled=True),
    )
    col_keys, column_entries = (
        lax.all_gather(keys, "row", axis=0, tiled=True),
        lax.all_gather(values, "row", axis=0, tiled=True),
    )
    query_blocks = row_queries.shape[0] // BLOCK
    key_blocks = col_keys.shape[0] // BLOCK
    slot_keys, slot_live = block_slots(
        contacts, lax.axis_index("col") * key_blocks, key_blocks, MOST
    )
    query_split = row_queries.reshape(query_blocks, BLOCK, head_count, head_dim)
    grad_split = row_cotangents.reshape(query_blocks, BLOCK, head_count, head_dim)
    key_split = col_keys.reshape(key_blocks, BLOCK, head_count, head_dim)
    value_split = column_entries.reshape(key_blocks, BLOCK, head_count, head_dim)
    norm_split = jnp.transpose(row_norms.reshape(head_count, query_blocks, BLOCK), (1, 0, 2))
    delta_split = jnp.transpose(row_deltas.reshape(head_count, query_blocks, BLOCK), (1, 0, 2))
    step_blocks = math.gcd(query_blocks, 4)
    step_count = query_blocks // step_blocks

    def step_inputs(step_index):
        first_block = step_index * step_blocks
        query_portion = lax.dynamic_slice_in_dim(query_split, first_block, step_blocks, 0)
        grad_part = lax.dynamic_slice_in_dim(grad_split, first_block, step_blocks, 0)
        norm_part = lax.dynamic_slice_in_dim(norm_split, first_block, step_blocks, 0)
        delta_part = lax.dynamic_slice_in_dim(delta_split, first_block, step_blocks, 0)
        keys_part = lax.dynamic_slice_in_dim(slot_keys, first_block, step_blocks, 0)
        live_part = lax.dynamic_slice_in_dim(slot_live, first_block, step_blocks, 0)
        return (
            query_portion,
            grad_part,
            norm_part,
            delta_part,
            keys_part,
            live_part,
            key_split[keys_part],
            value_split[keys_part],
        )

    def value_grads_of(weights, grad_part):
        return jnp.einsum(
            "bshqk,bqhd->bskhd",
            weights.astype(jnp.bfloat16),
            grad_part,
            preferred_element_type=jnp.float32,
        )

    def query_key_grads(score_grad, query_portion, key_part):
        query_grad = jnp.einsum(
            "bshqk,bskhd->bqhd", score_grad, key_part, preferred_element_type=jnp.float32
        )
        key_grad = jnp.einsum(
            "bshqk,bqhd->bskhd", score_grad, query_portion, preferred_element_type=jnp.float32
        )
        return (query_grad, key_grad)

    key_start = jnp.zeros((key_blocks, BLOCK * model_width), jnp.float32)
    query_start = jnp.zeros((query_blocks, BLOCK, head_count, head_dim), jnp.float32)

    def full_step(step_index, carry):
        query_sum, key_sum, value_total = carry
        (
            query_portion,
            grad_part,
            norm_part,
            delta_part,
            keys_part,
            live_part,
            key_part,
            payload_slice,
        ) = step_inputs(step_index)
        weights = tile_weights(query_portion, key_part, norm_part, live_part, score_scale)
        value_grad = value_grads_of(weights, grad_part)
        score_grad = tile_score_grads(weights, grad_part, payload_slice, delta_part, score_scale)
        query_grad, key_grad = query_key_grads(score_grad, query_portion, key_part)
        query_sum = lax.dynamic_update_slice_in_dim(
            query_sum, query_grad, step_index * step_blocks, 0
        )
        key_sum = fold_keys(key_sum, key_grad, keys_part, live_part)
        value_total = fold_keys(value_total, value_grad, keys_part, live_part)
        return (query_sum, key_sum, value_total)

    query_sum, key_sum, value_total = lax.fori_loop(
        0, step_count, full_step, (query_start, key_start, key_start)
    )
    key_grads, value_grads = (
        lax.psum_scatter(key_sum.reshape(-1, model_width), "row", scatter_dimension=0, tiled=True),
        lax.psum_scatter(
            value_total.reshape(-1, model_width), "row", scatter_dimension=0, tiled=True
        ),
    )
    query_grads = lax.psum_scatter(
        query_sum.reshape(-1, model_width), "col", scatter_dimension=0, tiled=True
    )
    return (
        query_grads.astype(jnp.bfloat16),
        key_grads.astype(jnp.bfloat16),
        value_grads.astype(jnp.bfloat16),
    )


def solution(mesh):
    in_specs = (
        P(("groups", "row", "col"), None),
        P(("groups", "col", "row"), None),
        P(("groups", "col", "row"), None),
        P(("groups", "row", "col"), None),
        P(("groups", "row", "col"), None),
        P(None, ("groups", "row", "col")),
        P(("groups", "row"), None),
    )
    out_specs = (
        P(("groups", "row", "col"), None),
        P(("groups", "col", "row"), None),
        P(("groups", "col", "row"), None),
    )
    return jax.shard_map(body, mesh=mesh, in_specs=in_specs, out_specs=out_specs, check_vma=False)
```

profile of v0, /device:TPU:0, one launch (start us, length us, event | category | flops | bytes accessed | tf_op | source)
XLA Modules:
  0.0 189.8 jit_solution(813422545370484695)
XLA Ops:
  7.2 1.1 copy.67
  8.3 17.6 %all_gather.22 = bf16[512,512]{1,0:T(8,128)(2,1)S(1)} all-gather(bf16[128,512]{1,0:T(8,128)(2,1)} %param.11), channel_id=1, replica_groups=mesh['groups'=2,'row'=4,'col'=4] {'col'}, dimensions={0}, use_global_device_ids=true | all-gather | bytes 655360 | tf_op jit(solution)/shard_map/all_gather | solution.py:66
  27.2 13.6 %all_gather.20 = f32[8,512]{1,0:T(8,128)S(1)} all-gather(f32[8,128]{1,0:T(8,128)} %param.12), channel_id=1, replica_groups=mesh['groups'=2,'row'=4,'col'=4] {'col'}, dimensions={1}, use_global_device_ids=true | all-gather | bytes 20480 | tf_op jit(solution)/shard_map/all_gather | solution.py:69
  41.9 13.1 %all_gather.23 = f32[8,512]{1,0:T(8,128)S(1)} all-gather(f32[8,128]{1,0:T(8,128)S(1)} %bitcast.65), channel_id=1, replica_groups=mesh['groups'=2,'row'=4,'col'=4] {'col'}, dimensions={1}, use_global_device_ids=true | all-gather | bytes 20480 | tf_op jit(solution)/shard_map/all_gather | solution.py:70
  55.0 15.1 %all_gather.19 = bf16[512,512]{1,0:T(8,128)(2,1)S(1)} all-gather(bf16[128,512]{1,0:T(8,128)(2,1)} %param.7), channel_id=1, replica_groups=mesh['groups'=2,'row'=4,'col'=4] {'col'}, dimensions={0}, use_global_device_ids=true | all-gather | bytes 655360 | tf_op jit(solution)/shard_map/all_gather | solution.py:65
  70.5 7.2 %all_gather.18 = bf16[512,512]{1,0:T(8,128)(2,1)S(1)} all-gather(bf16[128,512]{1,0:T(8,128)(2,1)S(1)} %copy-done.4), channel_id=1, replica_groups=mesh['groups'=2,'row'=4,'col'=4] {'row'}, dimensions={0}, use_global_device_ids=true | all-gather | bytes 655360 | tf_op jit(solution)/shard_map/all_gather | solution.py:73
  78.8 7.3 %all_gather.21 = bf16[512,512]{1,0:T(8,128)(2,1)S(1)} all-gather(bf16[128,512]{1,0:T(8,128)(2,1)S(1)} %copy-done.5), channel_id=1, replica_groups=mesh['groups'=2,'row'=4,'col'=4] {'row'}, dimensions={0}, use_global_device_ids=true | all-gather | bytes 655360 | tf_op jit(solution)/shard_map/all_gather | solution.py:74
  88.4 2.2 %gather_fusion.1 = bf16[16,128,8,64]{1,3,2,0:T(8,128)(2,1)} fusion(bf16[4,128,8,64]{1,3,2,0:T(8,128)(2,1)S(1)} %copy.63, s32[1024]{0:T(1024)S(1)} %pad_clamp_fusion), kind=kCustom, calls=%fused_computation.1 | custom fusion | bytes 4194368 | tf_op jit(solution)/shard_map/while/body/eval_jaxpr/gather | solution.py:106
  91.6 1.3 fusion.13
  93.3 3.3 %fusion.4 = bf16[4,4,8,128,128]{3,4,1,2,0:T(8,128)(2,1)S(1)} fusion(f32[4,8,4,128,128]{4,3,2,1,0:T(8,128)S(1)} %fusion.13, f32[4,8,128]{2,1,0:T(8,128)S(1)} %bitcast.66, f32[4,8,128]{2,1,0:T(8,128)S(1)} %bitcast.63, pred[4,4]{1,0:T(4,128)(4,1)S(1)} %fusion.25, bf16[4,4,128,8,64]{2,4,3,1,0:T(8,128)(2,1)S(1)} %bitcast.56, ...), kind=kOutput, calls=%fused_computation.7 | convolution fusion | flops 283115520 | bytes 15237136 | tf_op jit(solution)/shard_map/while/body/eval_jaxpr/bqhd,bskhd->bshqk/dot_general | solution.py:33
  100.1 5.7 %convolution_bitcast_fusion = f32[4,4,128,8,64]{2,4,1,3,0:T(8,128)} fusion(bf16[4,4,8,128,128]{3,4,1,2,0:T(8,128)(2,1)} %copy-done.1, bf16[4,128,8,64,1]{1,0,3,2,4:T(4,128)(2,1)S(1)} %bitcast.58), kind=kOutput, calls=%fused_computation.13 | convolution fusion | flops 268435456 | bytes 8912896 | tf_op jit(solution)/shard_map/while/body/eval_jaxpr/bshqk,bqhd->bskhd/dot_general | solution.py:121
  105.7 7.0 %copy.74 = f32[4,4,128,8,64]{4,3,2,1,0:T(8,128)} copy(f32[4,4,128,8,64]{2,4,1,3,0:T(8,128)} %convolution_bitcast_fusion) | data formatting | bytes 8388608 | tf_op jit(solution)/shard_map/while/body/eval_jaxpr/bshqk,bqhd->bskhd/transpose | solution.py:121
  112.7 6.0 %reshape.85 = f32[16,65536]{1,0:T(8,128)} reshape(f32[4,4,128,8,64]{4,3,2,1,0:T(8,128)} %copy.74) | data formatting | bytes 8388608 | tf_op jit(solution)/shard_map/while/body/eval_jaxpr/reshape | solution.py:43
  118.8 3.8 %fusion.29 = f32[4,65536]{1,0:T(4,128)S(1)} fusion(f32[16,65536]{1,0:T(8,128)} %reshape.85, s32[16]{0:T(128)S(1)} %eq.46, pred[16]{0:T(512)(128)(4,1)S(1)} %and.33), kind=kOutput, calls=%fused_computation.37 | convolution fusion | flops 50331776 | bytes 5242960 | tf_op jit(solution)/shard_map/while/body/eval_jaxpr/dot_general | solution.py:47
  122.5 1.8 reshape.86
  124.4 7.1 %fusion.9 = f32[4,4,128,8,64]{2,4,1,3,0:T(8,128)} fusion(f32[4,8,4,128,128]{4,3,2,1,0:T(8,128)} %copy-done, f32[4,8,128]{2,1,0:T(8,128)S(1)} %bitcast.64, pred[4,4]{1,0:T(4,128)(4,1)S(1)} %fusion.25, bf16[4,128,8,64,1]{1,0,3,2,4:T(4,128)(2,1)S(1)} %bitcast.62), kind=kOutput, calls=%fused_computation.12 | convolution fusion | flops 276824064 | bytes 13123600 | tf_op jit(solution)/shard_map/while/body/eval_jaxpr/bshqk,bqhd->bskhd/dot_general | solution.py:110
  131.4 7.0 %copy.77 = f32[4,4,128,8,64]{4,3,2,1,0:T(8,128)} copy(f32[4,4,128,8,64]{2,4,1,3,0:T(8,128)} %fusion.9) | data formatting | bytes 8388608 | tf_op jit(solution)/shard_map/while/body/eval_jaxpr/bshqk,bqhd->bskhd/transpose | solution.py:110
  138.4 6.0 %reshape.87 = f32[16,65536]{1,0:T(8,128)} reshape(f32[4,4,128,8,64]{4,3,2,1,0:T(8,128)} %copy.77) | data formatting | bytes 8388608 | tf_op jit(solution)/shard_map/while/body/eval_jaxpr/reshape | solution.py:43
  144.4 3.9 %fusion.27 = f32[4,65536]{1,0:T(4,128)S(1)} fusion(f32[16,65536]{1,0:T(8,128)} %reshape.87, s32[16]{0:T(128)S(1)} %eq.46, pred[16]{0:T(512)(128)(4,1)S(1)} %and.33), kind=kOutput, calls=%fused_computation.36 | convolution fusion | flops 50331776 | bytes 5242960 | tf_op jit(solution)/shard_map/while/body/eval_jaxpr/dot_general | solution.py:47
  148.3 1.7 reshape.88
  151.8 2.4 %reduce-scatter.6.cloned.1.call-done = f32[128,512]{1,0:T(8,128)} async-done(((f32[512,512]{1,0:T(8,128)}), f32[128,512]{1,0:T(8,128)}) %reduce-scatter.6.cloned.1.call-update) | async-done | bytes 262160 | tf_op jit(solution)/shard_map/reduce_scatter | solution.py:156
  154.1 1.6 convert_element_type.34
  155.8 25.9 %reduce-scatter.8.cloned.1.call-done = f32[128,512]{1,0:T(8,128)} async-done(((f32[512,512]{1,0:T(8,128)}), f32[128,512]{1,0:T(8,128)}) %reduce-scatter.8.cloned.1.call-update) | async-done | bytes 262160 | tf_op jit(solution)/shard_map/reduce_scatter | solution.py:157
  181.6 1.6 convert_element_type.36
  (45 shorter events, 12.7 us)
Async XLA Ops:
  7.2 63.3 %copy-start.4 = (bf16[128,512]{1,0:T(8,128)(2,1)S(1)}, bf16[128,512]{1,0:T(8,128)(2,1)}, u32[]{:S(2)}) copy-start(bf16[128,512]{1,0:T(8,128)(2,1)} %param.8) | copy-start | bytes 393220
  7.2 71.6 %copy-start.5 = (bf16[128,512]{1,0:T(8,128)(2,1)S(1)}, bf16[128,512]{1,0:T(8,128)(2,1)}, u32[]{:S(2)}) copy-start(bf16[128,512]{1,0:T(8,128)(2,1)} %param.9) | copy-start | bytes 393220
  7.2 142.8 %reduce-scatter.4.cloned.1.call-start = ((), (), s32[]{:S(2)}) async-start(), calls=%async_computation.3 | async-start | bytes 1310720 | tf_op jit(solution)/shard_map/reduce_scatter | solution.py:161
  91.6 1.6 copy-start.2
  91.6 1.7 copy-start.3
  92.9 3.7 %copy-start = (f32[4,8,4,128,128]{4,3,2,1,0:T(8,128)}, f32[4,8,4,128,128]{4,3,2,1,0:T(8,128)S(1)}, u32[]{:S(2)}) copy-start(f32[4,8,4,128,128]{4,3,2,1,0:T(8,128)S(1)} %fusion.13) | copy-start | bytes 25165828
  96.6 2.0 %copy-start.1 = (bf16[4,4,8,128,128]{3,4,1,2,0:T(8,128)(2,1)}, bf16[4,4,8,128,128]{3,4,1,2,0:T(8,128)(2,1)S(1)}, u32[]{:S(2)}) copy-start(bf16[4,4,8,128,128]{3,4,1,2,0:T(8,128)(2,1)S(1)} %fusion.4) | copy-start | bytes 12582916
  99.7 54.5 %reduce-scatter.6.cloned.1.call-start = ((), (), s32[]{:S(2)}) async-start(), calls=%async_computation.4 | async-start | bytes 1310720 | tf_op jit(solution)/shard_map/reduce_scatter | solution.py:156
  124.3 57.3 %reduce-scatter.8.cloned.1.call-start = ((), (), s32[]{:S(2)}) async-start(), calls=%async_computation.5 | async-start | bytes 1310720 | tf_op jit(solution)/shard_map/reduce_scatter | solution.py:157
Sparse Core Ops, SparseCore 0:
  99.8 28.0 reduce-scatter.3
  130.6 23.5 reduce-scatter.5
  156.7 24.9 reduce-scatter.7
where the time goes:
time: 190 us
  blocking collectives  73.9 us (39%)
  local copies, waits for them, and re-layouts  42 us (22%)
  waiting for transfers between devices  28.3 us (15%)
  matrix products  25.9 us (14%)
  between operations  14 us (7%)
  other arithmetic  5.45 us (3%)
    reduce_scatter x1, waiting for transfers between devices, body(): lax.psum_scatter(value_total.reshape(-1, model_width), 'row', scatter_dim...  25.9 us
    all_gather x1, blocking collectives, body(): lax.all_gather(out_grad, 'col', axis=0, tiled=True)  17.6 us
    all_gather x1, blocking collectives, body(): lax.all_gather(queries, 'col', axis=0, tiled=True)  15.1 us
    all_gather x1, blocking collectives, body(): lax.all_gather(log_norm, 'col', axis=1, tiled=True)  13.6 us
    all_gather x1, blocking collectives, body(): lax.all_gather(row_delta, 'col', axis=1, tiled=True)  13.1 us
    reshape x2, local copies, waits for them, and re-layouts, fold_keys(): flattened = partial_value.reshape(keys_part.size, running.shape[1])  12 us
    dot_general x2, matrix products, fold_keys(): jnp.dot(owners.astype(jnp.float32), flattened, precision=lax.Precision.HI...  7.68 us
    all_gather x1, blocking collectives, body(): lax.all_gather(values, 'row', axis=0, tiled=True)  7.29 us
  transfers between devices with their start and end apart: 3, of which 2 were waited for; matrix products, arithmetic and copies ran while one was open for 28% of the time, Pallas kernels for 0%

commit v1 on v0

v1 whole, which is shorter than its diff:
```python
import math

import jax
import jax.numpy as jnp
from jax import lax
from jax.experimental import pallas as pl
from jax.experimental.pallas import tpu as pltpu
from jax.sharding import Mesh
from jax.sharding import PartitionSpec as P

BLOCK = 128
LANES = 128
HEADS = 8
STATS = 16
GROUP = 4
NT = (((1,), (1,)), ((), ()))
NN = (((1,), (0,)), ((), ()))
VMEM = pl.BlockSpec(memory_space=pltpu.VMEM)
SMEM = pl.BlockSpec(memory_space=pltpu.SMEM)


def split_three(x):
    hi = x.astype(jnp.bfloat16).astype(jnp.float32)
    rest = x - hi
    mid = rest.astype(jnp.bfloat16).astype(jnp.float32)
    return hi, mid, rest - mid


def pack_kernel(where_ref, contacts_ref, q_ref, k_ref, v_ref, o_ref, g_ref, norm_ref, *rest):
    outs, messages = rest[:HEADS], rest[HEADS]
    width = q_ref.shape[1]
    head_dim = width // HEADS
    me, column = where_ref[0], where_ref[1]
    products = g_ref[...].astype(jnp.float32) * o_ref[...].astype(jnp.float32)
    hi = products.astype(jnp.bfloat16)
    lo = (products - hi.astype(jnp.float32)).astype(jnp.bfloat16)
    owner = lax.broadcasted_iota(jnp.int32, (HEADS, width), 1) // head_dim
    picks = (owner == lax.broadcasted_iota(jnp.int32, (HEADS, width), 0)).astype(jnp.bfloat16)
    delta = lax.dot_general(picks, hi, NT, preferred_element_type=jnp.float32)
    delta += lax.dot_general(picks, lo, NT, preferred_element_type=jnp.float32)
    lane = lax.broadcasted_iota(jnp.int32, (1, LANES), 1)
    listed = jnp.zeros((1, LANES), jnp.float32)
    for i in range(contacts_ref.shape[1]):
        listed = jnp.where(lane == i, contacts_ref[column, i].astype(jnp.float32), listed)
    norm_parts = split_three(norm_ref[...])
    delta_parts = split_three(delta)
    blank = jnp.zeros((STATS - 7, LANES), jnp.float32)
    for h in range(HEADS):
        cols = slice(h * head_dim, (h + 1) * head_dim)
        rows = [part[h : h + 1] for part in norm_parts + delta_parts]
        stats = jnp.concatenate(rows + [listed, blank], axis=0).astype(jnp.bfloat16)
        messages[h, :BLOCK, :] = jnp.concatenate([k_ref[:, cols], v_ref[:, cols]], axis=1)
        messages[h, BLOCK : 2 * BLOCK, :] = jnp.concatenate([q_ref[:, cols], g_ref[:, cols]], axis=1)
        messages[h, 2 * BLOCK :, :] = stats
    for s in range(HEADS):
        outs[s][...] = messages[me ^ s]


def attend_kernel(sizes, where_ref, *rest):
    shares, across, columns, contact_count = sizes
    rows = rest[:HEADS]
    (other_ref, mine_ref, theirs_ref, dq_ref, kv, kt, weights, total, listed, places, sem) = rest[HEADS:]
    me, share = where_ref[0], where_ref[1]
    head_dim = LANES // 2
    score_scale = 1.0 / math.sqrt(head_dim)
    count = shares * HEADS
    for s in range(HEADS):
        kv[s] = rows[s][:BLOCK, :]
        listed[s : s + 1, :] = rows[s][2 * BLOCK :, :].astype(jnp.float32)[6:7].astype(jnp.int32)
    block = listed[...]
    col = block // (across * shares)
    rem = block - col * (across * shares)
    first = rem // shares
    second = rem - first * shares
    slot = (first * columns + col) ^ me
    listed[...] = (second ^ share) * HEADS + slot
    copy = pltpu.make_async_copy(listed, places, sem)
    copy.start()
    for j in range(count - HEADS):
        kv[HEADS + j] = other_ref[j * BLOCK : (j + 1) * BLOCK, :]
    total[...] = jnp.zeros_like(total)
    for j in range(count):
        kt[j] = kv[j].astype(jnp.float32).T[:head_dim, :].astype(jnp.bfloat16)
    low = lax.broadcasted_iota(jnp.int32, (BLOCK, LANES), 1) < head_dim
    for s in range(HEADS):
        both = rows[s][BLOCK : 2 * BLOCK, :]
        weights[s, :BLOCK, :] = jnp.where(low, both, jnp.zeros_like(both))
        weights[s, BLOCK:, :] = jnp.where(low, jnp.zeros_like(both), both)
    copy.wait()
    factor = score_scale * math.log2(math.e)
    for s in range(HEADS):
        stats = rows[s][2 * BLOCK :, :].astype(jnp.float32)
        norm = (stats[0:1] + stats[1:2] + stats[2:3]) * math.log2(math.e)
        delta = stats[3:4] + stats[4:5] + stats[5:6]
        weight = weights[s]
        dq = jnp.zeros((head_dim, BLOCK), jnp.float32)
        for t in range(0, contact_count, GROUP):
            spots = [places[s, t + i] for i in range(min(GROUP, contact_count - t))]
            keys = jnp.concatenate([kv[i] for i in spots], axis=0)
            pair = lax.dot_general(keys, weight, NT, preferred_element_type=jnp.float32)
            probs = jnp.exp2(pair[:, :BLOCK] * factor - norm)
            slope = (probs * (pair[:, BLOCK:] - delta)).astype(jnp.bfloat16)
            joined = jnp.concatenate([slope, probs.astype(jnp.bfloat16)], axis=1)
            grads = lax.dot_general(joined, weight, NN, preferred_element_type=jnp.float32)
            for n, i in enumerate(spots):
                total[i] += grads[n * BLOCK : (n + 1) * BLOCK]
            flat = jnp.concatenate([kt[i] for i in spots], axis=1)
            dq += lax.dot_general(flat, slope, NN, preferred_element_type=jnp.float32)
        dq_ref[s] = (dq * score_scale).astype(jnp.bfloat16)
    final = jnp.where(lax.broadcasted_iota(jnp.int32, (1, LANES), 1) < head_dim, score_scale, 1.0)
    for s in range(HEADS):
        mine_ref[s] = total[s] * final
    for j in range(count - HEADS):
        theirs_ref[j] = (total[HEADS + j] * final).astype(theirs_ref.dtype)


def join_kernel(mine_ref, theirs_ref, dq_ref, *outs):
    for s in range(HEADS):
        both = mine_ref[s] + theirs_ref[s].astype(jnp.float32)
        outs[s][:BLOCK, :] = both.astype(jnp.bfloat16)
        outs[s][BLOCK:, :] = dq_ref[s]


def unpack_kernel(where_ref, *rest):
    parts = rest[:HEADS]
    dq_ref, dk_ref, dv_ref, messages = rest[HEADS:]
    me = where_ref[0]
    head_dim = LANES // 2
    for s in range(HEADS):
        messages[me ^ s] = parts[s][...]
    for h in range(0, HEADS, 2):
        cols = slice(h * head_dim, (h + 2) * head_dim)
        even, odd = messages[h, :BLOCK, :], messages[h + 1, :BLOCK, :]
        dk_ref[:, cols] = jnp.concatenate([even[:, :head_dim], odd[:, :head_dim]], axis=1)
        dv_ref[:, cols] = jnp.concatenate([even[:, head_dim:], odd[:, head_dim:]], axis=1)
        turned = jnp.concatenate([messages[h, BLOCK:, :], messages[h + 1, BLOCK:, :]], axis=0)
        dq_ref[:, cols] = turned.astype(jnp.float32).T.astype(jnp.bfloat16)


def exchange(parts, peers):
    names = ("across", "col")
    moved = [parts[0]]
    for s in range(1, peers):
        moved.append(lax.ppermute(parts[s], names, [(j, j ^ s) for j in range(peers)]))
    return moved


def body(queries, keys, values, outputs, out_grad, log_norm, contacts):
    bf16, f32 = jnp.bfloat16, jnp.float32
    width = queries.shape[1]
    columns = lax.axis_size("col")
    across = lax.axis_size("across")
    shares = lax.axis_size("share")
    contact_count = contacts.shape[1]
    count = shares * HEADS
    column = lax.axis_index("col")
    me = lax.axis_index("across") * columns + column
    share = lax.axis_index("share")
    swap = shares == 2
    params = pltpu.CompilerParams(vmem_limit_bytes=48 * 1024 * 1024)
    length = 2 * BLOCK + STATS
    packed = pl.pallas_call(
        pack_kernel,
        out_shape=[jax.ShapeDtypeStruct((length, LANES), bf16)] * HEADS,
        in_specs=[SMEM, SMEM] + [VMEM] * 6,
        out_specs=[VMEM] * HEADS,
        scratch_shapes=[pltpu.VMEM((HEADS, length, LANES), bf16)],
        compiler_params=params,
    )(jnp.stack([me, column]).astype(jnp.int32), contacts, queries, keys, values, outputs, out_grad, log_norm)
    moved = exchange(packed, HEADS)
    own = jnp.concatenate([m[:BLOCK] for m in moved], axis=0)
    if swap:
        other = lax.ppermute(own, "share", [(0, 1), (1, 0)])
    else:
        gathered = lax.all_gather(own, "share", axis=0, tiled=False)
        turn = (jnp.arange(1, shares) ^ share).astype(jnp.int32)
        other = gathered[turn].reshape(-1, LANES)
    mine, theirs, dq = pl.pallas_call(
        lambda *refs: attend_kernel((shares, across, columns, contact_count), *refs),
        out_shape=[
            jax.ShapeDtypeStruct((HEADS, BLOCK, LANES), f32),
            jax.ShapeDtypeStruct((count - HEADS, BLOCK, LANES), bf16),
            jax.ShapeDtypeStruct((HEADS, LANES // 2, BLOCK), bf16),
        ],
        in_specs=[SMEM] + [VMEM] * (HEADS + 1),
        out_specs=[VMEM] * 3,
        scratch_shapes=[
            pltpu.VMEM((count, BLOCK, LANES), bf16),
            pltpu.VMEM((count, LANES // 2, BLOCK), bf16),
            pltpu.VMEM((HEADS, 2 * BLOCK, LANES), bf16),
            pltpu.VMEM((count, BLOCK, LANES), f32),
            pltpu.VMEM((HEADS, LANES), jnp.int32),
            pltpu.SMEM((HEADS, LANES), jnp.int32),
            pltpu.SemaphoreType.DMA,
        ],
        compiler_params=params,
    )(jnp.stack([me, share]).astype(jnp.int32), *moved, other)
    if swap:
        arrived = lax.ppermute(theirs, "share", [(0, 1), (1, 0)])
    else:
        full = jnp.zeros((shares, HEADS, BLOCK, LANES), f32)
        turn = (jnp.arange(1, shares) ^ share).astype(jnp.int32)
        full = full.at[turn].set(theirs.reshape(shares - 1, HEADS, BLOCK, LANES).astype(f32))
        arrived = lax.psum_scatter(full, "share", scatter_dimension=0, tiled=False)
    joined = pl.pallas_call(
        join_kernel,
        out_shape=[jax.ShapeDtypeStruct((BLOCK + LANES // 2, LANES), bf16)] * HEADS,
        in_specs=[VMEM] * 3,
        out_specs=[VMEM] * HEADS,
        compiler_params=params,
    )(mine, arrived, dq)
    back = exchange(joined, HEADS)
    return pl.pallas_call(
        unpack_kernel,
        out_shape=[jax.ShapeDtypeStruct((BLOCK, width), bf16)] * 3,
        in_specs=[SMEM] + [VMEM] * HEADS,
        out_specs=[VMEM] * 3,
        scratch_shapes=[pltpu.VMEM((HEADS, BLOCK + LANES // 2, LANES), bf16)],
        compiler_params=params,
    )(jnp.stack([me]).astype(jnp.int32), *back)


def solution(mesh):
    groups, rows, columns = (mesh.shape[a] for a in ("groups", "row", "col"))
    across = HEADS // columns
    shape = (groups, across, rows // across, columns)
    split = Mesh(mesh.devices.reshape(shape), ("groups", "across", "share", "col"))
    query_side = ("groups", "across", "share", "col")
    key_side = ("groups", "col", "across", "share")
    in_specs = (
        P(query_side, None),
        P(key_side, None),
        P(key_side, None),
        P(query_side, None),
        P(query_side, None),
        P(None, query_side),
        P(("groups", "across", "share"), None),
    )
    out_specs = (P(query_side, None), P(key_side, None), P(key_side, None))
    return jax.shard_map(body, mesh=split, in_specs=in_specs, out_specs=out_specs, check_vma=False)
```

time: 190 us -> 53.2 us (0.28)
  blocking collectives: 73.9 us -> 0 us
  local copies, waits for them, and re-layouts: 42 us -> 5.19 us
  starting transfers between devices: 0.3 us -> 26.6 us
  matrix products: 25.9 us -> 0 us
  waiting for transfers between devices: 28.3 us -> 11.8 us
  between operations: 14 us -> 0.75 us
  Pallas kernels: 0 us -> 8.4 us
  other arithmetic: 5.45 us -> 0.15 us
    all_gather x6 -> x0, blocking collectives: 73.9 us -> none  [the longest x1 17.6 us: body(): lax.all_gather(out_grad, 'col', axis=0, tiled=True)]
    reduce_scatter x3 -> x0, waiting for transfers between devices: 28.2 us -> none  [the longest x1 25.9 us: body(): lax.psum_scatter(value_total.reshape(-1, model_width), 'row', scatter_dim...]
    ppermute x0 -> x16, starting transfers between devices: none -> 26.6 us  [the longest x14 26.4 us: exchange(): lax.ppermute(parts[s], names, [(j, j ^ s) for j in range(peers)])]
    dot_general x7 -> x0, matrix products: 25.9 us -> none  [the longest x2 7.68 us: fold_keys(): jnp.dot(owners.astype(jnp.float32), flattened, precision=lax.Precision.HI...]
    reshape x10 -> x0, local copies, waits for them, and re-layouts: 18.9 us -> none  [the longest x2 12 us: fold_keys(): flattened = partial_value.reshape(keys_part.size, running.shape[1])]
    transpose x3 -> x0, local copies, waits for them, and re-layouts: 14.6 us -> none  [the longest x1 7.01 us: query_key_grads(): jnp.einsum('bshqk,bqhd->bskhd', score_grad, query_portion, preferred_elem...]
    ppermute x0 -> x16, waiting for transfers between devices: none -> 11.8 us  [the longest x14 9 us: exchange(): lax.ppermute(parts[s], names, [(j, j ^ s) for j in range(peers)])]
    pallas_call x0 -> x4, Pallas kernels: none -> 8.4 us  [the longest x1 6.59 us: body(): pl.pallas_call(lambda *refs: attend_kernel((shares, across, columns, cont...]
  transfers between devices with their start and end apart: 3 -> 16, of which waited for: 2 -> 6; matrix products, arithmetic and copies ran while one was open for 28% -> 0% of each run, Pallas kernels for 0% -> 0%
where the time goes in v1:
time: 53.2 us; the launch traced here: 52.9 us
  starting transfers between devices  26.6 us (50%)
  waiting for transfers between devices  11.8 us (22%)
  Pallas kernels  8.4 us (16%)
  local copies, waits for them, and re-layouts  5.19 us (10%)
  between operations  0.75 us (1%)
    ppermute x14, starting transfers between devices, exchange(): lax.ppermute(parts[s], names, [(j, j ^ s) for j in range(peers)])  26.4 us
    ppermute x14, waiting for transfers between devices, exchange(): lax.ppermute(parts[s], names, [(j, j ^ s) for j in range(peers)])  9 us
    pallas_call x1, Pallas kernels, body(): pl.pallas_call(lambda *refs: attend_kernel((shares, across, columns, cont...  6.59 us
    unnamed x21, local copies, waits for them, and re-layouts  5.18 us
    ppermute x1, waiting for transfers between devices, body(): other = lax.ppermute(own, 'share', [(0, 1), (1, 0)])  1.45 us
    ppermute x1, waiting for transfers between devices, body(): arrived = lax.ppermute(theirs, 'share', [(0, 1), (1, 0)])  1.4 us
  transfers between devices with their start and end apart: 16, of which 6 were waited for; matrix products, arithmetic and copies ran while one was open for 0% of the time, Pallas kernels for 0%

profile of v1, /device:TPU:0, one launch (start us, length us, event | category | flops | bytes accessed | tf_op | source)
XLA Modules:
  0.0 52.9 jit_solution(4079769302040210031)
XLA Ops:
  0.7 0.6 %copy-done.5 = f32[8,128]{1,0:T(8,128)S(1)} copy-done((f32[8,128]{1,0:T(8,128)S(1)}, f32[8,128]{1,0:T(8,128)}, u32[]{:S(2)}) %copy-start.5) | copy-done | bytes 4120
  1.3 0.9 %copy-done = bf16[128,512]{1,0:T(8,128)(2,1)S(1)} copy-done((bf16[128,512]{1,0:T(8,128)(2,1)S(1)}, bf16[128,512]{1,0:T(8,128)(2,1)}, u32[]{:S(2)}) %copy-start) | copy-done | bytes 131096
  2.2 0.9 %copy-done.1 = bf16[128,512]{1,0:T(8,128)(2,1)S(1)} copy-done((bf16[128,512]{1,0:T(8,128)(2,1)S(1)}, bf16[128,512]{1,0:T(8,128)(2,1)}, u32[]{:S(2)}) %copy-start.1) | copy-done | bytes 131096
  3.1 0.9 %copy-done.2 = bf16[128,512]{1,0:T(8,128)(2,1)S(1)} copy-done((bf16[128,512]{1,0:T(8,128)(2,1)S(1)}, bf16[128,512]{1,0:T(8,128)(2,1)}, u32[]{:S(2)}) %copy-start.2) | copy-done | bytes 131096
  4.1 0.9 %copy-done.3 = bf16[128,512]{1,0:T(8,128)(2,1)S(1)} copy-done((bf16[128,512]{1,0:T(8,128)(2,1)S(1)}, bf16[128,512]{1,0:T(8,128)(2,1)}, u32[]{:S(2)}) %copy-start.3) | copy-done | bytes 131096
  5.0 0.9 %copy-done.4 = bf16[128,512]{1,0:T(8,128)(2,1)S(1)} copy-done((bf16[128,512]{1,0:T(8,128)(2,1)S(1)}, bf16[128,512]{1,0:T(8,128)(2,1)}, u32[]{:S(2)}) %copy-start.4) | copy-done | bytes 131096
  5.9 0.8 %shard_map.94 = (bf16[272,128]{1,0:T(8,128)(2,1)S(1)}, bf16[272,128]{1,0:T(8,128)(2,1)S(1)}, bf16[272,128]{1,0:T(8,128)(2,1)S(1)}, bf16[272,128]{1,0:T(8,128)(2,...) custom-call(s32[2]{0:T(128)S(1)} %pad_add_fusion.1.where_ref, ...), custom_call_target="tpu_custom_call" | custom-call | tf_op jit(solution)/shard_map/pallas_call | solution.py:162
  6.7 3.1 %collective-permute-start = (bf16[272,128]{1,0:T(8,128)(2,1)S(1)}, bf16[272,128]{1,0:T(8,128)(2,1)S(1)}, u32[]{:S(2)}, u32[]{:S(2)}) collective-permute-start(bf16[272,128]{1,0:T(8,128)(2,1)S(1)} %get-tuple-element.23), channel_id=1, source_target_pairs={{0,1},{1,0},{2,3},{3,2},{8,9},{9,8},{10,11},{11,10},{4,5},{5,4},{6... | collective-permute-start | bytes 208904 | tf_op jit(solution)/shard_map/ppermute | solution.py:144
  9.8 2.6 %collective-permute-start.1 = (bf16[272,128]{1,0:T(8,128)(2,1)S(1)}, bf16[272,128]{1,0:T(8,128)(2,1)S(1)}, u32[]{:S(2)}, u32[]{:S(2)}) collective-permute-start(bf16[272,128]{1,0:T(8,128)(2,1)S(1)} %get-tuple-element.24), channel_id=1, source_target_pairs={{0,2},{1,3},{2,0},{3,1},{8,10},{9,11},{10,8},{11,9},{4,6},{5,7},{6... | collective-permute-start | bytes 208904 | tf_op jit(solution)/shard_map/ppermute | solution.py:144
  12.4 1.7 %collective-permute-start.3 = (bf16[272,128]{1,0:T(8,128)(2,1)S(1)}, bf16[272,128]{1,0:T(8,128)(2,1)S(1)}, u32[]{:S(2)}, u32[]{:S(2)}) collective-permute-start(bf16[272,128]{1,0:T(8,128)(2,1)S(1)} %get-tuple-element.26), channel_id=1, source_target_pairs={{0,8},{1,9},{2,10},{3,11},{8,0},{9,1},{10,2},{11,3},{4,12},{5,13},... | collective-permute-start | bytes 208904 | tf_op jit(solution)/shard_map/ppermute | solution.py:144
  14.1 0.6 %collective-permute-start.4 = (bf16[272,128]{1,0:T(8,128)(2,1)S(1)}, bf16[272,128]{1,0:T(8,128)(2,1)S(1)}, u32[]{:S(2)}, u32[]{:S(2)}) collective-permute-start(bf16[272,128]{1,0:T(8,128)(2,1)S(1)} %get-tuple-element.27), channel_id=1, source_target_pairs={{0,9},{1,8},{2,11},{3,10},{8,1},{9,0},{10,3},{11,2},{4,13},{5,12},... | collective-permute-start | bytes 208904 | tf_op jit(solution)/shard_map/ppermute | solution.py:144
  14.7 4.4 %collective-permute-start.5 = (bf16[272,128]{1,0:T(8,128)(2,1)S(1)}, bf16[272,128]{1,0:T(8,128)(2,1)S(1)}, u32[]{:S(2)}, u32[]{:S(2)}) collective-permute-start(bf16[272,128]{1,0:T(8,128)(2,1)S(1)} %get-tuple-element.28), channel_id=1, source_target_pairs={{0,10},{1,11},{2,8},{3,9},{8,2},{9,3},{10,0},{11,1},{4,14},{5,15},... | collective-permute-start | bytes 208904 | tf_op jit(solution)/shard_map/ppermute | solution.py:144
  19.2 2.8 %collective-permute-start.6 = (bf16[272,128]{1,0:T(8,128)(2,1)S(1)}, bf16[272,128]{1,0:T(8,128)(2,1)S(1)}, u32[]{:S(2)}, u32[]{:S(2)}) collective-permute-start(bf16[272,128]{1,0:T(8,128)(2,1)S(1)} %get-tuple-element.29), channel_id=1, source_target_pairs={{0,11},{1,10},{2,9},{3,8},{8,3},{9,2},{10,1},{11,0},{4,15},{5,14},... | collective-permute-start | bytes 208904 | tf_op jit(solution)/shard_map/ppermute | solution.py:144
  22.0 1.9 %collective-permute-done.5.refs_7_ = bf16[272,128]{1,0:T(8,128)(2,1)S(1)} collective-permute-done((bf16[272,128]{1,0:T(8,128)(2,1)S(1)}, bf16[272,128]{1,0:T(8,128)(2,1)S(1)}, u32[]{:S(2)}, u32[]{:S(2)}) %collective-permute-start.5) | collective-permute-done | bytes 69664 | tf_op jit(solution)/shard_map/ppermute | solution.py:144
  23.9 2.3 %collective-permute-done.6.refs_8_ = bf16[272,128]{1,0:T(8,128)(2,1)S(1)} collective-permute-done((bf16[272,128]{1,0:T(8,128)(2,1)S(1)}, bf16[272,128]{1,0:T(8,128)(2,1)S(1)}, u32[]{:S(2)}, u32[]{:S(2)}) %collective-permute-start.6) | collective-permute-done | bytes 69664 | tf_op jit(solution)/shard_map/ppermute | solution.py:144
  26.3 1.4 %collective-permute-done.7.refs_9_ = bf16[1024,128]{1,0:T(8,128)(2,1)S(1)} collective-permute-done((bf16[1024,128]{1,0:T(8,128)(2,1)S(1)}, bf16[1024,128]{1,0:T(8,128)(2,1)S(1)}, u32[]{:S(2)}, u32[]{:S(2)}) %collective-permute-start.7) | collective-permute-done | bytes 262176 | tf_op jit(solution)/shard_map/ppermute | solution.py:173
  27.8 6.6 %shard_map.95 = (f32[8,128,128]{2,1,0:T(8,128)S(1)}, bf16[8,128,128]{2,1,0:T(8,128)(2,1)S(1)}, bf16[8,64,128]{2,1,0:T(8,128)(2,1)S(1)}) custom-call(s32[2]{0:T(128)S(1)} %pad_add_fusion.refs_0_, bf16[272,128]{1,0:T(8,128)(2,1)S(1)} %get-tuple-element.22.refs_1_, bf16[272,128]{1,0:T(8,128)(2,1)S(1)} %collective-permute-done.refs_2_, ...), custom_call_target="tpu_custom_call" | custom-call | tf_op jit(solution)/shard_map/pallas_call | solution.py:178
  34.6 1.4 %collective-permute-done.8.theirs_ref = bf16[8,128,128]{2,1,0:T(8,128)(2,1)S(1)} collective-permute-done((bf16[8,128,128]{2,1,0:T(8,128)(2,1)S(1)}, bf16[8,128,128]{2,1,0:T(8,128)(2,1)S(1)}, u32[]{:S(2)}, u32[]{:S(2)}) %collective-permute-start.8) | collective-permute-done | bytes 262176 | tf_op jit(solution)/shard_map/ppermute | solution.py:199
  36.1 2.4 %collective-permute-start.10 = (bf16[192,128]{1,0:T(8,128)(2,1)S(1)}, bf16[192,128]{1,0:T(8,128)(2,1)S(1)}, u32[]{:S(2)}, u32[]{:S(2)}) collective-permute-start(bf16[192,128]{1,0:T(8,128)(2,1)S(1)} %get-tuple-element.35), channel_id=1, source_target_pairs={{0,2},{1,3},{2,0},{3,1},{8,10},{9,11},{10,8},{11,9},{4,6},{5,7},{6... | collective-permute-start | bytes 147464 | tf_op jit(solution)/shard_map/ppermute | solution.py:144
  38.6 1.9 %collective-permute-start.11 = (bf16[192,128]{1,0:T(8,128)(2,1)S(1)}, bf16[192,128]{1,0:T(8,128)(2,1)S(1)}, u32[]{:S(2)}, u32[]{:S(2)}) collective-permute-start(bf16[192,128]{1,0:T(8,128)(2,1)S(1)} %get-tuple-element.36), channel_id=1, source_target_pairs={{0,3},{1,2},{2,1},{3,0},{8,11},{9,10},{10,9},{11,8},{4,7},{5,6},{6... | collective-permute-start | bytes 147464 | tf_op jit(solution)/shard_map/ppermute | solution.py:144
  41.1 4.1 %collective-permute-start.14 = (bf16[192,128]{1,0:T(8,128)(2,1)S(1)}, bf16[192,128]{1,0:T(8,128)(2,1)S(1)}, u32[]{:S(2)}, u32[]{:S(2)}) collective-permute-start(bf16[192,128]{1,0:T(8,128)(2,1)S(1)} %get-tuple-element.39), channel_id=1, source_target_pairs={{0,10},{1,11},{2,8},{3,9},{8,2},{9,3},{10,0},{11,1},{4,14},{5,15},... | collective-permute-start | bytes 147464 | tf_op jit(solution)/shard_map/ppermute | solution.py:144
  45.2 2.0 %collective-permute-start.15 = (bf16[192,128]{1,0:T(8,128)(2,1)S(1)}, bf16[192,128]{1,0:T(8,128)(2,1)S(1)}, u32[]{:S(2)}, u32[]{:S(2)}) collective-permute-start(bf16[192,128]{1,0:T(8,128)(2,1)S(1)} %get-tuple-element.40), channel_id=1, source_target_pairs={{0,11},{1,10},{2,9},{3,8},{8,3},{9,2},{10,1},{11,0},{4,15},{5,14},... | collective-permute-start | bytes 147464 | tf_op jit(solution)/shard_map/ppermute | solution.py:144
  47.7 4.4 %collective-permute-done.15.rest_7_ = bf16[192,128]{1,0:T(8,128)(2,1)S(1)} collective-permute-done((bf16[192,128]{1,0:T(8,128)(2,1)S(1)}, bf16[192,128]{1,0:T(8,128)(2,1)S(1)}, u32[]{:S(2)}, u32[]{:S(2)}) %collective-permute-start.15) | collective-permute-done | bytes 49184 | tf_op jit(solution)/shard_map/ppermute | solution.py:144
  52.0 0.9 %shard_map.97 = (bf16[128,512]{1,0:T(8,128)(2,1)}, bf16[128,512]{1,0:T(8,128)(2,1)}, bf16[128,512]{1,0:T(8,128)(2,1)}) custom-call(s32[1]{0:T(128)} %bitcast.where_ref, bf16[192,128]{1,0:T(8,128)(2,1)S(1)} %get-tuple-element.33.rest_0_, bf16[192,128]{1,0:T(8,128)(2,1)S(1)} %collective-permute-done.9.rest_1_, ...), custom_call_target="tpu_custom_call" | custom-call | tf_op jit(solution)/shard_map/pallas_call | solution.py:213
  (36 shorter events, 1.6 us)
Async XLA Ops:
  0.6 0.7 %copy-start.5 = (f32[8,128]{1,0:T(8,128)S(1)}, f32[8,128]{1,0:T(8,128)}, u32[]{:S(2)}) copy-start(f32[8,128]{1,0:T(8,128)} %norm_ref.1) | copy-start | bytes 12292
  0.7 0.7 %copy-start.6 = (s32[4,12]{1,0:T(4,128)S(1)}, s32[4,12]{1,0:T(4,128)}, u32[]{:S(2)}) copy-start(s32[4,12]{1,0:T(4,128)} %contacts_ref.1) | copy-start | bytes 580
  1.3 0.9 %copy-start = (bf16[128,512]{1,0:T(8,128)(2,1)S(1)}, bf16[128,512]{1,0:T(8,128)(2,1)}, u32[]{:S(2)}) copy-start(bf16[128,512]{1,0:T(8,128)(2,1)} %q_ref.1) | copy-start | bytes 393220
  2.2 0.9 %copy-start.1 = (bf16[128,512]{1,0:T(8,128)(2,1)S(1)}, bf16[128,512]{1,0:T(8,128)(2,1)}, u32[]{:S(2)}) copy-start(bf16[128,512]{1,0:T(8,128)(2,1)} %k_ref.1) | copy-start | bytes 393220
  3.1 0.9 %copy-start.2 = (bf16[128,512]{1,0:T(8,128)(2,1)S(1)}, bf16[128,512]{1,0:T(8,128)(2,1)}, u32[]{:S(2)}) copy-start(bf16[128,512]{1,0:T(8,128)(2,1)} %v_ref.1) | copy-start | bytes 393220
  4.1 0.9 %copy-start.3 = (bf16[128,512]{1,0:T(8,128)(2,1)S(1)}, bf16[128,512]{1,0:T(8,128)(2,1)}, u32[]{:S(2)}) copy-start(bf16[128,512]{1,0:T(8,128)(2,1)} %o_ref.1) | copy-start | bytes 393220
  5.0 0.9 %copy-start.4 = (bf16[128,512]{1,0:T(8,128)(2,1)S(1)}, bf16[128,512]{1,0:T(8,128)(2,1)}, u32[]{:S(2)}) copy-start(bf16[128,512]{1,0:T(8,128)(2,1)} %g_ref.1) | copy-start | bytes 393220
  6.7 8.0 %collective-permute-start = (bf16[272,128]{1,0:T(8,128)(2,1)S(1)}, bf16[272,128]{1,0:T(8,128)(2,1)S(1)}, u32[]{:S(2)}, u32[]{:S(2)}) collective-permute-start(bf16[272,128]{1,0:T(8,128)(2,1)S(1)} %get-tuple-element.23), channel_id=1, source_target_pairs={{0,1},{1,0},{2,3},{3,2},{8,9},{9,8},{10,11},{11,10},{4,5},{5,4},{6... | collective-permute-start | bytes 208904 | tf_op jit(solution)/shard_map/ppermute | solution.py:144
  9.8 9.4 %collective-permute-start.1 = (bf16[272,128]{1,0:T(8,128)(2,1)S(1)}, bf16[272,128]{1,0:T(8,128)(2,1)S(1)}, u32[]{:S(2)}, u32[]{:S(2)}) collective-permute-start(bf16[272,128]{1,0:T(8,128)(2,1)S(1)} %get-tuple-element.24), channel_id=1, source_target_pairs={{0,2},{1,3},{2,0},{3,1},{8,10},{9,11},{10,8},{11,9},{4,6},{5,7},{6... | collective-permute-start | bytes 208904 | tf_op jit(solution)/shard_map/ppermute | solution.py:144
  12.4 9.6 %collective-permute-start.2 = (bf16[272,128]{1,0:T(8,128)(2,1)S(1)}, bf16[272,128]{1,0:T(8,128)(2,1)S(1)}, u32[]{:S(2)}, u32[]{:S(2)}) collective-permute-start(bf16[272,128]{1,0:T(8,128)(2,1)S(1)} %get-tuple-element.25), channel_id=1, source_target_pairs={{0,3},{1,2},{2,1},{3,0},{8,11},{9,10},{10,9},{11,8},{4,7},{5,6},{6... | collective-permute-start | bytes 208904 | tf_op jit(solution)/shard_map/ppermute | solution.py:144
  12.4 9.6 %collective-permute-start.3 = (bf16[272,128]{1,0:T(8,128)(2,1)S(1)}, bf16[272,128]{1,0:T(8,128)(2,1)S(1)}, u32[]{:S(2)}, u32[]{:S(2)}) collective-permute-start(bf16[272,128]{1,0:T(8,128)(2,1)S(1)} %get-tuple-element.26), channel_id=1, source_target_pairs={{0,8},{1,9},{2,10},{3,11},{8,0},{9,1},{10,2},{11,3},{4,12},{5,13},... | collective-permute-start | bytes 208904 | tf_op jit(solution)/shard_map/ppermute | solution.py:144
  14.1 7.9 %collective-permute-start.4 = (bf16[272,128]{1,0:T(8,128)(2,1)S(1)}, bf16[272,128]{1,0:T(8,128)(2,1)S(1)}, u32[]{:S(2)}, u32[]{:S(2)}) collective-permute-start(bf16[272,128]{1,0:T(8,128)(2,1)S(1)} %get-tuple-element.27), channel_id=1, source_target_pairs={{0,9},{1,8},{2,11},{3,10},{8,1},{9,0},{10,3},{11,2},{4,13},{5,12},... | collective-permute-start | bytes 208904 | tf_op jit(solution)/shard_map/ppermute | solution.py:144
  14.7 9.2 %collective-permute-start.5 = (bf16[272,128]{1,0:T(8,128)(2,1)S(1)}, bf16[272,128]{1,0:T(8,128)(2,1)S(1)}, u32[]{:S(2)}, u32[]{:S(2)}) collective-permute-start(bf16[272,128]{1,0:T(8,128)(2,1)S(1)} %get-tuple-element.28), channel_id=1, source_target_pairs={{0,10},{1,11},{2,8},{3,9},{8,2},{9,3},{10,0},{11,1},{4,14},{5,15},... | collective-permute-start | bytes 208904 | tf_op jit(solution)/shard_map/ppermute | solution.py:144
  19.2 7.1 %collective-permute-start.6 = (bf16[272,128]{1,0:T(8,128)(2,1)S(1)}, bf16[272,128]{1,0:T(8,128)(2,1)S(1)}, u32[]{:S(2)}, u32[]{:S(2)}) collective-permute-start(bf16[272,128]{1,0:T(8,128)(2,1)S(1)} %get-tuple-element.29), channel_id=1, source_target_pairs={{0,11},{1,10},{2,9},{3,8},{8,3},{9,2},{10,1},{11,0},{4,15},{5,14},... | collective-permute-start | bytes 208904 | tf_op jit(solution)/shard_map/ppermute | solution.py:144
  26.2 1.5 %collective-permute-start.7 = (bf16[1024,128]{1,0:T(8,128)(2,1)S(1)}, bf16[1024,128]{1,0:T(8,128)(2,1)S(1)}, u32[]{:S(2)}, u32[]{:S(2)}) collective-permute-start(bf16[1024,128]{1,0:T(8,128)(2,1)S(1)} %slice_dynamic-update-slice_fusion), channel_id=1, source_target_pairs={{0,4},{4,0},{1,5},{5,1},{2,6},{6,2},{3,7},{7,3},{8,12},{12,8},{9,1... | collective-permute-start | bytes 786440 | tf_op jit(solution)/shard_map/ppermute | solution.py:173
  34.4 1.6 %collective-permute-start.8 = (bf16[8,128,128]{2,1,0:T(8,128)(2,1)S(1)}, bf16[8,128,128]{2,1,0:T(8,128)(2,1)S(1)}, u32[]{:S(2)}, u32[]{:S(2)}) collective-permute-start(bf16[8,128,128]{2,1,0:T(8,128)(2,1)S(1)} %get-tuple-element.31), channel_id=1, source_target_pairs={{0,4},{4,0},{1,5},{5,1},{2,6},{6,2},{3,7},{7,3},{8,12},{12,8},{9,1... | collective-permute-start | bytes 786440 | tf_op jit(solution)/shard_map/ppermute | solution.py:199
  36.0 5.1 %collective-permute-start.9 = (bf16[192,128]{1,0:T(8,128)(2,1)S(1)}, bf16[192,128]{1,0:T(8,128)(2,1)S(1)}, u32[]{:S(2)}, u32[]{:S(2)}) collective-permute-start(bf16[192,128]{1,0:T(8,128)(2,1)S(1)} %get-tuple-element.34), channel_id=1, source_target_pairs={{0,1},{1,0},{2,3},{3,2},{8,9},{9,8},{10,11},{11,10},{4,5},{5,4},{6... | collective-permute-start | bytes 147464 | tf_op jit(solution)/shard_map/ppermute | solution.py:144
  36.1 9.1 %collective-permute-start.10 = (bf16[192,128]{1,0:T(8,128)(2,1)S(1)}, bf16[192,128]{1,0:T(8,128)(2,1)S(1)}, u32[]{:S(2)}, u32[]{:S(2)}) collective-permute-start(bf16[192,128]{1,0:T(8,128)(2,1)S(1)} %get-tuple-element.35), channel_id=1, source_target_pairs={{0,2},{1,3},{2,0},{3,1},{8,10},{9,11},{10,8},{11,9},{4,6},{5,7},{6... | collective-permute-start | bytes 147464 | tf_op jit(solution)/shard_map/ppermute | solution.py:144
  38.6 8.7 %collective-permute-start.11 = (bf16[192,128]{1,0:T(8,128)(2,1)S(1)}, bf16[192,128]{1,0:T(8,128)(2,1)S(1)}, u32[]{:S(2)}, u32[]{:S(2)}) collective-permute-start(bf16[192,128]{1,0:T(8,128)(2,1)S(1)} %get-tuple-element.36), channel_id=1, source_target_pairs={{0,3},{1,2},{2,1},{3,0},{8,11},{9,10},{10,9},{11,8},{4,7},{5,6},{6... | collective-permute-start | bytes 147464 | tf_op jit(solution)/shard_map/ppermute | solution.py:144
  40.5 6.8 %collective-permute-start.12 = (bf16[192,128]{1,0:T(8,128)(2,1)S(1)}, bf16[192,128]{1,0:T(8,128)(2,1)S(1)}, u32[]{:S(2)}, u32[]{:S(2)}) collective-permute-start(bf16[192,128]{1,0:T(8,128)(2,1)S(1)} %get-tuple-element.37), channel_id=1, source_target_pairs={{0,8},{1,9},{2,10},{3,11},{8,0},{9,1},{10,2},{11,3},{4,12},{5,13},... | collective-permute-start | bytes 147464 | tf_op jit(solution)/shard_map/ppermute | solution.py:144
  41.0 6.2 %collective-permute-start.13 = (bf16[192,128]{1,0:T(8,128)(2,1)S(1)}, bf16[192,128]{1,0:T(8,128)(2,1)S(1)}, u32[]{:S(2)}, u32[]{:S(2)}) collective-permute-start(bf16[192,128]{1,0:T(8,128)(2,1)S(1)} %get-tuple-element.38), channel_id=1, source_target_pairs={{0,9},{1,8},{2,11},{3,10},{8,1},{9,0},{10,3},{11,2},{4,13},{5,12},... | collective-permute-start | bytes 147464 | tf_op jit(solution)/shard_map/ppermute | solution.py:144
  41.1 6.5 %collective-permute-start.14 = (bf16[192,128]{1,0:T(8,128)(2,1)S(1)}, bf16[192,128]{1,0:T(8,128)(2,1)S(1)}, u32[]{:S(2)}, u32[]{:S(2)}) collective-permute-start(bf16[192,128]{1,0:T(8,128)(2,1)S(1)} %get-tuple-element.39), channel_id=1, source_target_pairs={{0,10},{1,11},{2,8},{3,9},{8,2},{9,3},{10,0},{11,1},{4,14},{5,15},... | collective-permute-start | bytes 147464 | tf_op jit(solution)/shard_map/ppermute | solution.py:144
  45.2 6.8 %collective-permute-start.15 = (bf16[192,128]{1,0:T(8,128)(2,1)S(1)}, bf16[192,128]{1,0:T(8,128)(2,1)S(1)}, u32[]{:S(2)}, u32[]{:S(2)}) collective-permute-start(bf16[192,128]{1,0:T(8,128)(2,1)S(1)} %get-tuple-element.40), channel_id=1, source_target_pairs={{0,11},{1,10},{2,9},{3,8},{8,3},{9,2},{10,1},{11,0},{4,15},{5,14},... | collective-permute-start | bytes 147464 | tf_op jit(solution)/shard_map/ppermute | solution.py:144

commit v2 on v1

--- a/solution.py
+++ b/solution.py
@@ -12,11 +12,14 @@
 LANES = 128
 HEADS = 8
 STATS = 16
-GROUP = 4
+GROUP = 12
 NT = (((1,), (1,)), ((), ()))
 NN = (((1,), (0,)), ((), ()))
 VMEM = pl.BlockSpec(memory_space=pltpu.VMEM)
 SMEM = pl.BlockSpec(memory_space=pltpu.SMEM)
+HBM = pl.BlockSpec(memory_space=pltpu.HBM)
+ORDER_OUT = (2, 4, 7, 5, 6, 1, 3)
+ORDER_BACK = (3, 2, 6, 7, 5, 4, 1)
 
 
 def split_three(x):
@@ -26,11 +29,19 @@
     return hi, mid, rest - mid
 
 
-def pack_kernel(where_ref, contacts_ref, q_ref, k_ref, v_ref, o_ref, g_ref, norm_ref, *rest):
-    outs, messages = rest[:HEADS], rest[HEADS]
+def pack_kernel(where_ref, contacts_hbm, *rest):
+    sources, outs = rest[:6], rest[6 : 6 + HEADS]
+    messages, contacts_ref, q_ref, k_ref, v_ref, o_ref, g_ref, norm_ref, sems = rest[6 + HEADS :]
+    targets = (q_ref, k_ref, v_ref, o_ref, g_ref, norm_ref)
+    copies = [pltpu.make_async_copy(a, b, sems.at[i]) for i, (a, b) in enumerate(zip(sources, targets))]
+    copies.append(pltpu.make_async_copy(contacts_hbm, contacts_ref, sems.at[6]))
+    for i in (4, 3, 5, 6, 0, 1, 2):
+        copies[i].start()
     width = q_ref.shape[1]
     head_dim = width // HEADS
     me, column = where_ref[0], where_ref[1]
+    for i in (4, 3, 5, 6):
+        copies[i].wait()
     products = g_ref[...].astype(jnp.float32) * o_ref[...].astype(jnp.float32)
     hi = products.astype(jnp.bfloat16)
     lo = (products - hi.astype(jnp.float32)).astype(jnp.bfloat16)
@@ -44,6 +55,8 @@
         listed = jnp.where(lane == i, contacts_ref[column, i].astype(jnp.float32), listed)
     norm_parts = split_three(norm_ref[...])
     delta_parts = split_three(delta)
+    for i in (0, 1, 2):
+        copies[i].wait()
     blank = jnp.zeros((STATS - 7, LANES), jnp.float32)
     for h in range(HEADS):
         cols = slice(h * head_dim, (h + 1) * head_dim)
@@ -58,7 +71,8 @@
 
 def attend_kernel(sizes, where_ref, *rest):
     shares, across, columns, contact_count = sizes
-    rows = rest[:HEADS]
+    order = (0,) + ORDER_OUT
+    rows = [rest[order.index(s)] for s in range(HEADS)]
     (other_ref, mine_ref, theirs_ref, dq_ref, kv, kt, weights, total, listed, places, sem) = rest[HEADS:]
     me, share = where_ref[0], where_ref[1]
     head_dim = LANES // 2
@@ -77,7 +91,8 @@
     copy = pltpu.make_async_copy(listed, places, sem)
     copy.start()
     for j in range(count - HEADS):
-        kv[HEADS + j] = other_ref[j * BLOCK : (j + 1) * BLOCK, :]
+        spot = HEADS * (1 + j // HEADS) + order[j % HEADS]
+        kv[spot] = other_ref[j * BLOCK : (j + 1) * BLOCK, :]
     total[...] = jnp.zeros_like(total)
     for j in range(count):
         kt[j] = kv[j].astype(jnp.float32).T[:head_dim, :].astype(jnp.bfloat16)
@@ -122,7 +137,8 @@
 
 
 def unpack_kernel(where_ref, *rest):
-    parts = rest[:HEADS]
+    order = (0,) + ORDER_BACK
+    parts = [rest[order.index(s)] for s in range(HEADS)]
     dq_ref, dk_ref, dv_ref, messages = rest[HEADS:]
     me = where_ref[0]
     head_dim = LANES // 2
@@ -137,11 +153,11 @@
         dq_ref[:, cols] = turned.astype(jnp.float32).T.astype(jnp.bfloat16)
 
 
-def exchange(parts, peers):
-    names = ("across", "col")
+def exchange(parts, order):
     moved = [parts[0]]
-    for s in range(1, peers):
-        moved.append(lax.ppermute(parts[s], names, [(j, j ^ s) for j in range(peers)]))
+    for s in order:
+        pairs = [(j, j ^ s) for j in range(HEADS)]
+        moved.append(lax.ppermute(parts[s], ("across", "col"), pairs))
     return moved
 
 
@@ -159,15 +175,24 @@
     swap = shares == 2
     params = pltpu.CompilerParams(vmem_limit_bytes=48 * 1024 * 1024)
     length = 2 * BLOCK + STATS
+    loaded = [
+        pltpu.with_memory_space_constraint(a, pltpu.HBM)
+        for a in (queries, keys, values, outputs, out_grad, log_norm)
+    ]
     packed = pl.pallas_call(
         pack_kernel,
         out_shape=[jax.ShapeDtypeStruct((length, LANES), bf16)] * HEADS,
-        in_specs=[SMEM, SMEM] + [VMEM] * 6,
+        in_specs=[SMEM] + [HBM] * 7,
         out_specs=[VMEM] * HEADS,
-        scratch_shapes=[pltpu.VMEM((HEADS, length, LANES), bf16)],
-        compiler_params=params,
-    )(jnp.stack([me, column]).astype(jnp.int32), contacts, queries, keys, values, outputs, out_grad, log_norm)
-    moved = exchange(packed, HEADS)
+        scratch_shapes=[
+            pltpu.VMEM((HEADS, length, LANES), bf16),
+            pltpu.SMEM(contacts.shape, jnp.int32),
+            *[pltpu.VMEM(a.shape, a.dtype) for a in loaded],
+            pltpu.SemaphoreType.DMA((7,)),
+        ],
+        compiler_params=params,
+    )(jnp.stack([me, column]).astype(jnp.int32), pltpu.with_memory_space_constraint(contacts, pltpu.HBM), *loaded)
+    moved = exchange(packed, ORDER_OUT)
     own = jnp.concatenate([m[:BLOCK] for m in moved], axis=0)
     if swap:
         other = lax.ppermute(own, "share", [(0, 1), (1, 0)])
@@ -209,7 +234,7 @@
         out_specs=[VMEM] * HEADS,
         compiler_params=params,
     )(mine, arrived, dq)
-    back = exchange(joined, HEADS)
+    back = exchange(joined, ORDER_BACK)
     return pl.pallas_call(
         unpack_kernel,
         out_shape=[jax.ShapeDtypeStruct((BLOCK, width), bf16)] * 3,

time: 53.2 us -> 44 us (0.83)
  local copies, waits for them, and re-layouts: 5.19 us -> 0.07 us
  waiting for transfers between devices: 11.8 us -> 9.5 us
  starting transfers between devices: 26.6 us -> 24.7 us
    unnamed x21 -> x7, local copies, waits for them, and re-layouts: 5.18 us -> 0.06 us
    ppermute x14, waiting for transfers between devices: 9 us -> 6.68 us  [exchange(): moved.append(lax.ppermute(parts[s], ('across', 'col'), pairs))]
    ppermute x14, starting transfers between devices: 26.4 us -> 24.5 us  [exchange(): moved.append(lax.ppermute(parts[s], ('across', 'col'), pairs))]
    pallas_call x1, Pallas kernels: 0.81 us -> 2.02 us  [body(): pl.pallas_call(pack_kernel, out_shape=[jax.ShapeDtypeStruct((length, LANE...]
    pallas_call x1, Pallas kernels: 6.59 us -> 5.73 us  [body(): pl.pallas_call(lambda *refs: attend_kernel((shares, across, columns, cont...]
  transfers between devices with their start and end apart: 16 -> 16, of which waited for: 6 -> 8; matrix products, arithmetic and copies ran while one was open for 0% -> 0% of each run, Pallas kernels for 0% -> 0%
where the time goes in v2:
time: 44 us; the launch traced here: 43.9 us
  starting transfers between devices  24.7 us (56%)
  waiting for transfers between devices  9.5 us (22%)
  Pallas kernels  8.75 us (20%)
  between operations  0.69 us (2%)
    ppermute x14, starting transfers between devices, exchange(): moved.append(lax.ppermute(parts[s], ('across', 'col'), pairs))  24.5 us
    ppermute x14, waiting for transfers between devices, exchange(): moved.append(lax.ppermute(parts[s], ('across', 'col'), pairs))  6.68 us
    pallas_call x1, Pallas kernels, body(): pl.pallas_call(lambda *refs: attend_kernel((shares, across, columns, cont...  5.73 us
    pallas_call x1, Pallas kernels, body(): pl.pallas_call(pack_kernel, out_shape=[jax.ShapeDtypeStruct((length, LANE...  2.02 us
    ppermute x1, waiting for transfers between devices, body(): other = lax.ppermute(own, 'share', [(0, 1), (1, 0)])  1.45 us
    ppermute x1, waiting for transfers between devices, body(): arrived = lax.ppermute(theirs, 'share', [(0, 1), (1, 0)])  1.38 us
    pallas_call x1, Pallas kernels, body(): pl.pallas_call(unpack_kernel, out_shape=[jax.ShapeDtypeStruct((BLOCK, wid...  0.94 us
  transfers between devices with their start and end apart: 16, of which 8 were waited for; matrix products, arithmetic and copies ran while one was open for 0% of the time, Pallas kernels for 0%

profile of v2, /device:TPU:0, one launch (start us, length us, event | category | flops | bytes accessed | tf_op | source)
XLA Modules:
  0.0 43.9 jit_solution(822639471773639589)
XLA Ops:
  0.7 2.0 %shard_map.94 = (bf16[272,128]{1,0:T(8,128)(2,1)S(1)}, bf16[272,128]{1,0:T(8,128)(2,1)S(1)}, bf16[272,128]{1,0:T(8,128)(2,1)S(1)}, bf16[272,128]{1,0:T(8,128)(2,...) custom-call(s32[2]{0:T(128)S(1)} %pad_add_fusion.1.where_ref, ...), custom_call_target="tpu_custom_call" | custom-call | tf_op jit(solution)/shard_map/pallas_call | solution.py:182
  2.7 4.1 %collective-permute-start = (bf16[272,128]{1,0:T(8,128)(2,1)S(1)}, bf16[272,128]{1,0:T(8,128)(2,1)S(1)}, u32[]{:S(2)}, u32[]{:S(2)}) collective-permute-start(bf16[272,128]{1,0:T(8,128)(2,1)S(1)} %get-tuple-element.23), channel_id=1, source_target_pairs={{0,2},{1,3},{2,0},{3,1},{8,10},{9,11},{10,8},{11,9},{4,6},{5,7},{6... | collective-permute-start | bytes 208904 | tf_op jit(solution)/shard_map/ppermute | solution.py:160
  6.8 1.5 %collective-permute-start.1 = (bf16[272,128]{1,0:T(8,128)(2,1)S(1)}, bf16[272,128]{1,0:T(8,128)(2,1)S(1)}, u32[]{:S(2)}, u32[]{:S(2)}) collective-permute-start(bf16[272,128]{1,0:T(8,128)(2,1)S(1)} %get-tuple-element.24), channel_id=1, source_target_pairs={{0,8},{1,9},{2,10},{3,11},{8,0},{9,1},{10,2},{11,3},{4,12},{5,13},... | collective-permute-start | bytes 208904 | tf_op jit(solution)/shard_map/ppermute | solution.py:160
  8.3 1.3 %collective-permute-start.2 = (bf16[272,128]{1,0:T(8,128)(2,1)S(1)}, bf16[272,128]{1,0:T(8,128)(2,1)S(1)}, u32[]{:S(2)}, u32[]{:S(2)}) collective-permute-start(bf16[272,128]{1,0:T(8,128)(2,1)S(1)} %get-tuple-element.25), channel_id=1, source_target_pairs={{0,11},{1,10},{2,9},{3,8},{8,3},{9,2},{10,1},{11,0},{4,15},{5,14},... | collective-permute-start | bytes 208904 | tf_op jit(solution)/shard_map/ppermute | solution.py:160
  9.7 0.5 %collective-permute-start.3 = (bf16[272,128]{1,0:T(8,128)(2,1)S(1)}, bf16[272,128]{1,0:T(8,128)(2,1)S(1)}, u32[]{:S(2)}, u32[]{:S(2)}) collective-permute-start(bf16[272,128]{1,0:T(8,128)(2,1)S(1)} %get-tuple-element.26), channel_id=1, source_target_pairs={{0,9},{1,8},{2,11},{3,10},{8,1},{9,0},{10,3},{11,2},{4,13},{5,12},... | collective-permute-start | bytes 208904 | tf_op jit(solution)/shard_map/ppermute | solution.py:160
  10.1 3.5 %collective-permute-start.4 = (bf16[272,128]{1,0:T(8,128)(2,1)S(1)}, bf16[272,128]{1,0:T(8,128)(2,1)S(1)}, u32[]{:S(2)}, u32[]{:S(2)}) collective-permute-start(bf16[272,128]{1,0:T(8,128)(2,1)S(1)} %get-tuple-element.27), channel_id=1, source_target_pairs={{0,10},{1,11},{2,8},{3,9},{8,2},{9,3},{10,0},{11,1},{4,14},{5,15},... | collective-permute-start | bytes 208904 | tf_op jit(solution)/shard_map/ppermute | solution.py:160
  13.6 0.7 %collective-permute-start.5 = (bf16[272,128]{1,0:T(8,128)(2,1)S(1)}, bf16[272,128]{1,0:T(8,128)(2,1)S(1)}, u32[]{:S(2)}, u32[]{:S(2)}) collective-permute-start(bf16[272,128]{1,0:T(8,128)(2,1)S(1)} %get-tuple-element.28), channel_id=1, source_target_pairs={{0,1},{1,0},{2,3},{3,2},{8,9},{9,8},{10,11},{11,10},{4,5},{5,4},{6... | collective-permute-start | bytes 208904 | tf_op jit(solution)/shard_map/ppermute | solution.py:160
  14.3 1.8 %collective-permute-start.6 = (bf16[272,128]{1,0:T(8,128)(2,1)S(1)}, bf16[272,128]{1,0:T(8,128)(2,1)S(1)}, u32[]{:S(2)}, u32[]{:S(2)}) collective-permute-start(bf16[272,128]{1,0:T(8,128)(2,1)S(1)} %get-tuple-element.29), channel_id=1, source_target_pairs={{0,3},{1,2},{2,1},{3,0},{8,11},{9,10},{10,9},{11,8},{4,7},{5,6},{6... | collective-permute-start | bytes 208904 | tf_op jit(solution)/shard_map/ppermute | solution.py:160
  16.1 0.2 collective-permute-done.3.refs_5_
  16.3 3.1 %collective-permute-done.4.refs_6_ = bf16[272,128]{1,0:T(8,128)(2,1)S(1)} collective-permute-done((bf16[272,128]{1,0:T(8,128)(2,1)S(1)}, bf16[272,128]{1,0:T(8,128)(2,1)S(1)}, u32[]{:S(2)}, u32[]{:S(2)}) %collective-permute-start.4) | collective-permute-done | bytes 69664 | tf_op jit(solution)/shard_map/ppermute | solution.py:160
  19.4 1.1 %collective-permute-done.6.refs_8_ = bf16[272,128]{1,0:T(8,128)(2,1)S(1)} collective-permute-done((bf16[272,128]{1,0:T(8,128)(2,1)S(1)}, bf16[272,128]{1,0:T(8,128)(2,1)S(1)}, u32[]{:S(2)}, u32[]{:S(2)}) %collective-permute-start.6) | collective-permute-done | bytes 69664 | tf_op jit(solution)/shard_map/ppermute | solution.py:160
  20.6 1.4 %collective-permute-done.7.refs_9_ = bf16[1024,128]{1,0:T(8,128)(2,1)S(1)} collective-permute-done((bf16[1024,128]{1,0:T(8,128)(2,1)S(1)}, bf16[1024,128]{1,0:T(8,128)(2,1)S(1)}, u32[]{:S(2)}, u32[]{:S(2)}) %collective-permute-start.7) | collective-permute-done | bytes 262176 | tf_op jit(solution)/shard_map/ppermute | solution.py:198
  22.0 5.7 %shard_map.95 = (f32[8,128,128]{2,1,0:T(8,128)S(1)}, bf16[8,128,128]{2,1,0:T(8,128)(2,1)S(1)}, bf16[8,64,128]{2,1,0:T(8,128)(2,1)S(1)}) custom-call(s32[2]{0:T(128)S(1)} %pad_add_fusion.refs_0_, bf16[272,128]{1,0:T(8,128)(2,1)S(1)} %get-tuple-element.22.refs_1_, bf16[272,128]{1,0:T(8,128)(2,1)S(1)} %collective-permute-done.refs_2_, ...), custom_call_target="tpu_custom_call" | custom-call | tf_op jit(solution)/shard_map/pallas_call | solution.py:203
  27.8 0.2 collective-permute-start.8
  28.0 1.4 %collective-permute-done.8.theirs_ref = bf16[8,128,128]{2,1,0:T(8,128)(2,1)S(1)} collective-permute-done((bf16[8,128,128]{2,1,0:T(8,128)(2,1)S(1)}, bf16[8,128,128]{2,1,0:T(8,128)(2,1)S(1)}, u32[]{:S(2)}, u32[]{:S(2)}) %collective-permute-start.8) | collective-permute-done | bytes 262176 | tf_op jit(solution)/shard_map/ppermute | solution.py:224
  29.4 1.9 %collective-permute-start.9 = (bf16[192,128]{1,0:T(8,128)(2,1)S(1)}, bf16[192,128]{1,0:T(8,128)(2,1)S(1)}, u32[]{:S(2)}, u32[]{:S(2)}) collective-permute-start(bf16[192,128]{1,0:T(8,128)(2,1)S(1)} %get-tuple-element.34), channel_id=1, source_target_pairs={{0,3},{1,2},{2,1},{3,0},{8,11},{9,10},{10,9},{11,8},{4,7},{5,6},{6... | collective-permute-start | bytes 147464 | tf_op jit(solution)/shard_map/ppermute | solution.py:160
  31.3 3.8 %collective-permute-start.11 = (bf16[192,128]{1,0:T(8,128)(2,1)S(1)}, bf16[192,128]{1,0:T(8,128)(2,1)S(1)}, u32[]{:S(2)}, u32[]{:S(2)}) collective-permute-start(bf16[192,128]{1,0:T(8,128)(2,1)S(1)} %get-tuple-element.36), channel_id=1, source_target_pairs={{0,10},{1,11},{2,8},{3,9},{8,2},{9,3},{10,0},{11,1},{4,14},{5,15},... | collective-permute-start | bytes 147464 | tf_op jit(solution)/shard_map/ppermute | solution.py:160
  35.1 2.0 %collective-permute-start.12 = (bf16[192,128]{1,0:T(8,128)(2,1)S(1)}, bf16[192,128]{1,0:T(8,128)(2,1)S(1)}, u32[]{:S(2)}, u32[]{:S(2)}) collective-permute-start(bf16[192,128]{1,0:T(8,128)(2,1)S(1)} %get-tuple-element.37), channel_id=1, source_target_pairs={{0,11},{1,10},{2,9},{3,8},{8,3},{9,2},{10,1},{11,0},{4,15},{5,14},... | collective-permute-start | bytes 147464 | tf_op jit(solution)/shard_map/ppermute | solution.py:160
  37.1 1.6 %collective-permute-start.14 = (bf16[192,128]{1,0:T(8,128)(2,1)S(1)}, bf16[192,128]{1,0:T(8,128)(2,1)S(1)}, u32[]{:S(2)}, u32[]{:S(2)}) collective-permute-start(bf16[192,128]{1,0:T(8,128)(2,1)S(1)} %get-tuple-element.39), channel_id=1, source_target_pairs={{0,8},{1,9},{2,10},{3,11},{8,0},{9,1},{10,2},{11,3},{4,12},{5,13},... | collective-permute-start | bytes 147464 | tf_op jit(solution)/shard_map/ppermute | solution.py:160
  38.7 1.9 %collective-permute-start.15 = (bf16[192,128]{1,0:T(8,128)(2,1)S(1)}, bf16[192,128]{1,0:T(8,128)(2,1)S(1)}, u32[]{:S(2)}, u32[]{:S(2)}) collective-permute-start(bf16[192,128]{1,0:T(8,128)(2,1)S(1)} %get-tuple-element.40), channel_id=1, source_target_pairs={{0,1},{1,0},{2,3},{3,2},{8,9},{9,8},{10,11},{11,10},{4,5},{5,4},{6... | collective-permute-start | bytes 147464 | tf_op jit(solution)/shard_map/ppermute | solution.py:160
  40.6 0.3 collective-permute-done.11.rest_3_
  41.0 1.1 %collective-permute-done.12.rest_4_ = bf16[192,128]{1,0:T(8,128)(2,1)S(1)} collective-permute-done((bf16[192,128]{1,0:T(8,128)(2,1)S(1)}, bf16[192,128]{1,0:T(8,128)(2,1)S(1)}, u32[]{:S(2)}, u32[]{:S(2)}) %collective-permute-start.12) | collective-permute-done | bytes 49184 | tf_op jit(solution)/shard_map/ppermute | solution.py:160
  42.1 0.9 %collective-permute-done.13.rest_5_ = bf16[192,128]{1,0:T(8,128)(2,1)S(1)} collective-permute-done((bf16[192,128]{1,0:T(8,128)(2,1)S(1)}, bf16[192,128]{1,0:T(8,128)(2,1)S(1)}, u32[]{:S(2)}, u32[]{:S(2)}) %collective-permute-start.13) | collective-permute-done | bytes 49184 | tf_op jit(solution)/shard_map/ppermute | solution.py:160
  42.9 0.9 %shard_map.97 = (bf16[128,512]{1,0:T(8,128)(2,1)}, bf16[128,512]{1,0:T(8,128)(2,1)}, bf16[128,512]{1,0:T(8,128)(2,1)}) custom-call(s32[1]{0:T(128)} %bitcast.where_ref, bf16[192,128]{1,0:T(8,128)(2,1)S(1)} %get-tuple-element.33.rest_0_, bf16[192,128]{1,0:T(8,128)(2,1)S(1)} %collective-permute-done.9.rest_1_, ...), custom_call_target="tpu_custom_call" | custom-call | tf_op jit(solution)/shard_map/pallas_call | solution.py:238
  (22 shorter events, 0.3 us)
Async XLA Ops:
  2.7 10.9 %collective-permute-start = (bf16[272,128]{1,0:T(8,128)(2,1)S(1)}, bf16[272,128]{1,0:T(8,128)(2,1)S(1)}, u32[]{:S(2)}, u32[]{:S(2)}) collective-permute-start(bf16[272,128]{1,0:T(8,128)(2,1)S(1)} %get-tuple-element.23), channel_id=1, source_target_pairs={{0,2},{1,3},{2,0},{3,1},{8,10},{9,11},{10,8},{11,9},{4,6},{5,7},{6... | collective-permute-start | bytes 208904 | tf_op jit(solution)/shard_map/ppermute | solution.py:160
  6.8 7.4 %collective-permute-start.1 = (bf16[272,128]{1,0:T(8,128)(2,1)S(1)}, bf16[272,128]{1,0:T(8,128)(2,1)S(1)}, u32[]{:S(2)}, u32[]{:S(2)}) collective-permute-start(bf16[272,128]{1,0:T(8,128)(2,1)S(1)} %get-tuple-element.24), channel_id=1, source_target_pairs={{0,8},{1,9},{2,10},{3,11},{8,0},{9,1},{10,2},{11,3},{4,12},{5,13},... | collective-permute-start | bytes 208904 | tf_op jit(solution)/shard_map/ppermute | solution.py:160
  8.3 7.7 %collective-permute-start.2 = (bf16[272,128]{1,0:T(8,128)(2,1)S(1)}, bf16[272,128]{1,0:T(8,128)(2,1)S(1)}, u32[]{:S(2)}, u32[]{:S(2)}) collective-permute-start(bf16[272,128]{1,0:T(8,128)(2,1)S(1)} %get-tuple-element.25), channel_id=1, source_target_pairs={{0,11},{1,10},{2,9},{3,8},{8,3},{9,2},{10,1},{11,0},{4,15},{5,14},... | collective-permute-start | bytes 208904 | tf_op jit(solution)/shard_map/ppermute | solution.py:160
  9.7 6.6 %collective-permute-start.3 = (bf16[272,128]{1,0:T(8,128)(2,1)S(1)}, bf16[272,128]{1,0:T(8,128)(2,1)S(1)}, u32[]{:S(2)}, u32[]{:S(2)}) collective-permute-start(bf16[272,128]{1,0:T(8,128)(2,1)S(1)} %get-tuple-element.26), channel_id=1, source_target_pairs={{0,9},{1,8},{2,11},{3,10},{8,1},{9,0},{10,3},{11,2},{4,13},{5,12},... | collective-permute-start | bytes 208904 | tf_op jit(solution)/shard_map/ppermute | solution.py:160
  10.1 9.2 %collective-permute-start.4 = (bf16[272,128]{1,0:T(8,128)(2,1)S(1)}, bf16[272,128]{1,0:T(8,128)(2,1)S(1)}, u32[]{:S(2)}, u32[]{:S(2)}) collective-permute-start(bf16[272,128]{1,0:T(8,128)(2,1)S(1)} %get-tuple-element.27), channel_id=1, source_target_pairs={{0,10},{1,11},{2,8},{3,9},{8,2},{9,3},{10,0},{11,1},{4,14},{5,15},... | collective-permute-start | bytes 208904 | tf_op jit(solution)/shard_map/ppermute | solution.py:160
  13.6 5.8 %collective-permute-start.5 = (bf16[272,128]{1,0:T(8,128)(2,1)S(1)}, bf16[272,128]{1,0:T(8,128)(2,1)S(1)}, u32[]{:S(2)}, u32[]{:S(2)}) collective-permute-start(bf16[272,128]{1,0:T(8,128)(2,1)S(1)} %get-tuple-element.28), channel_id=1, source_target_pairs={{0,1},{1,0},{2,3},{3,2},{8,9},{9,8},{10,11},{11,10},{4,5},{5,4},{6... | collective-permute-start | bytes 208904 | tf_op jit(solution)/shard_map/ppermute | solution.py:160
  14.3 6.2 %collective-permute-start.6 = (bf16[272,128]{1,0:T(8,128)(2,1)S(1)}, bf16[272,128]{1,0:T(8,128)(2,1)S(1)}, u32[]{:S(2)}, u32[]{:S(2)}) collective-permute-start(bf16[272,128]{1,0:T(8,128)(2,1)S(1)} %get-tuple-element.29), channel_id=1, source_target_pairs={{0,3},{1,2},{2,1},{3,0},{8,11},{9,10},{10,9},{11,8},{4,7},{5,6},{6... | collective-permute-start | bytes 208904 | tf_op jit(solution)/shard_map/ppermute | solution.py:160
  20.5 1.5 %collective-permute-start.7 = (bf16[1024,128]{1,0:T(8,128)(2,1)S(1)}, bf16[1024,128]{1,0:T(8,128)(2,1)S(1)}, u32[]{:S(2)}, u32[]{:S(2)}) collective-permute-start(bf16[1024,128]{1,0:T(8,128)(2,1)S(1)} %slice_dynamic-update-slice_fusion), channel_id=1, source_target_pairs={{0,4},{4,0},{1,5},{5,1},{2,6},{6,2},{3,7},{7,3},{8,12},{12,8},{9,1... | collective-permute-start | bytes 786440 | tf_op jit(solution)/shard_map/ppermute | solution.py:198
  27.8 1.6 %collective-permute-start.8 = (bf16[8,128,128]{2,1,0:T(8,128)(2,1)S(1)}, bf16[8,128,128]{2,1,0:T(8,128)(2,1)S(1)}, u32[]{:S(2)}, u32[]{:S(2)}) collective-permute-start(bf16[8,128,128]{2,1,0:T(8,128)(2,1)S(1)} %get-tuple-element.31), channel_id=1, source_target_pairs={{0,4},{4,0},{1,5},{5,1},{2,6},{6,2},{3,7},{7,3},{8,12},{12,8},{9,1... | collective-permute-start | bytes 786440 | tf_op jit(solution)/shard_map/ppermute | solution.py:224
  29.4 7.7 %collective-permute-start.9 = (bf16[192,128]{1,0:T(8,128)(2,1)S(1)}, bf16[192,128]{1,0:T(8,128)(2,1)S(1)}, u32[]{:S(2)}, u32[]{:S(2)}) collective-permute-start(bf16[192,128]{1,0:T(8,128)(2,1)S(1)} %get-tuple-element.34), channel_id=1, source_target_pairs={{0,3},{1,2},{2,1},{3,0},{8,11},{9,10},{10,9},{11,8},{4,7},{5,6},{6... | collective-permute-start | bytes 147464 | tf_op jit(solution)/shard_map/ppermute | solution.py:160
  31.3 7.4 %collective-permute-start.10 = (bf16[192,128]{1,0:T(8,128)(2,1)S(1)}, bf16[192,128]{1,0:T(8,128)(2,1)S(1)}, u32[]{:S(2)}, u32[]{:S(2)}) collective-permute-start(bf16[192,128]{1,0:T(8,128)(2,1)S(1)} %get-tuple-element.35), channel_id=1, source_target_pairs={{0,2},{1,3},{2,0},{3,1},{8,10},{9,11},{10,8},{11,9},{4,6},{5,7},{6... | collective-permute-start | bytes 147464 | tf_op jit(solution)/shard_map/ppermute | solution.py:160
  31.3 9.7 %collective-permute-start.11 = (bf16[192,128]{1,0:T(8,128)(2,1)S(1)}, bf16[192,128]{1,0:T(8,128)(2,1)S(1)}, u32[]{:S(2)}, u32[]{:S(2)}) collective-permute-start(bf16[192,128]{1,0:T(8,128)(2,1)S(1)} %get-tuple-element.36), channel_id=1, source_target_pairs={{0,10},{1,11},{2,8},{3,9},{8,2},{9,3},{10,0},{11,1},{4,14},{5,15},... | collective-permute-start | bytes 147464 | tf_op jit(solution)/shard_map/ppermute | solution.py:160
  35.1 6.9 %collective-permute-start.12 = (bf16[192,128]{1,0:T(8,128)(2,1)S(1)}, bf16[192,128]{1,0:T(8,128)(2,1)S(1)}, u32[]{:S(2)}, u32[]{:S(2)}) collective-permute-start(bf16[192,128]{1,0:T(8,128)(2,1)S(1)} %get-tuple-element.37), channel_id=1, source_target_pairs={{0,11},{1,10},{2,9},{3,8},{8,3},{9,2},{10,1},{11,0},{4,15},{5,14},... | collective-permute-start | bytes 147464 | tf_op jit(solution)/shard_map/ppermute | solution.py:160
  37.1 5.8 %collective-permute-start.13 = (bf16[192,128]{1,0:T(8,128)(2,1)S(1)}, bf16[192,128]{1,0:T(8,128)(2,1)S(1)}, u32[]{:S(2)}, u32[]{:S(2)}) collective-permute-start(bf16[192,128]{1,0:T(8,128)(2,1)S(1)} %get-tuple-element.38), channel_id=1, source_target_pairs={{0,9},{1,8},{2,11},{3,10},{8,1},{9,0},{10,3},{11,2},{4,13},{5,12},... | collective-permute-start | bytes 147464 | tf_op jit(solution)/shard_map/ppermute | solution.py:160
  37.1 5.8 %collective-permute-start.14 = (bf16[192,128]{1,0:T(8,128)(2,1)S(1)}, bf16[192,128]{1,0:T(8,128)(2,1)S(1)}, u32[]{:S(2)}, u32[]{:S(2)}) collective-permute-start(bf16[192,128]{1,0:T(8,128)(2,1)S(1)} %get-tuple-element.39), channel_id=1, source_target_pairs={{0,8},{1,9},{2,10},{3,11},{8,0},{9,1},{10,2},{11,3},{4,12},{5,13},... | collective-permute-start | bytes 147464 | tf_op jit(solution)/shard_map/ppermute | solution.py:160
  38.7 4.2 %collective-permute-start.15 = (bf16[192,128]{1,0:T(8,128)(2,1)S(1)}, bf16[192,128]{1,0:T(8,128)(2,1)S(1)}, u32[]{:S(2)}, u32[]{:S(2)}) collective-permute-start(bf16[192,128]{1,0:T(8,128)(2,1)S(1)} %get-tuple-element.40), channel_id=1, source_target_pairs={{0,1},{1,0},{2,3},{3,2},{8,9},{9,8},{10,11},{11,10},{4,5},{5,4},{6... | collective-permute-start | bytes 147464 | tf_op jit(solution)/shard_map/ppermute | solution.py:160

commit v3 on v2

v3 whole, which is shorter than its diff:
```python
import math

import jax
import jax.numpy as jnp
from jax import lax
from jax.experimental import pallas as pl
from jax.experimental.pallas import tpu as pltpu
from jax.sharding import Mesh
from jax.sharding import PartitionSpec as P

BLOCK = 128
LANES = 128
HEADS = 8
STATS = 16
STEP = 2
AHEAD = 3
NT = (((1,), (1,)), ((), ()))
NN = (((1,), (0,)), ((), ()))
VMEM = pl.BlockSpec(memory_space=pltpu.VMEM)
SMEM = pl.BlockSpec(memory_space=pltpu.SMEM)
HBM = pl.BlockSpec(memory_space=pltpu.HBM)
ORDER_OUT = (2, 4, 7, 5, 6, 1, 3)
ORDER_BACK = (3, 2, 6, 7, 5, 4, 1)


def contact_plan(sizes):
    shares, contact_count = sizes[0], sizes[3]
    home = max(0, contact_count - (shares - 1) * HEADS)
    return home // 2, contact_count - home + home // 2, contact_count


def number():
    return lax.axis_index("across") * lax.axis_size("col") + lax.axis_index("col")


def split_three(x):
    hi = x.astype(jnp.bfloat16).astype(jnp.float32)
    rest = x - hi
    mid = rest.astype(jnp.bfloat16).astype(jnp.float32)
    return hi, mid, rest - mid


def listed_contacts(contacts_ref, column, share, sizes):
    shares, across, columns, contact_count = sizes
    start, end, _ = contact_plan(sizes)
    home = start + contact_count - end
    target = lax.broadcasted_iota(jnp.int32, (HEADS, LANES), 0)
    lane = lax.broadcasted_iota(jnp.int32, (HEADS, LANES), 1)
    spots, ranks = [], []
    for i in range(contact_count):
        block = contacts_ref[column, i]
        col = block // (across * shares)
        rem = block - col * (across * shares)
        row = rem // shares
        away = (rem - row * shares) ^ share
        spots.append(away * HEADS + (target ^ (row * columns + col)))
        ranks.append(jnp.where(away == 0, 0, contact_count) + i)
    listed = jnp.zeros((HEADS, LANES), jnp.int32)
    for i in range(contact_count):
        rank = sum((ranks[j] < ranks[i]).astype(jnp.int32) for j in range(contact_count) if j != i)
        after = jnp.where(rank < home, rank + end - start, rank - home + start)
        listed = jnp.where(lane == jnp.where(rank < start, rank, after), spots[i], listed)
    return listed


def pack_kernel(sizes, contacts_hbm, *rest):
    sources, outs = rest[:6], rest[6 : 6 + HEADS]
    messages, contacts_ref, q_ref, k_ref, v_ref, o_ref, g_ref, norm_ref, sems = rest[6 + HEADS :]
    targets = (q_ref, k_ref, v_ref, o_ref, g_ref, norm_ref)
    copies = [pltpu.make_async_copy(a, b, sems.at[i]) for i, (a, b) in enumerate(zip(sources, targets))]
    copies.append(pltpu.make_async_copy(contacts_hbm, contacts_ref, sems.at[6]))
    for i in (6, 4, 3, 5, 0, 1, 2):
        copies[i].start()
    width = q_ref.shape[1]
    head_dim = width // HEADS
    me, column, share = number(), lax.axis_index("col"), lax.axis_index("share")
    copies[6].wait()
    listed = listed_contacts(contacts_ref, column, share, sizes).astype(jnp.float32)
    for i in (4, 3, 5):
        copies[i].wait()
    products = g_ref[...].astype(jnp.float32) * o_ref[...].astype(jnp.float32)
    hi = products.astype(jnp.bfloat16)
    lo = (products - hi.astype(jnp.float32)).astype(jnp.bfloat16)
    owner = lax.broadcasted_iota(jnp.int32, (HEADS, width), 1) // head_dim
    picks = (owner == lax.broadcasted_iota(jnp.int32, (HEADS, width), 0)).astype(jnp.bfloat16)
    delta = lax.dot_general(picks, hi, NT, preferred_element_type=jnp.float32)
    delta += lax.dot_general(picks, lo, NT, preferred_element_type=jnp.float32)
    norm_parts = split_three(norm_ref[...])
    delta_parts = split_three(delta)
    for i in (0, 1, 2):
        copies[i].wait()
    blank = jnp.zeros((STATS - 7, LANES), jnp.float32)
    for h in range(HEADS):
        cols = slice(h * head_dim, (h + 1) * head_dim)
        rows = [part[h : h + 1] for part in (listed,) + norm_parts + delta_parts]
        stats = jnp.concatenate(rows + [blank], axis=0).astype(jnp.bfloat16)
        messages[h, :BLOCK, :] = jnp.concatenate([k_ref[:, cols], v_ref[:, cols]], axis=1)
        messages[h, BLOCK : 2 * BLOCK, :] = jnp.concatenate([q_ref[:, cols], g_ref[:, cols]], axis=1)
        messages[h, 2 * BLOCK :, :] = stats
    for s in range(HEADS):
        outs[s][...] = messages[me ^ s]


def fill_turned(kt, kv, j):
    kt[j] = kv[j].astype(jnp.float32).T[: LANES // 2, :].astype(jnp.bfloat16)


def fill_weight(weight, both):
    low = lax.broadcasted_iota(jnp.int32, (BLOCK, LANES), 1) < LANES // 2
    weight[:BLOCK, :] = jnp.where(low, both, jnp.zeros_like(both))
    weight[BLOCK:, :] = jnp.where(low, jnp.zeros_like(both), both)


def by_slot(refs):
    order = (0,) + ORDER_OUT
    return [refs[order.index(s)] for s in range(HEADS)]


def lists_of(rows):
    taken = [row[2 * BLOCK :, :].astype(jnp.float32)[0:1] for row in rows]
    return jnp.concatenate(taken, axis=0).astype(jnp.int32)


def run(jobs, kv, kt, total):
    head_dim = LANES // 2
    factor = math.log2(math.e) / math.sqrt(head_dim)
    steps = [(n, job[2][t : t + STEP]) for n, job in enumerate(jobs) for t in range(0, len(job[2]), STEP)]
    pairs, probabilities = {}, {}
    sums = [jnp.zeros((head_dim, BLOCK), jnp.float32) for _ in jobs]

    def score(x):
        n, spots = steps[x]
        block = jnp.concatenate([kv[i] for i in spots], axis=0)
        pairs[x] = lax.dot_general(block, jobs[n][1][...], NT, preferred_element_type=jnp.float32)

    def soften(x):
        stats = jobs[steps[x][0]][0][2 * BLOCK :, :].astype(jnp.float32)
        norm = (stats[1:2] + stats[2:3] + stats[3:4]) * math.log2(math.e)
        delta = stats[4:5] + stats[5:6] + stats[6:7]
        pair = pairs.pop(x)
        probs = jnp.exp2(pair[:, :BLOCK] * factor - norm)
        slope = (probs * (pair[:, BLOCK:] - delta)).astype(jnp.bfloat16)
        probabilities[x] = (slope, probs.astype(jnp.bfloat16))

    def spread(x):
        n, spots = steps[x]
        slope, probs = probabilities.pop(x)
        joined = jnp.concatenate([slope, probs], axis=1)
        grads = lax.dot_general(joined, jobs[n][1][...], NN, preferred_element_type=jnp.float32)
        for m, i in enumerate(spots):
            total[i] += grads[m * BLOCK : (m + 1) * BLOCK]
        flat = jnp.concatenate([kt[i] for i in spots], axis=1)
        sums[n] += lax.dot_general(flat, slope, NN, preferred_element_type=jnp.float32)

    for x in range(len(steps) + AHEAD + 1):
        if x < len(steps):
            score(x)
        if 0 <= x - AHEAD < len(steps):
            soften(x - AHEAD)
        if 0 <= x - AHEAD - 1:
            spread(x - AHEAD - 1)
    return sums


def first_kernel(sizes, *rest):
    rows = by_slot(rest[:HEADS])
    kv, kt, weights, total, dq = rest[HEADS:]
    start = contact_plan(sizes)[0]
    lists = lists_of(rows)
    total[...] = jnp.zeros_like(total)
    for s in range(HEADS):
        kv[s] = rows[s][:BLOCK, :]
        fill_turned(kt, kv, s)
        fill_weight(weights.at[s], rows[s][BLOCK : 2 * BLOCK, :])
    jobs = [(rows[s], weights.at[s], [lists[s, i] for i in range(start)]) for s in range(HEADS)]
    for s, part in enumerate(run(jobs, kv, kt, total)):
        dq[s] = part


def second_kernel(sizes, *rest):
    rows = by_slot(rest[:HEADS])
    other_ref, _, _, weights, _, _, kv, kt, total, dq, theirs_ref = rest[HEADS:]
    start, end, _ = contact_plan(sizes)
    lists = lists_of(rows)
    order = (0,) + ORDER_OUT
    for j in range((sizes[0] - 1) * HEADS):
        spot = HEADS * (1 + j // HEADS) + order[j % HEADS]
        kv[spot] = other_ref[j * BLOCK : (j + 1) * BLOCK, :]
        fill_turned(kt, kv, spot)
    jobs = [(rows[s], weights.at[s], [lists[s, i] for i in range(start, end)]) for s in range(HEADS)]
    for s, part in enumerate(run(jobs, kv, kt, total)):
        dq[s] += part
    final = final_scale()
    for j in range(theirs_ref.shape[0]):
        theirs_ref[j] = (total[HEADS + j] * final).astype(theirs_ref.dtype)


def third_kernel(sizes, *rest):
    rows = by_slot(rest[:HEADS])
    kv, kt, weights, total_in, dq_in, mine_ref, dq_ref, total = rest[HEADS:]
    _, start, end = contact_plan(sizes)
    lists = lists_of(rows)
    for s in range(HEADS):
        total[s] = total_in[s]
    jobs = [(rows[s], weights.at[s], [lists[s, i] for i in range(start, end)]) for s in range(HEADS)]
    for s, part in enumerate(run(jobs, kv, kt, total)):
        dq_ref[s] = ((dq_in[s] + part) / math.sqrt(LANES // 2)).astype(jnp.bfloat16)
    final = final_scale()
    for s in range(HEADS):
        mine_ref[s] = total[s] * final


def final_scale():
    lane = lax.broadcasted_iota(jnp.int32, (1, LANES), 1)
    return jnp.where(lane < LANES // 2, 1.0 / math.sqrt(LANES // 2), 1.0)


def join_kernel(mine_ref, theirs_ref, dq_ref, *outs):
    for s in range(HEADS):
        both = mine_ref[s] + theirs_ref[s].astype(jnp.float32)
        outs[s][:BLOCK, :] = both.astype(jnp.bfloat16)
        outs[s][BLOCK:, :] = dq_ref[s]


def unpack_kernel(*rest):
    order = (0,) + ORDER_BACK
    parts = [rest[order.index(s)] for s in range(HEADS)]
    dq_ref, dk_ref, dv_ref, messages = rest[HEADS:]
    me = number()
    head_dim = LANES // 2
    for s in range(HEADS):
        messages[me ^ s] = parts[s][...]
    for h in range(0, HEADS, 2):
        cols = slice(h * head_dim, (h + 2) * head_dim)
        even, odd = messages[h, :BLOCK, :], messages[h + 1, :BLOCK, :]
        dk_ref[:, cols] = jnp.concatenate([even[:, :head_dim], odd[:, :head_dim]], axis=1)
        dv_ref[:, cols] = jnp.concatenate([even[:, head_dim:], odd[:, head_dim:]], axis=1)
        turned = jnp.concatenate([messages[h, BLOCK:, :], messages[h + 1, BLOCK:, :]], axis=0)
        dq_ref[:, cols] = turned.astype(jnp.float32).T.astype(jnp.bfloat16)


def exchange(parts, order):
    moved = {0: parts[0]}
    for s in order:
        pairs = [(j, j ^ s) for j in range(HEADS)]
        moved[s] = lax.ppermute(parts[s], ("across", "col"), pairs)
    return moved


def gather_keys(own, shares, share):
    if shares == 2:
        return lax.ppermute(own, "share", [(0, 1), (1, 0)])
    gathered = lax.all_gather(own, "share", axis=0, tiled=False)
    return gathered[jnp.arange(1, shares) ^ share].reshape(-1, LANES)


def sum_shares(theirs, shares, share):
    if shares == 2:
        return lax.ppermute(theirs, "share", [(0, 1), (1, 0)])
    full = jnp.zeros((shares, HEADS, BLOCK, LANES), jnp.float32)
    parts = theirs.reshape(shares - 1, HEADS, BLOCK, LANES).astype(jnp.float32)
    full = full.at[jnp.arange(1, shares) ^ share].set(parts)
    return lax.psum_scatter(full, "share", scatter_dimension=0, tiled=False)


def call(kernel, outs, in_specs, scratch=(), tiles=0, aliases=None):
    flops = tiles * 10 * BLOCK * BLOCK * (LANES // 2)
    cost = pl.CostEstimate(flops=flops, bytes_accessed=1 << 20, transcendentals=tiles * BLOCK * BLOCK)
    return pl.pallas_call(
        kernel,
        out_shape=[jax.ShapeDtypeStruct(shape, dtype) for shape, dtype in outs],
        in_specs=in_specs,
        out_specs=[VMEM] * len(outs),
        scratch_shapes=list(scratch),
        cost_estimate=cost if tiles else None,
        input_output_aliases=aliases or {},
        compiler_params=pltpu.CompilerParams(vmem_limit_bytes=48 * 1024 * 1024),
    )


def body(queries, keys, values, outputs, out_grad, log_norm, contacts):
    bf16, f32 = jnp.bfloat16, jnp.float32
    width = queries.shape[1]
    columns = lax.axis_size("col")
    across = lax.axis_size("across")
    shares = lax.axis_size("share")
    contact_count = contacts.shape[1]
    sizes = (shares, across, columns, contact_count)
    count = shares * HEADS
    half = LANES // 2
    share = lax.axis_index("share")
    length = 2 * BLOCK + STATS
    loaded = [
        pltpu.with_memory_space_constraint(a, pltpu.HBM)
        for a in (contacts, queries, keys, values, outputs, out_grad, log_norm)
    ]
    packed = call(
        lambda *refs: pack_kernel(sizes, *refs),
        [((length, LANES), bf16)] * HEADS,
        [HBM] * 7,
        [
            pltpu.VMEM((HEADS, length, LANES), bf16),
            pltpu.SMEM(contacts.shape, jnp.int32),
            *[pltpu.VMEM(a.shape, a.dtype) for a in loaded[1:]],
            pltpu.SemaphoreType.DMA((7,)),
        ],
    )(*loaded)
    moved = exchange(packed, ORDER_OUT)
    order = (0,) + ORDER_OUT
    rows = [moved[s] for s in order]
    start, end, _ = contact_plan(sizes)
    own = jnp.concatenate([row[:BLOCK] for row in rows], axis=0)
    other = gather_keys(own, shares, share)
    held = [
        ((count, BLOCK, LANES), bf16),
        ((count, half, LANES), bf16),
        ((HEADS, 2 * BLOCK, LANES), bf16),
        ((count, BLOCK, LANES), f32),
        ((HEADS, half, BLOCK), f32),
    ]
    kv, kt, weights, total, dq = call(
        lambda *refs: first_kernel(sizes, *refs),
        held,
        [VMEM] * HEADS,
        tiles=HEADS * start + 12,
    )(*rows)
    kv, kt, total, dq, theirs = call(
        lambda *refs: second_kernel(sizes, *refs),
        [held[0], held[1], held[3], held[4], ((count - HEADS, BLOCK, LANES), bf16)],
        [VMEM] * (HEADS + 6),
        tiles=HEADS * (end - start),
        aliases={HEADS + 1: 0, HEADS + 2: 1, HEADS + 4: 2, HEADS + 5: 3},
    )(*rows, other, kv, kt, weights, total, dq)
    arrived = sum_shares(theirs, shares, share)
    mine, dq = call(
        lambda *refs: third_kernel(sizes, *refs),
        [((HEADS, BLOCK, LANES), f32), ((HEADS, half, BLOCK), bf16)],
        [VMEM] * (HEADS + 5),
        [pltpu.VMEM((HEADS, BLOCK, LANES), f32)],
        tiles=HEADS * (contact_count - end) + 1,
    )(*rows, kv, kt, weights, total, dq)
    joined = call(
        join_kernel,
        [((BLOCK + half, LANES), bf16)] * HEADS,
        [VMEM] * 3,
    )(mine, arrived, dq)
    back = exchange(joined, ORDER_BACK)
    return call(
        unpack_kernel,
        [((BLOCK, width), bf16)] * 3,
        [VMEM] * HEADS,
        [pltpu.VMEM((HEADS, BLOCK + half, LANES), bf16)],
    )(*[back[s] for s in (0,) + ORDER_BACK])


def solution(mesh):
    groups, rows, columns = (mesh.shape[a] for a in ("groups", "row", "col"))
    across = HEADS // columns
    shape = (groups, across, rows // across, columns)
    split = Mesh(mesh.devices.reshape(shape), ("groups", "across", "share", "col"))
    query_side = ("groups", "across", "share", "col")
    key_side = ("groups", "col", "across", "share")
    in_specs = (
        P(query_side, None),
        P(key_side, None),
        P(key_side, None),
        P(query_side, None),
        P(query_side, None),
        P(None, query_side),
        P(("groups", "across", "share"), None),
    )
    out_specs = (P(query_side, None), P(key_side, None), P(key_side, None))
    return jax.shard_map(body, mesh=split, in_specs=in_specs, out_specs=out_specs, check_vma=False)
```

time: 44 us -> 40.6 us (0.923)
  waiting for transfers between devices: 9.5 us -> 7.71 us
  Pallas kernels: 8.75 us -> 7.26 us
    ppermute x16, waiting for transfers between devices: 9.5 us -> 7.71 us  [the longest x14 6.69 us: exchange(): moved[s] = lax.ppermute(parts[s], ('across', 'col'), pairs)]
    pallas_call x4 -> x6, Pallas kernels: 8.75 us -> 7.26 us  [the longest x1 2.84 us: body(): call(lambda *refs: second_kernel(sizes, *refs), [held[0], held[1], held[3...]
  transfers between devices with their start and end apart: 16 -> 16, of which waited for: 8 -> 8; matrix products, arithmetic and copies ran while one was open for 0% -> 0% of each run, Pallas kernels for 0% -> 5%
where the time goes in v3:
time: 40.6 us; the launch traced here: 40.4 us
  starting transfers between devices  24.7 us (61%)
  waiting for transfers between devices  7.71 us (19%)
  Pallas kernels  7.26 us (18%)
  between operations  0.69 us (2%)
    ppermute x14, starting transfers between devices, exchange(): moved[s] = lax.ppermute(parts[s], ('across', 'col'), pairs)  24.5 us
    ppermute x14, waiting for transfers between devices, exchange(): moved[s] = lax.ppermute(parts[s], ('across', 'col'), pairs)  6.69 us
    pallas_call x1, Pallas kernels, body(): call(lambda *refs: second_kernel(sizes, *refs), [held[0], held[1], held[3...  2.84 us
    pallas_call x1, Pallas kernels, body(): call(lambda *refs: pack_kernel(sizes, *refs), [((length, LANES), bf16)] *...  1.52 us
    pallas_call x1, Pallas kernels, body(): call(lambda *refs: first_kernel(sizes, *refs), held, [VMEM] * HEADS, tile...  0.96 us
    pallas_call x1, Pallas kernels, body(): call(unpack_kernel, [((BLOCK, width), bf16)] * 3, [VMEM] * HEADS, [pltpu....  0.95 us
    pallas_call x1, Pallas kernels, body(): call(lambda *refs: third_kernel(sizes, *refs), [((HEADS, BLOCK, LANES), f...  0.93 us
  transfers between devices with their start and end apart: 16, of which 8 were waited for; matrix products, arithmetic and copies ran while one was open for 0% of the time, Pallas kernels for 5%

profile of v3, /device:TPU:0, one launch (start us, length us, event | category | flops | bytes accessed | tf_op | source)
XLA Modules:
  0.0 40.4 jit_solution(2793837045353266862)
XLA Ops:
  0.6 1.5 %shard_map.94 = (bf16[272,128]{1,0:T(8,128)(2,1)S(1)}, bf16[272,128]{1,0:T(8,128)(2,1)S(1)}, bf16[272,128]{1,0:T(8,128)(2,1)S(1)}, bf16[272,128]{1,0:T(8,128)(2,...) custom-call(s32[4,12]{1,0:T(4,128)} %refs_0_.1, ...), custom_call_target="tpu_custom_call" | custom-call | tf_op jit(solution)/shard_map/pallas_call | solution.py:297
  2.2 4.1 %collective-permute-start = (bf16[272,128]{1,0:T(8,128)(2,1)S(1)}, bf16[272,128]{1,0:T(8,128)(2,1)S(1)}, u32[]{:S(2)}, u32[]{:S(2)}) collective-permute-start(bf16[272,128]{1,0:T(8,128)(2,1)S(1)} %get-tuple-element.32), channel_id=1, source_target_pairs={{0,2},{1,3},{2,0},{3,1},{8,10},{9,11},{10,8},{11,9},{4,6},{5,7},{6... | collective-permute-start | bytes 208904 | tf_op jit(solution)/shard_map/ppermute | solution.py:246
  6.3 1.5 %collective-permute-start.1 = (bf16[272,128]{1,0:T(8,128)(2,1)S(1)}, bf16[272,128]{1,0:T(8,128)(2,1)S(1)}, u32[]{:S(2)}, u32[]{:S(2)}) collective-permute-start(bf16[272,128]{1,0:T(8,128)(2,1)S(1)} %get-tuple-element.33), channel_id=1, source_target_pairs={{0,8},{1,9},{2,10},{3,11},{8,0},{9,1},{10,2},{11,3},{4,12},{5,13},... | collective-permute-start | bytes 208904 | tf_op jit(solution)/shard_map/ppermute | solution.py:246
  7.8 1.3 %collective-permute-start.2 = (bf16[272,128]{1,0:T(8,128)(2,1)S(1)}, bf16[272,128]{1,0:T(8,128)(2,1)S(1)}, u32[]{:S(2)}, u32[]{:S(2)}) collective-permute-start(bf16[272,128]{1,0:T(8,128)(2,1)S(1)} %get-tuple-element.34), channel_id=1, source_target_pairs={{0,11},{1,10},{2,9},{3,8},{8,3},{9,2},{10,1},{11,0},{4,15},{5,14},... | collective-permute-start | bytes 208904 | tf_op jit(solution)/shard_map/ppermute | solution.py:246
  9.1 0.5 %collective-permute-start.3 = (bf16[272,128]{1,0:T(8,128)(2,1)S(1)}, bf16[272,128]{1,0:T(8,128)(2,1)S(1)}, u32[]{:S(2)}, u32[]{:S(2)}) collective-permute-start(bf16[272,128]{1,0:T(8,128)(2,1)S(1)} %get-tuple-element.35), channel_id=1, source_target_pairs={{0,9},{1,8},{2,11},{3,10},{8,1},{9,0},{10,3},{11,2},{4,13},{5,12},... | collective-permute-start | bytes 208904 | tf_op jit(solution)/shard_map/ppermute | solution.py:246
  9.6 3.5 %collective-permute-start.4 = (bf16[272,128]{1,0:T(8,128)(2,1)S(1)}, bf16[272,128]{1,0:T(8,128)(2,1)S(1)}, u32[]{:S(2)}, u32[]{:S(2)}) collective-permute-start(bf16[272,128]{1,0:T(8,128)(2,1)S(1)} %get-tuple-element.36), channel_id=1, source_target_pairs={{0,10},{1,11},{2,8},{3,9},{8,2},{9,3},{10,0},{11,1},{4,14},{5,15},... | collective-permute-start | bytes 208904 | tf_op jit(solution)/shard_map/ppermute | solution.py:246
  13.0 0.7 %collective-permute-start.5 = (bf16[272,128]{1,0:T(8,128)(2,1)S(1)}, bf16[272,128]{1,0:T(8,128)(2,1)S(1)}, u32[]{:S(2)}, u32[]{:S(2)}) collective-permute-start(bf16[272,128]{1,0:T(8,128)(2,1)S(1)} %get-tuple-element.37), channel_id=1, source_target_pairs={{0,1},{1,0},{2,3},{3,2},{8,9},{9,8},{10,11},{11,10},{4,5},{5,4},{6... | collective-permute-start | bytes 208904 | tf_op jit(solution)/shard_map/ppermute | solution.py:246
  13.7 1.8 %collective-permute-start.6 = (bf16[272,128]{1,0:T(8,128)(2,1)S(1)}, bf16[272,128]{1,0:T(8,128)(2,1)S(1)}, u32[]{:S(2)}, u32[]{:S(2)}) collective-permute-start(bf16[272,128]{1,0:T(8,128)(2,1)S(1)} %get-tuple-element.38), channel_id=1, source_target_pairs={{0,3},{1,2},{2,1},{3,0},{8,11},{9,10},{10,9},{11,8},{4,7},{5,6},{6... | collective-permute-start | bytes 208904 | tf_op jit(solution)/shard_map/ppermute | solution.py:246
  15.7 3.1 %collective-permute-done.4.refs_5_ = bf16[272,128]{1,0:T(8,128)(2,1)S(1)} collective-permute-done((bf16[272,128]{1,0:T(8,128)(2,1)S(1)}, bf16[272,128]{1,0:T(8,128)(2,1)S(1)}, u32[]{:S(2)}, u32[]{:S(2)}) %collective-permute-start.4) | collective-permute-done | bytes 69664 | tf_op jit(solution)/shard_map/ppermute | solution.py:246
  18.8 1.1 %collective-permute-done.6.refs_7_ = bf16[272,128]{1,0:T(8,128)(2,1)S(1)} collective-permute-done((bf16[272,128]{1,0:T(8,128)(2,1)S(1)}, bf16[272,128]{1,0:T(8,128)(2,1)S(1)}, u32[]{:S(2)}, u32[]{:S(2)}) %collective-permute-start.6) | collective-permute-done | bytes 69664 | tf_op jit(solution)/shard_map/ppermute | solution.py:246
  19.9 1.0 %shard_map.95 = (bf16[16,128,128]{2,1,0:T(8,128)(2,1)S(1)}, bf16[16,64,128]{2,1,0:T(8,128)(2,1)S(1)}, bf16[8,256,128]{2,1,0:T(8,128)(2,1)S(1)}, f32[16,128,128]{2,1,0:T(8,128)S(1)}, f32[8,64,128]{2,1,0:T(8,128)S(1)}) custom-call(bf16[272,128]{1,0:T(8,128)(2,1)S(1)} %get-tuple-element.31.refs_0_, bf16[272,128]{1,0:T(8,128)(2,1)S(1)} %collective-permute-done.refs_1_, ...), custom_call_target="tpu_custom_call" | custom-call | flops 293601280 | bytes 1048576 | tf_op jit(solution)/shard_map/pallas_call | solution.py:321
  20.9 0.6 %collective-permute-done.7.refs_8_ = bf16[1024,128]{1,0:T(8,128)(2,1)S(1)} collective-permute-done((bf16[1024,128]{1,0:T(8,128)(2,1)S(1)}, bf16[1024,128]{1,0:T(8,128)(2,1)S(1)}, u32[]{:S(2)}, u32[]{:S(2)}) %collective-permute-start.7) | collective-permute-done | bytes 262176 | tf_op jit(solution)/shard_map/ppermute | solution.py:252
  21.4 2.8 %shard_map.96 = (bf16[16,128,128]{2,1,0:T(8,128)(2,1)S(1)}, bf16[16,64,128]{2,1,0:T(8,128)(2,1)S(1)}, f32[16,128,128]{2,1,0:T(8,128)S(1)}, f32[8,64,128]{2,1,0:T(8,128)S(1)}, bf16[8,128,128]{2,1,0:T(8,128)(2,1)S(1)}) custom-call(bf16[272,128]{1,0:T(8,128)(2,1)S(1)} %get-tuple-element.31.re, ...), custom_call_target="tpu_custom_call", output_to_operand_aliasing={{0}: (9, {}), {1}: (10, {}), {2}: (12, {}), {3}: (13, {})} | custom-call | flops 671088640 | bytes 1048576 | tf_op jit(solution)/shard_map/pallas_call | solution.py:327
  24.5 0.9 %shard_map.97 = (f32[8,128,128]{2,1,0:T(8,128)S(1)}, bf16[8,64,128]{2,1,0:T(8,128)(2,1)S(1)}) custom-call(bf16[272,128]{1,0:T(8,128)(2,1)S(1)} %get-tuple-element.31.refs_0_, bf16[272,128]{1,0:T(8,128)(2,1)S(1)} %collective-permute-done.refs_1_, bf16[272,128]{1,0:T(8,128)(2,1)S(1)} %collective-permute-done.1.refs_2_, ...), custom_call_target="tpu_custom_call" | custom-call | flops 178257920 | bytes 1048576 | tf_op jit(solution)/shard_map/pallas_call | solution.py:335
  25.4 0.5 %collective-permute-done.8.theirs_ref = bf16[8,128,128]{2,1,0:T(8,128)(2,1)S(1)} collective-permute-done((bf16[8,128,128]{2,1,0:T(8,128)(2,1)S(1)}, bf16[8,128,128]{2,1,0:T(8,128)(2,1)S(1)}, u32[]{:S(2)}, u32[]{:S(2)}) %collective-permute-start.8) | collective-permute-done | bytes 262176 | tf_op jit(solution)/shard_map/ppermute | solution.py:259
  25.9 1.9 %collective-permute-start.9 = (bf16[192,128]{1,0:T(8,128)(2,1)S(1)}, bf16[192,128]{1,0:T(8,128)(2,1)S(1)}, u32[]{:S(2)}, u32[]{:S(2)}) collective-permute-start(bf16[192,128]{1,0:T(8,128)(2,1)S(1)} %get-tuple-element.52), channel_id=1, source_target_pairs={{0,3},{1,2},{2,1},{3,0},{8,11},{9,10},{10,9},{11,8},{4,7},{5,6},{6... | collective-permute-start | bytes 147464 | tf_op jit(solution)/shard_map/ppermute | solution.py:246
  27.8 3.8 %collective-permute-start.11 = (bf16[192,128]{1,0:T(8,128)(2,1)S(1)}, bf16[192,128]{1,0:T(8,128)(2,1)S(1)}, u32[]{:S(2)}, u32[]{:S(2)}) collective-permute-start(bf16[192,128]{1,0:T(8,128)(2,1)S(1)} %get-tuple-element.54), channel_id=1, source_target_pairs={{0,10},{1,11},{2,8},{3,9},{8,2},{9,3},{10,0},{11,1},{4,14},{5,15},... | collective-permute-start | bytes 147464 | tf_op jit(solution)/shard_map/ppermute | solution.py:246
  31.6 2.0 %collective-permute-start.12 = (bf16[192,128]{1,0:T(8,128)(2,1)S(1)}, bf16[192,128]{1,0:T(8,128)(2,1)S(1)}, u32[]{:S(2)}, u32[]{:S(2)}) collective-permute-start(bf16[192,128]{1,0:T(8,128)(2,1)S(1)} %get-tuple-element.55), channel_id=1, source_target_pairs={{0,11},{1,10},{2,9},{3,8},{8,3},{9,2},{10,1},{11,0},{4,15},{5,14},... | collective-permute-start | bytes 147464 | tf_op jit(solution)/shard_map/ppermute | solution.py:246
  33.6 1.6 %collective-permute-start.14 = (bf16[192,128]{1,0:T(8,128)(2,1)S(1)}, bf16[192,128]{1,0:T(8,128)(2,1)S(1)}, u32[]{:S(2)}, u32[]{:S(2)}) collective-permute-start(bf16[192,128]{1,0:T(8,128)(2,1)S(1)} %get-tuple-element.57), channel_id=1, source_target_pairs={{0,8},{1,9},{2,10},{3,11},{8,0},{9,1},{10,2},{11,3},{4,12},{5,13},... | collective-permute-start | bytes 147464 | tf_op jit(solution)/shard_map/ppermute | solution.py:246
  35.3 1.9 %collective-permute-start.15 = (bf16[192,128]{1,0:T(8,128)(2,1)S(1)}, bf16[192,128]{1,0:T(8,128)(2,1)S(1)}, u32[]{:S(2)}, u32[]{:S(2)}) collective-permute-start(bf16[192,128]{1,0:T(8,128)(2,1)S(1)} %get-tuple-element.58), channel_id=1, source_target_pairs={{0,1},{1,0},{2,3},{3,2},{8,9},{9,8},{10,11},{11,10},{4,5},{5,4},{6... | collective-permute-start | bytes 147464 | tf_op jit(solution)/shard_map/ppermute | solution.py:246
  37.1 0.3 collective-permute-done.11.rest_3_
  37.5 1.1 %collective-permute-done.12.rest_4_ = bf16[192,128]{1,0:T(8,128)(2,1)S(1)} collective-permute-done((bf16[192,128]{1,0:T(8,128)(2,1)S(1)}, bf16[192,128]{1,0:T(8,128)(2,1)S(1)}, u32[]{:S(2)}, u32[]{:S(2)}) %collective-permute-start.12) | collective-permute-done | bytes 49184 | tf_op jit(solution)/shard_map/ppermute | solution.py:246
  38.6 0.9 %collective-permute-done.13.rest_5_ = bf16[192,128]{1,0:T(8,128)(2,1)S(1)} collective-permute-done((bf16[192,128]{1,0:T(8,128)(2,1)S(1)}, bf16[192,128]{1,0:T(8,128)(2,1)S(1)}, u32[]{:S(2)}, u32[]{:S(2)}) %collective-permute-start.13) | collective-permute-done | bytes 49184 | tf_op jit(solution)/shard_map/ppermute | solution.py:246
  39.5 1.0 %shard_map.99 = (bf16[128,512]{1,0:T(8,128)(2,1)}, bf16[128,512]{1,0:T(8,128)(2,1)}, bf16[128,512]{1,0:T(8,128)(2,1)}) custom-call(bf16[192,128]{1,0:T(8,128)(2,1)S(1)} %get-tuple-element.51.rest_0_, bf16[192,128]{1,0:T(8,128)(2,1)S(1)} %collective-permute-done.9.rest_1_, bf16[192,128]{1,0:T(8,128)(2,1)S(1)} %collective-permute-done.10.rest_2_, ...), custom_call_target="tpu_custom_call" | custom-call | tf_op jit(solution)/shard_map/pallas_call | solution.py:348
  (22 shorter events, 0.5 us)
Async XLA Ops:
  2.2 10.9 %collective-permute-start = (bf16[272,128]{1,0:T(8,128)(2,1)S(1)}, bf16[272,128]{1,0:T(8,128)(2,1)S(1)}, u32[]{:S(2)}, u32[]{:S(2)}) collective-permute-start(bf16[272,128]{1,0:T(8,128)(2,1)S(1)} %get-tuple-element.32), channel_id=1, source_target_pairs={{0,2},{1,3},{2,0},{3,1},{8,10},{9,11},{10,8},{11,9},{4,6},{5,7},{6... | collective-permute-start | bytes 208904 | tf_op jit(solution)/shard_map/ppermute | solution.py:246
  6.3 7.4 %collective-permute-start.1 = (bf16[272,128]{1,0:T(8,128)(2,1)S(1)}, bf16[272,128]{1,0:T(8,128)(2,1)S(1)}, u32[]{:S(2)}, u32[]{:S(2)}) collective-permute-start(bf16[272,128]{1,0:T(8,128)(2,1)S(1)} %get-tuple-element.33), channel_id=1, source_target_pairs={{0,8},{1,9},{2,10},{3,11},{8,0},{9,1},{10,2},{11,3},{4,12},{5,13},... | collective-permute-start | bytes 208904 | tf_op jit(solution)/shard_map/ppermute | solution.py:246
  7.8 7.7 %collective-permute-start.2 = (bf16[272,128]{1,0:T(8,128)(2,1)S(1)}, bf16[272,128]{1,0:T(8,128)(2,1)S(1)}, u32[]{:S(2)}, u32[]{:S(2)}) collective-permute-start(bf16[272,128]{1,0:T(8,128)(2,1)S(1)} %get-tuple-element.34), channel_id=1, source_target_pairs={{0,11},{1,10},{2,9},{3,8},{8,3},{9,2},{10,1},{11,0},{4,15},{5,14},... | collective-permute-start | bytes 208904 | tf_op jit(solution)/shard_map/ppermute | solution.py:246
  9.1 6.6 %collective-permute-start.3 = (bf16[272,128]{1,0:T(8,128)(2,1)S(1)}, bf16[272,128]{1,0:T(8,128)(2,1)S(1)}, u32[]{:S(2)}, u32[]{:S(2)}) collective-permute-start(bf16[272,128]{1,0:T(8,128)(2,1)S(1)} %get-tuple-element.35), channel_id=1, source_target_pairs={{0,9},{1,8},{2,11},{3,10},{8,1},{9,0},{10,3},{11,2},{4,13},{5,12},... | collective-permute-start | bytes 208904 | tf_op jit(solution)/shard_map/ppermute | solution.py:246
  9.6 9.2 %collective-permute-start.4 = (bf16[272,128]{1,0:T(8,128)(2,1)S(1)}, bf16[272,128]{1,0:T(8,128)(2,1)S(1)}, u32[]{:S(2)}, u32[]{:S(2)}) collective-permute-start(bf16[272,128]{1,0:T(8,128)(2,1)S(1)} %get-tuple-element.36), channel_id=1, source_target_pairs={{0,10},{1,11},{2,8},{3,9},{8,2},{9,3},{10,0},{11,1},{4,14},{5,15},... | collective-permute-start | bytes 208904 | tf_op jit(solution)/shard_map/ppermute | solution.py:246
  13.0 5.8 %collective-permute-start.5 = (bf16[272,128]{1,0:T(8,128)(2,1)S(1)}, bf16[272,128]{1,0:T(8,128)(2,1)S(1)}, u32[]{:S(2)}, u32[]{:S(2)}) collective-permute-start(bf16[272,128]{1,0:T(8,128)(2,1)S(1)} %get-tuple-element.37), channel_id=1, source_target_pairs={{0,1},{1,0},{2,3},{3,2},{8,9},{9,8},{10,11},{11,10},{4,5},{5,4},{6... | collective-permute-start | bytes 208904 | tf_op jit(solution)/shard_map/ppermute | solution.py:246
  13.7 6.2 %collective-permute-start.6 = (bf16[272,128]{1,0:T(8,128)(2,1)S(1)}, bf16[272,128]{1,0:T(8,128)(2,1)S(1)}, u32[]{:S(2)}, u32[]{:S(2)}) collective-permute-start(bf16[272,128]{1,0:T(8,128)(2,1)S(1)} %get-tuple-element.38), channel_id=1, source_target_pairs={{0,3},{1,2},{2,1},{3,0},{8,11},{9,10},{10,9},{11,8},{4,7},{5,6},{6... | collective-permute-start | bytes 208904 | tf_op jit(solution)/shard_map/ppermute | solution.py:246
  19.9 1.5 %collective-permute-start.7 = (bf16[1024,128]{1,0:T(8,128)(2,1)S(1)}, bf16[1024,128]{1,0:T(8,128)(2,1)S(1)}, u32[]{:S(2)}, u32[]{:S(2)}) collective-permute-start(bf16[1024,128]{1,0:T(8,128)(2,1)S(1)} %slice_dynamic-update-slice_fusion), channel_id=1, source_target_pairs={{0,4},{4,0},{1,5},{5,1},{2,6},{6,2},{3,7},{7,3},{8,12},{12,8},{9,1... | collective-permute-start | bytes 786440 | tf_op jit(solution)/shard_map/ppermute | solution.py:252
  24.3 1.6 %collective-permute-start.8 = (bf16[8,128,128]{2,1,0:T(8,128)(2,1)S(1)}, bf16[8,128,128]{2,1,0:T(8,128)(2,1)S(1)}, u32[]{:S(2)}, u32[]{:S(2)}) collective-permute-start(bf16[8,128,128]{2,1,0:T(8,128)(2,1)S(1)} %get-tuple-element.49), channel_id=1, source_target_pairs={{0,4},{4,0},{1,5},{5,1},{2,6},{6,2},{3,7},{7,3},{8,12},{12,8},{9,1... | collective-permute-start | bytes 786440 | tf_op jit(solution)/shard_map/ppermute | solution.py:259
  25.9 7.7 %collective-permute-start.9 = (bf16[192,128]{1,0:T(8,128)(2,1)S(1)}, bf16[192,128]{1,0:T(8,128)(2,1)S(1)}, u32[]{:S(2)}, u32[]{:S(2)}) collective-permute-start(bf16[192,128]{1,0:T(8,128)(2,1)S(1)} %get-tuple-element.52), channel_id=1, source_target_pairs={{0,3},{1,2},{2,1},{3,0},{8,11},{9,10},{10,9},{11,8},{4,7},{5,6},{6... | collective-permute-start | bytes 147464 | tf_op jit(solution)/shard_map/ppermute | solution.py:246
  27.8 7.4 %collective-permute-start.10 = (bf16[192,128]{1,0:T(8,128)(2,1)S(1)}, bf16[192,128]{1,0:T(8,128)(2,1)S(1)}, u32[]{:S(2)}, u32[]{:S(2)}) collective-permute-start(bf16[192,128]{1,0:T(8,128)(2,1)S(1)} %get-tuple-element.53), channel_id=1, source_target_pairs={{0,2},{1,3},{2,0},{3,1},{8,10},{9,11},{10,8},{11,9},{4,6},{5,7},{6... | collective-permute-start | bytes 147464 | tf_op jit(solution)/shard_map/ppermute | solution.py:246
  27.8 9.7 %collective-permute-start.11 = (bf16[192,128]{1,0:T(8,128)(2,1)S(1)}, bf16[192,128]{1,0:T(8,128)(2,1)S(1)}, u32[]{:S(2)}, u32[]{:S(2)}) collective-permute-start(bf16[192,128]{1,0:T(8,128)(2,1)S(1)} %get-tuple-element.54), channel_id=1, source_target_pairs={{0,10},{1,11},{2,8},{3,9},{8,2},{9,3},{10,0},{11,1},{4,14},{5,15},... | collective-permute-start | bytes 147464 | tf_op jit(solution)/shard_map/ppermute | solution.py:246
  31.6 6.9 %collective-permute-start.12 = (bf16[192,128]{1,0:T(8,128)(2,1)S(1)}, bf16[192,128]{1,0:T(8,128)(2,1)S(1)}, u32[]{:S(2)}, u32[]{:S(2)}) collective-permute-start(bf16[192,128]{1,0:T(8,128)(2,1)S(1)} %get-tuple-element.55), channel_id=1, source_target_pairs={{0,11},{1,10},{2,9},{3,8},{8,3},{9,2},{10,1},{11,0},{4,15},{5,14},... | collective-permute-start | bytes 147464 | tf_op jit(solution)/shard_map/ppermute | solution.py:246
  33.6 5.8 %collective-permute-start.13 = (bf16[192,128]{1,0:T(8,128)(2,1)S(1)}, bf16[192,128]{1,0:T(8,128)(2,1)S(1)}, u32[]{:S(2)}, u32[]{:S(2)}) collective-permute-start(bf16[192,128]{1,0:T(8,128)(2,1)S(1)} %get-tuple-element.56), channel_id=1, source_target_pairs={{0,9},{1,8},{2,11},{3,10},{8,1},{9,0},{10,3},{11,2},{4,13},{5,12},... | collective-permute-start | bytes 147464 | tf_op jit(solution)/shard_map/ppermute | solution.py:246
  33.6 5.8 %collective-permute-start.14 = (bf16[192,128]{1,0:T(8,128)(2,1)S(1)}, bf16[192,128]{1,0:T(8,128)(2,1)S(1)}, u32[]{:S(2)}, u32[]{:S(2)}) collective-permute-start(bf16[192,128]{1,0:T(8,128)(2,1)S(1)} %get-tuple-element.57), channel_id=1, source_target_pairs={{0,8},{1,9},{2,10},{3,11},{8,0},{9,1},{10,2},{11,3},{4,12},{5,13},... | collective-permute-start | bytes 147464 | tf_op jit(solution)/shard_map/ppermute | solution.py:246
  35.3 4.2 %collective-permute-start.15 = (bf16[192,128]{1,0:T(8,128)(2,1)S(1)}, bf16[192,128]{1,0:T(8,128)(2,1)S(1)}, u32[]{:S(2)}, u32[]{:S(2)}) collective-permute-start(bf16[192,128]{1,0:T(8,128)(2,1)S(1)} %get-tuple-element.58), channel_id=1, source_target_pairs={{0,1},{1,0},{2,3},{3,2},{8,9},{9,8},{10,11},{11,10},{4,5},{5,4},{6... | collective-permute-start | bytes 147464 | tf_op jit(solution)/shard_map/ppermute | solution.py:246

commit v4 on v3

--- a/solution.py
+++ b/solution.py
@@ -19,14 +19,19 @@
 VMEM = pl.BlockSpec(memory_space=pltpu.VMEM)
 SMEM = pl.BlockSpec(memory_space=pltpu.SMEM)
 HBM = pl.BlockSpec(memory_space=pltpu.HBM)
-ORDER_OUT = (2, 4, 7, 5, 6, 1, 3)
+ORDER_OUT = (4, 2, 7, 5, 1, 6, 3)
 ORDER_BACK = (3, 2, 6, 7, 5, 4, 1)
+LATE = (6, 3)
+GROUPS = ((0, 4), (2, 7), (5, 1))
+EARLY = sum(GROUPS, ())
 
 
 def contact_plan(sizes):
     shares, contact_count = sizes[0], sizes[3]
     home = max(0, contact_count - (shares - 1) * HEADS)
-    return home // 2, contact_count - home + home // 2, contact_count
+    late = len(LATE) * (shares - 1 if home >= len(LATE) else shares)
+    away = contact_count - home
+    return max(0, away - late), away, away + home // 2, contact_count
 
 
 def number():
@@ -42,8 +47,8 @@
 
 def listed_contacts(contacts_ref, column, share, sizes):
     shares, across, columns, contact_count = sizes
-    start, end, _ = contact_plan(sizes)
-    home = start + contact_count - end
+    away_count = contact_plan(sizes)[1]
+    home = contact_count - away_count
     target = lax.broadcasted_iota(jnp.int32, (HEADS, LANES), 0)
     lane = lax.broadcasted_iota(jnp.int32, (HEADS, LANES), 1)
     spots, ranks = [], []
@@ -53,13 +58,15 @@
         rem = block - col * (across * shares)
         row = rem // shares
         away = (rem - row * shares) ^ share
-        spots.append(away * HEADS + (target ^ (row * columns + col)))
-        ranks.append(jnp.where(away == 0, 0, contact_count) + i)
+        slot = target ^ (row * columns + col)
+        late = sum((slot == s).astype(jnp.int32) for s in LATE)
+        spots.append(away * HEADS + slot)
+        ranks.append(jnp.where(away == 0, -late, 2 + late) * contact_count + i)
     listed = jnp.zeros((HEADS, LANES), jnp.int32)
     for i in range(contact_count):
         rank = sum((ranks[j] < ranks[i]).astype(jnp.int32) for j in range(contact_count) if j != i)
-        after = jnp.where(rank < home, rank + end - start, rank - home + start)
-        listed = jnp.where(lane == jnp.where(rank < start, rank, after), spots[i], listed)
+        place = jnp.where(rank < home, rank + away_count, rank - home)
+        listed = jnp.where(lane == place, spots[i], listed)
     return listed
 
 
@@ -111,13 +118,9 @@
     weight[BLOCK:, :] = jnp.where(low, jnp.zeros_like(both), both)
 
 
-def by_slot(refs):
-    order = (0,) + ORDER_OUT
-    return [refs[order.index(s)] for s in range(HEADS)]
-
-
 def lists_of(rows):
     taken = [row[2 * BLOCK :, :].astype(jnp.float32)[0:1] for row in rows]
+    taken += [jnp.zeros((1, LANES), jnp.float32)] * (HEADS - len(taken))
     return jnp.concatenate(taken, axis=0).astype(jnp.int32)
 
 
@@ -162,33 +165,65 @@
     return sums
 
 
-def first_kernel(sizes, *rest):
-    rows = by_slot(rest[:HEADS])
-    kv, kt, weights, total, dq = rest[HEADS:]
-    start = contact_plan(sizes)[0]
+def fill_own(kv, kt, weights, s, row):
+    kv[s] = row[:BLOCK, :]
+    fill_turned(kt, kv, s)
+    fill_weight(weights.at[s], row[BLOCK : 2 * BLOCK, :])
+
+
+def fill_other(kv, kt, slots, other_ref):
+    for j in range(other_ref.shape[0] // BLOCK):
+        spot = HEADS * (1 + j // len(slots)) + slots[j % len(slots)]
+        kv[spot] = other_ref[j * BLOCK : (j + 1) * BLOCK, :]
+        fill_turned(kt, kv, spot)
+
+
+def early_kernel(sizes, *rest):
+    rows = rest[: len(EARLY)]
+    others = rest[len(EARLY) : len(EARLY) + len(GROUPS)]
+    kv, kt, weights, total, dq = rest[len(EARLY) + len(GROUPS) :]
+    end = contact_plan(sizes)[0]
     lists = lists_of(rows)
     total[...] = jnp.zeros_like(total)
-    for s in range(HEADS):
-        kv[s] = rows[s][:BLOCK, :]
-        fill_turned(kt, kv, s)
-        fill_weight(weights.at[s], rows[s][BLOCK : 2 * BLOCK, :])
-    jobs = [(rows[s], weights.at[s], [lists[s, i] for i in range(start)]) for s in range(HEADS)]
-    for s, part in enumerate(run(jobs, kv, kt, total)):
+    dq[...] = jnp.zeros_like(dq)
+    for s, row in zip(EARLY, rows):
+        fill_own(kv, kt, weights, s, row)
+    for slots, other_ref in zip(GROUPS, others):
+        fill_other(kv, kt, slots, other_ref)
+    jobs = [(rows[n], weights.at[s], [lists[n, i] for i in range(end)]) for n, s in enumerate(EARLY)]
+    for s, part in zip(EARLY, run(jobs, kv, kt, total)):
         dq[s] = part
 
 
+def late_kernel(*rest):
+    out = rest[-1]
+    for n in range(len(LATE)):
+        out[n * BLOCK : (n + 1) * BLOCK, :] = rest[n][:BLOCK, :]
+
+
+def first_kernel(sizes, *rest):
+    rows = rest[:HEADS]
+    kv, kt, weights, total, dq = rest[HEADS + 5 :]
+    _, start, end, _ = contact_plan(sizes)
+    lists = lists_of(rows)
+    for s, row in zip(LATE, rows[len(EARLY) :]):
+        fill_own(kv, kt, weights, s, row)
+    jobs = [(rows[n], weights.at[s], [lists[n, i] for i in range(start, end)]) for n, s in enumerate(EARLY + LATE)]
+    for s, part in zip(EARLY + LATE, run(jobs, kv, kt, total)):
+        dq[s] += part
+
+
 def second_kernel(sizes, *rest):
-    rows = by_slot(rest[:HEADS])
+    rows = rest[:HEADS]
     other_ref, _, _, weights, _, _, kv, kt, total, dq, theirs_ref = rest[HEADS:]
-    start, end, _ = contact_plan(sizes)
+    start, end, _, _ = contact_plan(sizes)
     lists = lists_of(rows)
-    order = (0,) + ORDER_OUT
-    for j in range((sizes[0] - 1) * HEADS):
-        spot = HEADS * (1 + j // HEADS) + order[j % HEADS]
-        kv[spot] = other_ref[j * BLOCK : (j + 1) * BLOCK, :]
-        fill_turned(kt, kv, spot)
-    jobs = [(rows[s], weights.at[s], [lists[s, i] for i in range(start, end)]) for s in range(HEADS)]
-    for s, part in enumerate(run(jobs, kv, kt, total)):
+    fill_other(kv, kt, LATE, other_ref)
+    jobs = []
+    for n, s in enumerate(EARLY + LATE):
+        first = start if s in EARLY else 0
+        jobs.append((rows[n], weights.at[s], [lists[n, i] for i in range(first, end)]))
+    for s, part in zip(EARLY + LATE, run(jobs, kv, kt, total)):
         dq[s] += part
     final = final_scale()
     for j in range(theirs_ref.shape[0]):
@@ -196,14 +231,14 @@
 
 
 def third_kernel(sizes, *rest):
-    rows = by_slot(rest[:HEADS])
+    rows = rest[:HEADS]
     kv, kt, weights, total_in, dq_in, mine_ref, dq_ref, total = rest[HEADS:]
-    _, start, end = contact_plan(sizes)
+    _, _, start, end = contact_plan(sizes)
     lists = lists_of(rows)
     for s in range(HEADS):
         total[s] = total_in[s]
-    jobs = [(rows[s], weights.at[s], [lists[s, i] for i in range(start, end)]) for s in range(HEADS)]
-    for s, part in enumerate(run(jobs, kv, kt, total)):
+    jobs = [(rows[n], weights.at[s], [lists[n, i] for i in range(start, end)]) for n, s in enumerate(EARLY + LATE)]
+    for s, part in zip(EARLY + LATE, run(jobs, kv, kt, total)):
         dq_ref[s] = ((dq_in[s] + part) / math.sqrt(LANES // 2)).astype(jnp.bfloat16)
     final = final_scale()
     for s in range(HEADS):
@@ -225,18 +260,28 @@
 def unpack_kernel(*rest):
     order = (0,) + ORDER_BACK
     parts = [rest[order.index(s)] for s in range(HEADS)]
-    dq_ref, dk_ref, dv_ref, messages = rest[HEADS:]
+    dq_out, dk_out, dv_out, dq_ref, dk_ref, dv_ref, messages, sems = rest[HEADS:]
     me = number()
     head_dim = LANES // 2
     for s in range(HEADS):
         messages[me ^ s] = parts[s][...]
+    copies = [
+        pltpu.make_async_copy(a, b, sems.at[n])
+        for n, (a, b) in enumerate(((dk_ref, dk_out), (dv_ref, dv_out), (dq_ref, dq_out)))
+    ]
+    for target, first, copy in ((dk_ref, 0, copies[0]), (dv_ref, head_dim, copies[1])):
+        for h in range(0, HEADS, 2):
+            cols = slice(h * head_dim, (h + 2) * head_dim)
+            pair = [messages[h + n, :BLOCK, first : first + head_dim] for n in range(2)]
+            target[:, cols] = jnp.concatenate(pair, axis=1)
+        copy.start()
     for h in range(0, HEADS, 2):
         cols = slice(h * head_dim, (h + 2) * head_dim)
-        even, odd = messages[h, :BLOCK, :], messages[h + 1, :BLOCK, :]
-        dk_ref[:, cols] = jnp.concatenate([even[:, :head_dim], odd[:, :head_dim]], axis=1)
-        dv_ref[:, cols] = jnp.concatenate([even[:, head_dim:], odd[:, head_dim:]], axis=1)
         turned = jnp.concatenate([messages[h, BLOCK:, :], messages[h + 1, BLOCK:, :]], axis=0)
         dq_ref[:, cols] = turned.astype(jnp.float32).T.astype(jnp.bfloat16)
+    copies[2].start()
+    for copy in copies:
+        copy.wait()
 
 
 def exchange(parts, order):
@@ -263,16 +308,16 @@
     return lax.psum_scatter(full, "share", scatter_dimension=0, tiled=False)
 
 
-def call(kernel, outs, in_specs, scratch=(), tiles=0, aliases=None):
+def call(kernel, outs, in_specs, scratch=(), tiles=0, aliases=None, out_space=VMEM):
     flops = tiles * 10 * BLOCK * BLOCK * (LANES // 2)
-    cost = pl.CostEstimate(flops=flops, bytes_accessed=1 << 20, transcendentals=tiles * BLOCK * BLOCK)
+    cost = pl.CostEstimate(flops=flops, bytes_accessed=tiles << 14, transcendentals=tiles * BLOCK * BLOCK)
     return pl.pallas_call(
         kernel,
         out_shape=[jax.ShapeDtypeStruct(shape, dtype) for shape, dtype in outs],
         in_specs=in_specs,
-        out_specs=[VMEM] * len(outs),
+        out_specs=[out_space] * len(outs),
         scratch_shapes=list(scratch),
-        cost_estimate=cost if tiles else None,
+        cost_estimate=cost,
         input_output_aliases=aliases or {},
         compiler_params=pltpu.CompilerParams(vmem_limit_bytes=48 * 1024 * 1024),
     )
@@ -306,11 +351,8 @@
         ],
     )(*loaded)
     moved = exchange(packed, ORDER_OUT)
-    order = (0,) + ORDER_OUT
-    rows = [moved[s] for s in order]
-    start, end, _ = contact_plan(sizes)
-    own = jnp.concatenate([row[:BLOCK] for row in rows], axis=0)
-    other = gather_keys(own, shares, share)
+    early, late = [moved[s] for s in EARLY], [moved[s] for s in LATE]
+    plan = contact_plan(sizes)
     held = [
         ((count, BLOCK, LANES), bf16),
         ((count, half, LANES), bf16),
@@ -318,27 +360,38 @@
         ((count, BLOCK, LANES), f32),
         ((HEADS, half, BLOCK), f32),
     ]
+    others = [
+        gather_keys(jnp.concatenate([moved[s][:BLOCK] for s in slots], axis=0), shares, share) for slots in GROUPS
+    ]
+    kv, kt, weights, total, dq = call(
+        lambda *refs: early_kernel(sizes, *refs),
+        held,
+        [VMEM] * (len(EARLY) + len(GROUPS)),
+    )(*early, *others)
+    own = call(late_kernel, [((len(LATE) * BLOCK, LANES), bf16)], [VMEM] * (len(LATE) + 1))(*late, dq)[0]
+    other = gather_keys(own, shares, share)
     kv, kt, weights, total, dq = call(
         lambda *refs: first_kernel(sizes, *refs),
         held,
-        [VMEM] * HEADS,
-        tiles=HEADS * start + 12,
-    )(*rows)
+        [VMEM] * (HEADS + 5),
+        tiles=HEADS * (plan[2] - plan[1]) + 12,
+        aliases={HEADS + n: n for n in range(5)},
+    )(*early, *late, kv, kt, weights, total, dq)
     kv, kt, total, dq, theirs = call(
         lambda *refs: second_kernel(sizes, *refs),
         [held[0], held[1], held[3], held[4], ((count - HEADS, BLOCK, LANES), bf16)],
         [VMEM] * (HEADS + 6),
-        tiles=HEADS * (end - start),
+        tiles=HEADS * (plan[1] - plan[0]) + len(LATE) * plan[0],
         aliases={HEADS + 1: 0, HEADS + 2: 1, HEADS + 4: 2, HEADS + 5: 3},
-    )(*rows, other, kv, kt, weights, total, dq)
+    )(*early, *late, other, kv, kt, weights, total, dq)
     arrived = sum_shares(theirs, shares, share)
     mine, dq = call(
         lambda *refs: third_kernel(sizes, *refs),
         [((HEADS, BLOCK, LANES), f32), ((HEADS, half, BLOCK), bf16)],
         [VMEM] * (HEADS + 5),
         [pltpu.VMEM((HEADS, BLOCK, LANES), f32)],
-        tiles=HEADS * (contact_count - end) + 1,
-    )(*rows, kv, kt, weights, total, dq)
+        tiles=HEADS * (plan[3] - plan[2]) + 1,
+    )(*early, *late, kv, kt, weights, total, dq)
     joined = call(
         join_kernel,
         [((BLOCK + half, LANES), bf16)] * HEADS,
@@ -349,7 +402,9 @@
         unpack_kernel,
         [((BLOCK, width), bf16)] * 3,
         [VMEM] * HEADS,
-        [pltpu.VMEM((HEADS, BLOCK + half, LANES), bf16)],
+        [pltpu.VMEM((BLOCK, width), bf16)] * 3
+        + [pltpu.VMEM((HEADS, BLOCK + half, LANES), bf16), pltpu.SemaphoreType.DMA((3,))],
+        out_space=HBM,
     )(*[back[s] for s in (0,) + ORDER_BACK])
 
 

time: 40.6 us -> 39.3 us (0.968)
  waiting for transfers between devices: 7.71 us -> 4.93 us
  starting transfers between devices: 24.7 us -> 26 us
    ppermute x14, waiting for transfers between devices: 6.69 us -> 3.08 us  [exchange(): moved[s] = lax.ppermute(parts[s], ('across', 'col'), pairs)]
    pallas_call x1 -> x3, Pallas kernels: 0.96 us -> 2.68 us  [the longest x1 1.79 us: body(): call(lambda *refs: early_kernel(sizes, *refs), held, [VMEM] * (len(EARLY)...]
    pallas_call x1, Pallas kernels: 2.84 us -> 1.38 us  [body(): call(lambda *refs: second_kernel(sizes, *refs), [held[0], held[1], held[3...]
    ppermute x1 -> x4, starting transfers between devices: 0.01 us -> 0.94 us  [gather_keys(): return lax.ppermute(own, 'share', [(0, 1), (1, 0)])]
    ppermute x1 -> x4, waiting for transfers between devices: 0.56 us -> 1.42 us  [gather_keys(): return lax.ppermute(own, 'share', [(0, 1), (1, 0)])]
  transfers between devices with their start and end apart: 16 -> 19, of which waited for: 8 -> 8; matrix products, arithmetic and copies ran while one was open for 0% -> 0% of each run, Pallas kernels for 5% -> 9%
where the time goes in v4:
time: 39.3 us; the launch traced here: 39.2 us
  starting transfers between devices  26 us (66%)
  Pallas kernels  7.47 us (19%)
  waiting for transfers between devices  4.93 us (13%)
  between operations  0.76 us (2%)
    ppermute x14, starting transfers between devices, exchange(): moved[s] = lax.ppermute(parts[s], ('across', 'col'), pairs)  24.8 us
    ppermute x14, waiting for transfers between devices, exchange(): moved[s] = lax.ppermute(parts[s], ('across', 'col'), pairs)  3.08 us
    pallas_call x1, Pallas kernels, body(): call(lambda *refs: early_kernel(sizes, *refs), held, [VMEM] * (len(EARLY)...  1.79 us
    pallas_call x1, Pallas kernels, body(): call(lambda *refs: pack_kernel(sizes, *refs), [((length, LANES), bf16)] *...  1.49 us
    ppermute x4, waiting for transfers between devices, gather_keys(): return lax.ppermute(own, 'share', [(0, 1), (1, 0)])  1.42 us
    pallas_call x1, Pallas kernels, body(): call(lambda *refs: second_kernel(sizes, *refs), [held[0], held[1], held[3...  1.38 us
    pallas_call x1, Pallas kernels, body(): call(lambda *refs: third_kernel(sizes, *refs), [((HEADS, BLOCK, LANES), f...  0.94 us
    ppermute x4, starting transfers between devices, gather_keys(): return lax.ppermute(own, 'share', [(0, 1), (1, 0)])  0.94 us
  transfers between devices with their start and end apart: 19, of which 8 were waited for; matrix products, arithmetic and copies ran while one was open for 0% of the time, Pallas kernels for 9%

profile of v4, /device:TPU:0, one launch (start us, length us, event | category | flops | bytes accessed | tf_op | source)
XLA Modules:
  0.0 39.2 jit_solution(236577454686146362)
XLA Ops:
  0.6 1.5 %shard_map.94 = (bf16[272,128]{1,0:T(8,128)(2,1)S(1)}, bf16[272,128]{1,0:T(8,128)(2,1)S(1)}, bf16[272,128]{1,0:T(8,128)(2,1)S(1)}, bf16[272,128]{1,0:T(8,128)(2,...) custom-call(s32[4,12]{1,0:T(4,128)} %refs_0_.1, ...), custom_call_target="tpu_custom_call" | custom-call | tf_op jit(solution)/shard_map/pallas_call | solution.py:342
  2.1 3.0 %collective-permute-start = (bf16[272,128]{1,0:T(8,128)(2,1)S(1)}, bf16[272,128]{1,0:T(8,128)(2,1)S(1)}, u32[]{:S(2)}, u32[]{:S(2)}) collective-permute-start(bf16[272,128]{1,0:T(8,128)(2,1)S(1)} %get-tuple-element.37), channel_id=1, source_target_pairs={{0,8},{1,9},{2,10},{3,11},{8,0},{9,1},{10,2},{11,3},{4,12},{5,13},... | collective-permute-start | bytes 208904 | tf_op jit(solution)/shard_map/ppermute | solution.py:291
  5.1 2.6 %collective-permute-start.1 = (bf16[272,128]{1,0:T(8,128)(2,1)S(1)}, bf16[272,128]{1,0:T(8,128)(2,1)S(1)}, u32[]{:S(2)}, u32[]{:S(2)}) collective-permute-start(bf16[272,128]{1,0:T(8,128)(2,1)S(1)} %get-tuple-element.38), channel_id=1, source_target_pairs={{0,2},{1,3},{2,0},{3,1},{8,10},{9,11},{10,8},{11,9},{4,6},{5,7},{6... | collective-permute-start | bytes 208904 | tf_op jit(solution)/shard_map/ppermute | solution.py:291
  7.7 1.3 %collective-permute-start.2 = (bf16[272,128]{1,0:T(8,128)(2,1)S(1)}, bf16[272,128]{1,0:T(8,128)(2,1)S(1)}, u32[]{:S(2)}, u32[]{:S(2)}) collective-permute-start(bf16[272,128]{1,0:T(8,128)(2,1)S(1)} %get-tuple-element.39), channel_id=1, source_target_pairs={{0,11},{1,10},{2,9},{3,8},{8,3},{9,2},{10,1},{11,0},{4,15},{5,14},... | collective-permute-start | bytes 208904 | tf_op jit(solution)/shard_map/ppermute | solution.py:291
  9.0 0.5 %collective-permute-start.3 = (bf16[272,128]{1,0:T(8,128)(2,1)S(1)}, bf16[272,128]{1,0:T(8,128)(2,1)S(1)}, u32[]{:S(2)}, u32[]{:S(2)}) collective-permute-start(bf16[272,128]{1,0:T(8,128)(2,1)S(1)} %get-tuple-element.40), channel_id=1, source_target_pairs={{0,9},{1,8},{2,11},{3,10},{8,1},{9,0},{10,3},{11,2},{4,13},{5,12},... | collective-permute-start | bytes 208904 | tf_op jit(solution)/shard_map/ppermute | solution.py:291
  9.5 2.5 %collective-permute-start.4 = (bf16[272,128]{1,0:T(8,128)(2,1)S(1)}, bf16[272,128]{1,0:T(8,128)(2,1)S(1)}, u32[]{:S(2)}, u32[]{:S(2)}) collective-permute-start(bf16[272,128]{1,0:T(8,128)(2,1)S(1)} %get-tuple-element.41), channel_id=1, source_target_pairs={{0,1},{1,0},{2,3},{3,2},{8,9},{9,8},{10,11},{11,10},{4,5},{5,4},{6... | collective-permute-start | bytes 208904 | tf_op jit(solution)/shard_map/ppermute | solution.py:291
  12.0 1.7 %collective-permute-start.5 = (bf16[272,128]{1,0:T(8,128)(2,1)S(1)}, bf16[272,128]{1,0:T(8,128)(2,1)S(1)}, u32[]{:S(2)}, u32[]{:S(2)}) collective-permute-start(bf16[272,128]{1,0:T(8,128)(2,1)S(1)} %get-tuple-element.42), channel_id=1, source_target_pairs={{0,10},{1,11},{2,8},{3,9},{8,2},{9,3},{10,0},{11,1},{4,14},{5,15},... | collective-permute-start | bytes 208904 | tf_op jit(solution)/shard_map/ppermute | solution.py:291
  13.7 2.8 %collective-permute-start.6 = (bf16[272,128]{1,0:T(8,128)(2,1)S(1)}, bf16[272,128]{1,0:T(8,128)(2,1)S(1)}, u32[]{:S(2)}, u32[]{:S(2)}) collective-permute-start(bf16[272,128]{1,0:T(8,128)(2,1)S(1)} %get-tuple-element.43), channel_id=1, source_target_pairs={{0,3},{1,2},{2,1},{3,0},{8,11},{9,10},{10,9},{11,8},{4,7},{5,6},{6... | collective-permute-start | bytes 208904 | tf_op jit(solution)/shard_map/ppermute | solution.py:291
  16.6 0.5 %collective-permute-start.8 = (bf16[256,128]{1,0:T(8,128)(2,1)S(1)}, bf16[256,128]{1,0:T(8,128)(2,1)S(1)}, u32[]{:S(2)}, u32[]{:S(2)}) collective-permute-start(bf16[256,128]{1,0:T(8,128)(2,1)S(1)} %pad_maximum_fusion.1), channel_id=1, source_target_pairs={{0,4},{4,0},{1,5},{5,1},{2,6},{6,2},{3,7},{7,3},{8,12},{12,8},{9,1... | collective-permute-start | bytes 196616 | tf_op jit(solution)/shard_map/ppermute | solution.py:297
  17.3 0.5 %collective-permute-done.7.refs_6_ = bf16[256,128]{1,0:T(8,128)(2,1)S(1)} collective-permute-done((bf16[256,128]{1,0:T(8,128)(2,1)S(1)}, bf16[256,128]{1,0:T(8,128)(2,1)S(1)}, u32[]{:S(2)}, u32[]{:S(2)}) %collective-permute-start.7) | collective-permute-done | bytes 65568 | tf_op jit(solution)/shard_map/ppermute | solution.py:297
  18.1 0.4 %collective-permute-done.9.refs_8_ = bf16[256,128]{1,0:T(8,128)(2,1)S(1)} collective-permute-done((bf16[256,128]{1,0:T(8,128)(2,1)S(1)}, bf16[256,128]{1,0:T(8,128)(2,1)S(1)}, u32[]{:S(2)}, u32[]{:S(2)}) %collective-permute-start.9) | collective-permute-done | bytes 65568 | tf_op jit(solution)/shard_map/ppermute | solution.py:297
  18.5 1.8 %shard_map.95 = (bf16[16,128,128]{2,1,0:T(8,128)(2,1)S(1)}, bf16[16,64,128]{2,1,0:T(8,128)(2,1)S(1)}, bf16[8,256,128]{2,1,0:T(8,128)(2,1)S(1)}, f32[16,128,128]{2,1,0:T(8,128)S(1)}, f32[8,64,128]{2,1,0:T(8,128)S(1)}) custom-call(bf16[272,128]{1,0:T(8,128)(2,1)S(1)} %get-tuple-element.36.refs_0_, bf16[272,128]{1,0:T(8,128)(2,1)S(1)} %collective-permute-done.refs_1_, ...), custom_call_target="tpu_custom_call" | custom-call | tf_op jit(solution)/shard_map/pallas_call | solution.py:366
  20.6 0.9 %shard_map.97 = (bf16[16,128,128]{2,1,0:T(8,128)(2,1)S(1)}, bf16[16,64,128]{2,1,0:T(8,128)(2,1)S(1)}, bf16[8,256,128]{2,1,0:T(8,128)(2,1)S(1)}, f32[16,128,128]{2,1,0:T(8,128)S(1)}, f32[8,64,128]{2,1,0:T(8,128)S(1)}) custom-call(bf16[272,128]{1,0:T(8,128)(2,1)S(1)} %get-tuple-element.3, ...), custom_call_target="tpu_custom_call", output_to_operand_aliasing={{0}: (8, {}), {1}: (9, {}), {2}: (10, {}), {3}: (11, {}), {... | custom-call | flops 293601280 | bytes 458752 | tf_op jit(solution)/shard_map/pallas_call | solution.py:373
  21.7 1.4 %shard_map.98 = (bf16[16,128,128]{2,1,0:T(8,128)(2,1)S(1)}, bf16[16,64,128]{2,1,0:T(8,128)(2,1)S(1)}, f32[16,128,128]{2,1,0:T(8,128)S(1)}, f32[8,64,128]{2,1,0:T(8,128)S(1)}, bf16[8,128,128]{2,1,0:T(8,128)(2,1)S(1)}) custom-call(bf16[272,128]{1,0:T(8,128)(2,1)S(1)} %get-tuple-element.36.re, ...), custom_call_target="tpu_custom_call", output_to_operand_aliasing={{0}: (9, {}), {1}: (10, {}), {2}: (12, {}), {3}: (13, {})} | custom-call | flops 293601280 | bytes 458752 | tf_op jit(solution)/shard_map/pallas_call | solution.py:380
  23.3 0.9 %shard_map.99 = (f32[8,128,128]{2,1,0:T(8,128)S(1)}, bf16[8,64,128]{2,1,0:T(8,128)(2,1)S(1)}) custom-call(bf16[272,128]{1,0:T(8,128)(2,1)S(1)} %get-tuple-element.36.refs_0_, bf16[272,128]{1,0:T(8,128)(2,1)S(1)} %collective-permute-done.refs_1_, bf16[272,128]{1,0:T(8,128)(2,1)S(1)} %collective-permute-done.1.refs_2_, ...), custom_call_target="tpu_custom_call" | custom-call | flops 178257920 | bytes 278528 | tf_op jit(solution)/shard_map/pallas_call | solution.py:388
  24.7 2.3 %collective-permute-start.12 = (bf16[192,128]{1,0:T(8,128)(2,1)S(1)}, bf16[192,128]{1,0:T(8,128)(2,1)S(1)}, u32[]{:S(2)}, u32[]{:S(2)}) collective-permute-start(bf16[192,128]{1,0:T(8,128)(2,1)S(1)} %get-tuple-element.62), channel_id=1, source_target_pairs={{0,3},{1,2},{2,1},{3,0},{8,11},{9,10},{10,9},{11,8},{4,7},{5,6},{6... | collective-permute-start | bytes 147464 | tf_op jit(solution)/shard_map/ppermute | solution.py:291
  27.1 0.4 %collective-permute-start.13 = (bf16[192,128]{1,0:T(8,128)(2,1)S(1)}, bf16[192,128]{1,0:T(8,128)(2,1)S(1)}, u32[]{:S(2)}, u32[]{:S(2)}) collective-permute-start(bf16[192,128]{1,0:T(8,128)(2,1)S(1)} %get-tuple-element.63), channel_id=1, source_target_pairs={{0,2},{1,3},{2,0},{3,1},{8,10},{9,11},{10,8},{11,9},{4,6},{5,7},{6... | collective-permute-start | bytes 147464 | tf_op jit(solution)/shard_map/ppermute | solution.py:291
  27.5 3.6 %collective-permute-start.14 = (bf16[192,128]{1,0:T(8,128)(2,1)S(1)}, bf16[192,128]{1,0:T(8,128)(2,1)S(1)}, u32[]{:S(2)}, u32[]{:S(2)}) collective-permute-start(bf16[192,128]{1,0:T(8,128)(2,1)S(1)} %get-tuple-element.64), channel_id=1, source_target_pairs={{0,10},{1,11},{2,8},{3,9},{8,2},{9,3},{10,0},{11,1},{4,14},{5,15},... | collective-permute-start | bytes 147464 | tf_op jit(solution)/shard_map/ppermute | solution.py:291
  31.1 1.3 %collective-permute-start.15 = (bf16[192,128]{1,0:T(8,128)(2,1)S(1)}, bf16[192,128]{1,0:T(8,128)(2,1)S(1)}, u32[]{:S(2)}, u32[]{:S(2)}) collective-permute-start(bf16[192,128]{1,0:T(8,128)(2,1)S(1)} %get-tuple-element.65), channel_id=1, source_target_pairs={{0,11},{1,10},{2,9},{3,8},{8,3},{9,2},{10,1},{11,0},{4,15},{5,14},... | collective-permute-start | bytes 147464 | tf_op jit(solution)/shard_map/ppermute | solution.py:291
  32.6 0.9 %collective-permute-start.17 = (bf16[192,128]{1,0:T(8,128)(2,1)S(1)}, bf16[192,128]{1,0:T(8,128)(2,1)S(1)}, u32[]{:S(2)}, u32[]{:S(2)}) collective-permute-start(bf16[192,128]{1,0:T(8,128)(2,1)S(1)} %get-tuple-element.67), channel_id=1, source_target_pairs={{0,8},{1,9},{2,10},{3,11},{8,0},{9,1},{10,2},{11,3},{4,12},{5,13},... | collective-permute-start | bytes 147464 | tf_op jit(solution)/shard_map/ppermute | solution.py:291
  33.4 0.7 %collective-permute-done.13.rest_2_ = bf16[192,128]{1,0:T(8,128)(2,1)S(1)} collective-permute-done((bf16[192,128]{1,0:T(8,128)(2,1)S(1)}, bf16[192,128]{1,0:T(8,128)(2,1)S(1)}, u32[]{:S(2)}, u32[]{:S(2)}) %collective-permute-start.13) | collective-permute-done | bytes 49184 | tf_op jit(solution)/shard_map/ppermute | solution.py:291
  34.2 1.8 %collective-permute-start.18 = (bf16[192,128]{1,0:T(8,128)(2,1)S(1)}, bf16[192,128]{1,0:T(8,128)(2,1)S(1)}, u32[]{:S(2)}, u32[]{:S(2)}) collective-permute-start(bf16[192,128]{1,0:T(8,128)(2,1)S(1)} %get-tuple-element.68), channel_id=1, source_target_pairs={{0,1},{1,0},{2,3},{3,2},{8,9},{9,8},{10,11},{11,10},{4,5},{5,4},{6... | collective-permute-start | bytes 147464 | tf_op jit(solution)/shard_map/ppermute | solution.py:291
  35.9 2.0 %collective-permute-done.15.rest_4_ = bf16[192,128]{1,0:T(8,128)(2,1)S(1)} collective-permute-done((bf16[192,128]{1,0:T(8,128)(2,1)S(1)}, bf16[192,128]{1,0:T(8,128)(2,1)S(1)}, u32[]{:S(2)}, u32[]{:S(2)}) %collective-permute-start.15) | collective-permute-done | bytes 49184 | tf_op jit(solution)/shard_map/ppermute | solution.py:291
  38.3 0.9 %shard_map.101 = (bf16[128,512]{1,0:T(8,128)(2,1)}, bf16[128,512]{1,0:T(8,128)(2,1)}, bf16[128,512]{1,0:T(8,128)(2,1)}) custom-call(bf16[192,128]{1,0:T(8,128)(2,1)S(1)} %get-tuple-element.61.rest_0_, bf16[192,128]{1,0:T(8,128)(2,1)S(1)} %collective-permute-done.12.rest_1_, bf16[192,128]{1,0:T(8,128)(2,1)S(1)} %collective-permute-done.13.rest_2_, ...), custom_call_target="tpu_custom_call" | custom-call | tf_op jit(solution)/shard_map/pallas_call | solution.py:401
  (31 shorter events, 2.0 us)
Async XLA Ops:
  2.1 9.9 %collective-permute-start = (bf16[272,128]{1,0:T(8,128)(2,1)S(1)}, bf16[272,128]{1,0:T(8,128)(2,1)S(1)}, u32[]{:S(2)}, u32[]{:S(2)}) collective-permute-start(bf16[272,128]{1,0:T(8,128)(2,1)S(1)} %get-tuple-element.37), channel_id=1, source_target_pairs={{0,8},{1,9},{2,10},{3,11},{8,0},{9,1},{10,2},{11,3},{4,12},{5,13},... | collective-permute-start | bytes 208904 | tf_op jit(solution)/shard_map/ppermute | solution.py:291
  5.1 8.5 %collective-permute-start.1 = (bf16[272,128]{1,0:T(8,128)(2,1)S(1)}, bf16[272,128]{1,0:T(8,128)(2,1)S(1)}, u32[]{:S(2)}, u32[]{:S(2)}) collective-permute-start(bf16[272,128]{1,0:T(8,128)(2,1)S(1)} %get-tuple-element.38), channel_id=1, source_target_pairs={{0,2},{1,3},{2,0},{3,1},{8,10},{9,11},{10,8},{11,9},{4,6},{5,7},{6... | collective-permute-start | bytes 208904 | tf_op jit(solution)/shard_map/ppermute | solution.py:291
  7.7 8.8 %collective-permute-start.2 = (bf16[272,128]{1,0:T(8,128)(2,1)S(1)}, bf16[272,128]{1,0:T(8,128)(2,1)S(1)}, u32[]{:S(2)}, u32[]{:S(2)}) collective-permute-start(bf16[272,128]{1,0:T(8,128)(2,1)S(1)} %get-tuple-element.39), channel_id=1, source_target_pairs={{0,11},{1,10},{2,9},{3,8},{8,3},{9,2},{10,1},{11,0},{4,15},{5,14},... | collective-permute-start | bytes 208904 | tf_op jit(solution)/shard_map/ppermute | solution.py:291
  9.0 7.6 %collective-permute-start.3 = (bf16[272,128]{1,0:T(8,128)(2,1)S(1)}, bf16[272,128]{1,0:T(8,128)(2,1)S(1)}, u32[]{:S(2)}, u32[]{:S(2)}) collective-permute-start(bf16[272,128]{1,0:T(8,128)(2,1)S(1)} %get-tuple-element.40), channel_id=1, source_target_pairs={{0,9},{1,8},{2,11},{3,10},{8,1},{9,0},{10,3},{11,2},{4,13},{5,12},... | collective-permute-start | bytes 208904 | tf_op jit(solution)/shard_map/ppermute | solution.py:291
  9.5 7.7 %collective-permute-start.4 = (bf16[272,128]{1,0:T(8,128)(2,1)S(1)}, bf16[272,128]{1,0:T(8,128)(2,1)S(1)}, u32[]{:S(2)}, u32[]{:S(2)}) collective-permute-start(bf16[272,128]{1,0:T(8,128)(2,1)S(1)} %get-tuple-element.41), channel_id=1, source_target_pairs={{0,1},{1,0},{2,3},{3,2},{8,9},{9,8},{10,11},{11,10},{4,5},{5,4},{6... | collective-permute-start | bytes 208904 | tf_op jit(solution)/shard_map/ppermute | solution.py:291
  12.0 8.3 %collective-permute-start.5 = (bf16[272,128]{1,0:T(8,128)(2,1)S(1)}, bf16[272,128]{1,0:T(8,128)(2,1)S(1)}, u32[]{:S(2)}, u32[]{:S(2)}) collective-permute-start(bf16[272,128]{1,0:T(8,128)(2,1)S(1)} %get-tuple-element.42), channel_id=1, source_target_pairs={{0,10},{1,11},{2,8},{3,9},{8,2},{9,3},{10,0},{11,1},{4,14},{5,15},... | collective-permute-start | bytes 208904 | tf_op jit(solution)/shard_map/ppermute | solution.py:291
  13.7 6.7 %collective-permute-start.6 = (bf16[272,128]{1,0:T(8,128)(2,1)S(1)}, bf16[272,128]{1,0:T(8,128)(2,1)S(1)}, u32[]{:S(2)}, u32[]{:S(2)}) collective-permute-start(bf16[272,128]{1,0:T(8,128)(2,1)S(1)} %get-tuple-element.43), channel_id=1, source_target_pairs={{0,3},{1,2},{2,1},{3,0},{8,11},{9,10},{10,9},{11,8},{4,7},{5,6},{6... | collective-permute-start | bytes 208904 | tf_op jit(solution)/shard_map/ppermute | solution.py:291
  16.5 1.3 %collective-permute-start.7 = (bf16[256,128]{1,0:T(8,128)(2,1)S(1)}, bf16[256,128]{1,0:T(8,128)(2,1)S(1)}, u32[]{:S(2)}, u32[]{:S(2)}) collective-permute-start(bf16[256,128]{1,0:T(8,128)(2,1)S(1)} %pad_maximum_fusion), channel_id=1, source_target_pairs={{0,4},{4,0},{1,5},{5,1},{2,6},{6,2},{3,7},{7,3},{8,12},{12,8},{9,1... | collective-permute-start | bytes 196616 | tf_op jit(solution)/shard_map/ppermute | solution.py:297
  16.6 1.4 %collective-permute-start.8 = (bf16[256,128]{1,0:T(8,128)(2,1)S(1)}, bf16[256,128]{1,0:T(8,128)(2,1)S(1)}, u32[]{:S(2)}, u32[]{:S(2)}) collective-permute-start(bf16[256,128]{1,0:T(8,128)(2,1)S(1)} %pad_maximum_fusion.1), channel_id=1, source_target_pairs={{0,4},{4,0},{1,5},{5,1},{2,6},{6,2},{3,7},{7,3},{8,12},{12,8},{9,1... | collective-permute-start | bytes 196616 | tf_op jit(solution)/shard_map/ppermute | solution.py:297
  17.2 1.3 %collective-permute-start.9 = (bf16[256,128]{1,0:T(8,128)(2,1)S(1)}, bf16[256,128]{1,0:T(8,128)(2,1)S(1)}, u32[]{:S(2)}, u32[]{:S(2)}) collective-permute-start(bf16[256,128]{1,0:T(8,128)(2,1)S(1)} %pad_maximum_fusion.2), channel_id=1, source_target_pairs={{0,4},{4,0},{1,5},{5,1},{2,6},{6,2},{3,7},{7,3},{8,12},{12,8},{9,1... | collective-permute-start | bytes 196616 | tf_op jit(solution)/shard_map/ppermute | solution.py:297
  20.3 1.3 %collective-permute-start.10 = (bf16[256,128]{1,0:T(8,128)(2,1)S(1)}, bf16[256,128]{1,0:T(8,128)(2,1)S(1)}, u32[]{:S(2)}, u32[]{:S(2)}) collective-permute-start(bf16[256,128]{1,0:T(8,128)(2,1)S(1)} %shard_map.96), channel_id=1, source_target_pairs={{0,4},{4,0},{1,5},{5,1},{2,6},{6,2},{3,7},{7,3},{8,12},{12,8},{9,1... | collective-permute-start | bytes 196616 | tf_op jit(solution)/shard_map/ppermute | solution.py:297
  23.1 1.6 %collective-permute-start.11 = (bf16[8,128,128]{2,1,0:T(8,128)(2,1)S(1)}, bf16[8,128,128]{2,1,0:T(8,128)(2,1)S(1)}, u32[]{:S(2)}, u32[]{:S(2)}) collective-permute-start(bf16[8,128,128]{2,1,0:T(8,128)(2,1)S(1)} %get-tuple-element.59), channel_id=1, source_target_pairs={{0,4},{4,0},{1,5},{5,1},{2,6},{6,2},{3,7},{7,3},{8,12},{12,8},{9,1... | collective-permute-start | bytes 786440 | tf_op jit(solution)/shard_map/ppermute | solution.py:304
  24.7 7.8 %collective-permute-start.12 = (bf16[192,128]{1,0:T(8,128)(2,1)S(1)}, bf16[192,128]{1,0:T(8,128)(2,1)S(1)}, u32[]{:S(2)}, u32[]{:S(2)}) collective-permute-start(bf16[192,128]{1,0:T(8,128)(2,1)S(1)} %get-tuple-element.62), channel_id=1, source_target_pairs={{0,3},{1,2},{2,1},{3,0},{8,11},{9,10},{10,9},{11,8},{4,7},{5,6},{6... | collective-permute-start | bytes 147464 | tf_op jit(solution)/shard_map/ppermute | solution.py:291
  27.1 7.1 %collective-permute-start.13 = (bf16[192,128]{1,0:T(8,128)(2,1)S(1)}, bf16[192,128]{1,0:T(8,128)(2,1)S(1)}, u32[]{:S(2)}, u32[]{:S(2)}) collective-permute-start(bf16[192,128]{1,0:T(8,128)(2,1)S(1)} %get-tuple-element.63), channel_id=1, source_target_pairs={{0,2},{1,3},{2,0},{3,1},{8,10},{9,11},{10,8},{11,9},{4,6},{5,7},{6... | collective-permute-start | bytes 147464 | tf_op jit(solution)/shard_map/ppermute | solution.py:291
  27.5 8.4 %collective-permute-start.14 = (bf16[192,128]{1,0:T(8,128)(2,1)S(1)}, bf16[192,128]{1,0:T(8,128)(2,1)S(1)}, u32[]{:S(2)}, u32[]{:S(2)}) collective-permute-start(bf16[192,128]{1,0:T(8,128)(2,1)S(1)} %get-tuple-element.64), channel_id=1, source_target_pairs={{0,10},{1,11},{2,8},{3,9},{8,2},{9,3},{10,0},{11,1},{4,14},{5,15},... | collective-permute-start | bytes 147464 | tf_op jit(solution)/shard_map/ppermute | solution.py:291
  31.1 6.9 %collective-permute-start.15 = (bf16[192,128]{1,0:T(8,128)(2,1)S(1)}, bf16[192,128]{1,0:T(8,128)(2,1)S(1)}, u32[]{:S(2)}, u32[]{:S(2)}) collective-permute-start(bf16[192,128]{1,0:T(8,128)(2,1)S(1)} %get-tuple-element.65), channel_id=1, source_target_pairs={{0,11},{1,10},{2,9},{3,8},{8,3},{9,2},{10,1},{11,0},{4,15},{5,14},... | collective-permute-start | bytes 147464 | tf_op jit(solution)/shard_map/ppermute | solution.py:291
  32.4 5.6 %collective-permute-start.16 = (bf16[192,128]{1,0:T(8,128)(2,1)S(1)}, bf16[192,128]{1,0:T(8,128)(2,1)S(1)}, u32[]{:S(2)}, u32[]{:S(2)}) collective-permute-start(bf16[192,128]{1,0:T(8,128)(2,1)S(1)} %get-tuple-element.66), channel_id=1, source_target_pairs={{0,9},{1,8},{2,11},{3,10},{8,1},{9,0},{10,3},{11,2},{4,13},{5,12},... | collective-permute-start | bytes 147464 | tf_op jit(solution)/shard_map/ppermute | solution.py:291
  32.6 5.5 %collective-permute-start.17 = (bf16[192,128]{1,0:T(8,128)(2,1)S(1)}, bf16[192,128]{1,0:T(8,128)(2,1)S(1)}, u32[]{:S(2)}, u32[]{:S(2)}) collective-permute-start(bf16[192,128]{1,0:T(8,128)(2,1)S(1)} %get-tuple-element.67), channel_id=1, source_target_pairs={{0,8},{1,9},{2,10},{3,11},{8,0},{9,1},{10,2},{11,3},{4,12},{5,13},... | collective-permute-start | bytes 147464 | tf_op jit(solution)/shard_map/ppermute | solution.py:291
  34.2 4.1 %collective-permute-start.18 = (bf16[192,128]{1,0:T(8,128)(2,1)S(1)}, bf16[192,128]{1,0:T(8,128)(2,1)S(1)}, u32[]{:S(2)}, u32[]{:S(2)}) collective-permute-start(bf16[192,128]{1,0:T(8,128)(2,1)S(1)} %get-tuple-element.68), channel_id=1, source_target_pairs={{0,1},{1,0},{2,3},{3,2},{8,9},{9,8},{10,11},{11,10},{4,5},{5,4},{6... | collective-permute-start | bytes 147464 | tf_op jit(solution)/shard_map/ppermute | solution.py:291

commit v5 on v4

--- a/solution.py
+++ b/solution.py
@@ -12,6 +12,7 @@
 LANES = 128
 HEADS = 8
 STATS = 16
+PIECE = 32
 STEP = 2
 AHEAD = 3
 NT = (((1,), (1,)), ((), ()))
@@ -74,17 +75,23 @@
     sources, outs = rest[:6], rest[6 : 6 + HEADS]
     messages, contacts_ref, q_ref, k_ref, v_ref, o_ref, g_ref, norm_ref, sems = rest[6 + HEADS :]
     targets = (q_ref, k_ref, v_ref, o_ref, g_ref, norm_ref)
-    copies = [pltpu.make_async_copy(a, b, sems.at[i]) for i, (a, b) in enumerate(zip(sources, targets))]
-    copies.append(pltpu.make_async_copy(contacts_hbm, contacts_ref, sems.at[6]))
-    for i in (6, 4, 3, 5, 0, 1, 2):
-        copies[i].start()
+    pairs = ((contacts_hbm, contacts_ref),) + tuple(zip(sources, targets))
+
+    def wait(*which):
+        for i in which:
+            pltpu.make_async_copy(*pairs[i], sems.at[i]).wait()
+
+    for i in (0, 5, 4, 6, 1, 2, 3):
+        a, b = pairs[i]
+        size = PIECE if a.shape[0] == BLOCK else a.shape[0]
+        for r in range(0, a.shape[0], size):
+            pltpu.make_async_copy(a.at[pl.ds(r, size)], b.at[pl.ds(r, size)], sems.at[i]).start()
     width = q_ref.shape[1]
     head_dim = width // HEADS
     me, column, share = number(), lax.axis_index("col"), lax.axis_index("share")
-    copies[6].wait()
+    wait(0)
     listed = listed_contacts(contacts_ref, column, share, sizes).astype(jnp.float32)
-    for i in (4, 3, 5):
-        copies[i].wait()
+    wait(5, 4, 6)
     products = g_ref[...].astype(jnp.float32) * o_ref[...].astype(jnp.float32)
     hi = products.astype(jnp.bfloat16)
     lo = (products - hi.astype(jnp.float32)).astype(jnp.bfloat16)
@@ -94,8 +101,7 @@
     delta += lax.dot_general(picks, lo, NT, preferred_element_type=jnp.float32)
     norm_parts = split_three(norm_ref[...])
     delta_parts = split_three(delta)
-    for i in (0, 1, 2):
-        copies[i].wait()
+    wait(1, 2, 3)
     blank = jnp.zeros((STATS - 7, LANES), jnp.float32)
     for h in range(HEADS):
         cols = slice(h * head_dim, (h + 1) * head_dim)

time: 39.3 us -> 39.3 us (level)
  no operation moved by 1% of the time
where the time goes in v5:
time: 39.3 us; the launch traced here: 39.1 us
  starting transfers between devices  26 us (66%)
  Pallas kernels  7.36 us (19%)
  waiting for transfers between devices  4.93 us (13%)
  between operations  0.76 us (2%)
    ppermute x14, starting transfers between devices, exchange(): moved[s] = lax.ppermute(parts[s], ('across', 'col'), pairs)  24.8 us
    ppermute x14, waiting for transfers between devices, exchange(): moved[s] = lax.ppermute(parts[s], ('across', 'col'), pairs)  3.08 us
    pallas_call x1, Pallas kernels, body(): call(lambda *refs: early_kernel(sizes, *refs), held, [VMEM] * (len(EARLY)...  1.79 us
    ppermute x4, waiting for transfers between devices, gather_keys(): return lax.ppermute(own, 'share', [(0, 1), (1, 0)])  1.42 us
    pallas_call x1, Pallas kernels, body(): call(lambda *refs: pack_kernel(sizes, *refs), [((length, LANES), bf16)] *...  1.39 us
    pallas_call x1, Pallas kernels, body(): call(lambda *refs: second_kernel(sizes, *refs), [held[0], held[1], held[3...  1.38 us
    pallas_call x1, Pallas kernels, body(): call(lambda *refs: third_kernel(sizes, *refs), [((HEADS, BLOCK, LANES), f...  0.94 us
    ppermute x4, starting transfers between devices, gather_keys(): return lax.ppermute(own, 'share', [(0, 1), (1, 0)])  0.94 us
  transfers between devices with their start and end apart: 19, of which 8 were waited for; matrix products, arithmetic and copies ran while one was open for 0% of the time, Pallas kernels for 9%

profile of v5, /device:TPU:0, one launch (start us, length us, event | category | flops | bytes accessed | tf_op | source)
XLA Modules:
  0.0 39.1 jit_solution(15003446538476200466)
XLA Ops:
  0.6 1.4 %shard_map.94 = (bf16[272,128]{1,0:T(8,128)(2,1)S(1)}, bf16[272,128]{1,0:T(8,128)(2,1)S(1)}, bf16[272,128]{1,0:T(8,128)(2,1)S(1)}, bf16[272,128]{1,0:T(8,128)(2,...) custom-call(s32[4,12]{1,0:T(4,128)} %refs_0_.1, ...), custom_call_target="tpu_custom_call" | custom-call | tf_op jit(solution)/shard_map/pallas_call | solution.py:348
  2.0 3.0 %collective-permute-start = (bf16[272,128]{1,0:T(8,128)(2,1)S(1)}, bf16[272,128]{1,0:T(8,128)(2,1)S(1)}, u32[]{:S(2)}, u32[]{:S(2)}) collective-permute-start(bf16[272,128]{1,0:T(8,128)(2,1)S(1)} %get-tuple-element.37), channel_id=1, source_target_pairs={{0,8},{1,9},{2,10},{3,11},{8,0},{9,1},{10,2},{11,3},{4,12},{5,13},... | collective-permute-start | bytes 208904 | tf_op jit(solution)/shard_map/ppermute | solution.py:297
  5.0 2.6 %collective-permute-start.1 = (bf16[272,128]{1,0:T(8,128)(2,1)S(1)}, bf16[272,128]{1,0:T(8,128)(2,1)S(1)}, u32[]{:S(2)}, u32[]{:S(2)}) collective-permute-start(bf16[272,128]{1,0:T(8,128)(2,1)S(1)} %get-tuple-element.38), channel_id=1, source_target_pairs={{0,2},{1,3},{2,0},{3,1},{8,10},{9,11},{10,8},{11,9},{4,6},{5,7},{6... | collective-permute-start | bytes 208904 | tf_op jit(solution)/shard_map/ppermute | solution.py:297
  7.6 1.3 %collective-permute-start.2 = (bf16[272,128]{1,0:T(8,128)(2,1)S(1)}, bf16[272,128]{1,0:T(8,128)(2,1)S(1)}, u32[]{:S(2)}, u32[]{:S(2)}) collective-permute-start(bf16[272,128]{1,0:T(8,128)(2,1)S(1)} %get-tuple-element.39), channel_id=1, source_target_pairs={{0,11},{1,10},{2,9},{3,8},{8,3},{9,2},{10,1},{11,0},{4,15},{5,14},... | collective-permute-start | bytes 208904 | tf_op jit(solution)/shard_map/ppermute | solution.py:297
  8.9 0.5 %collective-permute-start.3 = (bf16[272,128]{1,0:T(8,128)(2,1)S(1)}, bf16[272,128]{1,0:T(8,128)(2,1)S(1)}, u32[]{:S(2)}, u32[]{:S(2)}) collective-permute-start(bf16[272,128]{1,0:T(8,128)(2,1)S(1)} %get-tuple-element.40), channel_id=1, source_target_pairs={{0,9},{1,8},{2,11},{3,10},{8,1},{9,0},{10,3},{11,2},{4,13},{5,12},... | collective-permute-start | bytes 208904 | tf_op jit(solution)/shard_map/ppermute | solution.py:297
  9.4 2.5 %collective-permute-start.4 = (bf16[272,128]{1,0:T(8,128)(2,1)S(1)}, bf16[272,128]{1,0:T(8,128)(2,1)S(1)}, u32[]{:S(2)}, u32[]{:S(2)}) collective-permute-start(bf16[272,128]{1,0:T(8,128)(2,1)S(1)} %get-tuple-element.41), channel_id=1, source_target_pairs={{0,1},{1,0},{2,3},{3,2},{8,9},{9,8},{10,11},{11,10},{4,5},{5,4},{6... | collective-permute-start | bytes 208904 | tf_op jit(solution)/shard_map/ppermute | solution.py:297
  11.9 1.7 %collective-permute-start.5 = (bf16[272,128]{1,0:T(8,128)(2,1)S(1)}, bf16[272,128]{1,0:T(8,128)(2,1)S(1)}, u32[]{:S(2)}, u32[]{:S(2)}) collective-permute-start(bf16[272,128]{1,0:T(8,128)(2,1)S(1)} %get-tuple-element.42), channel_id=1, source_target_pairs={{0,10},{1,11},{2,8},{3,9},{8,2},{9,3},{10,0},{11,1},{4,14},{5,15},... | collective-permute-start | bytes 208904 | tf_op jit(solution)/shard_map/ppermute | solution.py:297
  13.6 2.8 %collective-permute-start.6 = (bf16[272,128]{1,0:T(8,128)(2,1)S(1)}, bf16[272,128]{1,0:T(8,128)(2,1)S(1)}, u32[]{:S(2)}, u32[]{:S(2)}) collective-permute-start(bf16[272,128]{1,0:T(8,128)(2,1)S(1)} %get-tuple-element.43), channel_id=1, source_target_pairs={{0,3},{1,2},{2,1},{3,0},{8,11},{9,10},{10,9},{11,8},{4,7},{5,6},{6... | collective-permute-start | bytes 208904 | tf_op jit(solution)/shard_map/ppermute | solution.py:297
  16.5 0.5 %collective-permute-start.8 = (bf16[256,128]{1,0:T(8,128)(2,1)S(1)}, bf16[256,128]{1,0:T(8,128)(2,1)S(1)}, u32[]{:S(2)}, u32[]{:S(2)}) collective-permute-start(bf16[256,128]{1,0:T(8,128)(2,1)S(1)} %pad_maximum_fusion.1), channel_id=1, source_target_pairs={{0,4},{4,0},{1,5},{5,1},{2,6},{6,2},{3,7},{7,3},{8,12},{12,8},{9,1... | collective-permute-start | bytes 196616 | tf_op jit(solution)/shard_map/ppermute | solution.py:303
  17.2 0.5 %collective-permute-done.7.refs_6_ = bf16[256,128]{1,0:T(8,128)(2,1)S(1)} collective-permute-done((bf16[256,128]{1,0:T(8,128)(2,1)S(1)}, bf16[256,128]{1,0:T(8,128)(2,1)S(1)}, u32[]{:S(2)}, u32[]{:S(2)}) %collective-permute-start.7) | collective-permute-done | bytes 65568 | tf_op jit(solution)/shard_map/ppermute | solution.py:303
  18.0 0.4 %collective-permute-done.9.refs_8_ = bf16[256,128]{1,0:T(8,128)(2,1)S(1)} collective-permute-done((bf16[256,128]{1,0:T(8,128)(2,1)S(1)}, bf16[256,128]{1,0:T(8,128)(2,1)S(1)}, u32[]{:S(2)}, u32[]{:S(2)}) %collective-permute-start.9) | collective-permute-done | bytes 65568 | tf_op jit(solution)/shard_map/ppermute | solution.py:303
  18.4 1.8 %shard_map.95 = (bf16[16,128,128]{2,1,0:T(8,128)(2,1)S(1)}, bf16[16,64,128]{2,1,0:T(8,128)(2,1)S(1)}, bf16[8,256,128]{2,1,0:T(8,128)(2,1)S(1)}, f32[16,128,128]{2,1,0:T(8,128)S(1)}, f32[8,64,128]{2,1,0:T(8,128)S(1)}) custom-call(bf16[272,128]{1,0:T(8,128)(2,1)S(1)} %get-tuple-element.36.refs_0_, bf16[272,128]{1,0:T(8,128)(2,1)S(1)} %collective-permute-done.refs_1_, ...), custom_call_target="tpu_custom_call" | custom-call | tf_op jit(solution)/shard_map/pallas_call | solution.py:372
  20.5 0.9 %shard_map.97 = (bf16[16,128,128]{2,1,0:T(8,128)(2,1)S(1)}, bf16[16,64,128]{2,1,0:T(8,128)(2,1)S(1)}, bf16[8,256,128]{2,1,0:T(8,128)(2,1)S(1)}, f32[16,128,128]{2,1,0:T(8,128)S(1)}, f32[8,64,128]{2,1,0:T(8,128)S(1)}) custom-call(bf16[272,128]{1,0:T(8,128)(2,1)S(1)} %get-tuple-element.3, ...), custom_call_target="tpu_custom_call", output_to_operand_aliasing={{0}: (8, {}), {1}: (9, {}), {2}: (10, {}), {3}: (11, {}), {... | custom-call | flops 293601280 | bytes 458752 | tf_op jit(solution)/shard_map/pallas_call | solution.py:379
  21.6 1.4 %shard_map.98 = (bf16[16,128,128]{2,1,0:T(8,128)(2,1)S(1)}, bf16[16,64,128]{2,1,0:T(8,128)(2,1)S(1)}, f32[16,128,128]{2,1,0:T(8,128)S(1)}, f32[8,64,128]{2,1,0:T(8,128)S(1)}, bf16[8,128,128]{2,1,0:T(8,128)(2,1)S(1)}) custom-call(bf16[272,128]{1,0:T(8,128)(2,1)S(1)} %get-tuple-element.36.re, ...), custom_call_target="tpu_custom_call", output_to_operand_aliasing={{0}: (9, {}), {1}: (10, {}), {2}: (12, {}), {3}: (13, {})} | custom-call | flops 293601280 | bytes 458752 | tf_op jit(solution)/shard_map/pallas_call | solution.py:386
  23.2 0.9 %shard_map.99 = (f32[8,128,128]{2,1,0:T(8,128)S(1)}, bf16[8,64,128]{2,1,0:T(8,128)(2,1)S(1)}) custom-call(bf16[272,128]{1,0:T(8,128)(2,1)S(1)} %get-tuple-element.36.refs_0_, bf16[272,128]{1,0:T(8,128)(2,1)S(1)} %collective-permute-done.refs_1_, bf16[272,128]{1,0:T(8,128)(2,1)S(1)} %collective-permute-done.1.refs_2_, ...), custom_call_target="tpu_custom_call" | custom-call | flops 178257920 | bytes 278528 | tf_op jit(solution)/shard_map/pallas_call | solution.py:394
  24.6 2.3 %collective-permute-start.12 = (bf16[192,128]{1,0:T(8,128)(2,1)S(1)}, bf16[192,128]{1,0:T(8,128)(2,1)S(1)}, u32[]{:S(2)}, u32[]{:S(2)}) collective-permute-start(bf16[192,128]{1,0:T(8,128)(2,1)S(1)} %get-tuple-element.62), channel_id=1, source_target_pairs={{0,3},{1,2},{2,1},{3,0},{8,11},{9,10},{10,9},{11,8},{4,7},{5,6},{6... | collective-permute-start | bytes 147464 | tf_op jit(solution)/shard_map/ppermute | solution.py:297
  27.0 0.4 %collective-permute-start.13 = (bf16[192,128]{1,0:T(8,128)(2,1)S(1)}, bf16[192,128]{1,0:T(8,128)(2,1)S(1)}, u32[]{:S(2)}, u32[]{:S(2)}) collective-permute-start(bf16[192,128]{1,0:T(8,128)(2,1)S(1)} %get-tuple-element.63), channel_id=1, source_target_pairs={{0,2},{1,3},{2,0},{3,1},{8,10},{9,11},{10,8},{11,9},{4,6},{5,7},{6... | collective-permute-start | bytes 147464 | tf_op jit(solution)/shard_map/ppermute | solution.py:297
  27.4 3.6 %collective-permute-start.14 = (bf16[192,128]{1,0:T(8,128)(2,1)S(1)}, bf16[192,128]{1,0:T(8,128)(2,1)S(1)}, u32[]{:S(2)}, u32[]{:S(2)}) collective-permute-start(bf16[192,128]{1,0:T(8,128)(2,1)S(1)} %get-tuple-element.64), channel_id=1, source_target_pairs={{0,10},{1,11},{2,8},{3,9},{8,2},{9,3},{10,0},{11,1},{4,14},{5,15},... | collective-permute-start | bytes 147464 | tf_op jit(solution)/shard_map/ppermute | solution.py:297
  31.0 1.3 %collective-permute-start.15 = (bf16[192,128]{1,0:T(8,128)(2,1)S(1)}, bf16[192,128]{1,0:T(8,128)(2,1)S(1)}, u32[]{:S(2)}, u32[]{:S(2)}) collective-permute-start(bf16[192,128]{1,0:T(8,128)(2,1)S(1)} %get-tuple-element.65), channel_id=1, source_target_pairs={{0,11},{1,10},{2,9},{3,8},{8,3},{9,2},{10,1},{11,0},{4,15},{5,14},... | collective-permute-start | bytes 147464 | tf_op jit(solution)/shard_map/ppermute | solution.py:297
  32.5 0.9 %collective-permute-start.17 = (bf16[192,128]{1,0:T(8,128)(2,1)S(1)}, bf16[192,128]{1,0:T(8,128)(2,1)S(1)}, u32[]{:S(2)}, u32[]{:S(2)}) collective-permute-start(bf16[192,128]{1,0:T(8,128)(2,1)S(1)} %get-tuple-element.67), channel_id=1, source_target_pairs={{0,8},{1,9},{2,10},{3,11},{8,0},{9,1},{10,2},{11,3},{4,12},{5,13},... | collective-permute-start | bytes 147464 | tf_op jit(solution)/shard_map/ppermute | solution.py:297
  33.3 0.7 %collective-permute-done.13.rest_2_ = bf16[192,128]{1,0:T(8,128)(2,1)S(1)} collective-permute-done((bf16[192,128]{1,0:T(8,128)(2,1)S(1)}, bf16[192,128]{1,0:T(8,128)(2,1)S(1)}, u32[]{:S(2)}, u32[]{:S(2)}) %collective-permute-start.13) | collective-permute-done | bytes 49184 | tf_op jit(solution)/shard_map/ppermute | solution.py:297
  34.1 1.8 %collective-permute-start.18 = (bf16[192,128]{1,0:T(8,128)(2,1)S(1)}, bf16[192,128]{1,0:T(8,128)(2,1)S(1)}, u32[]{:S(2)}, u32[]{:S(2)}) collective-permute-start(bf16[192,128]{1,0:T(8,128)(2,1)S(1)} %get-tuple-element.68), channel_id=1, source_target_pairs={{0,1},{1,0},{2,3},{3,2},{8,9},{9,8},{10,11},{11,10},{4,5},{5,4},{6... | collective-permute-start | bytes 147464 | tf_op jit(solution)/shard_map/ppermute | solution.py:297
  35.8 2.0 %collective-permute-done.15.rest_4_ = bf16[192,128]{1,0:T(8,128)(2,1)S(1)} collective-permute-done((bf16[192,128]{1,0:T(8,128)(2,1)S(1)}, bf16[192,128]{1,0:T(8,128)(2,1)S(1)}, u32[]{:S(2)}, u32[]{:S(2)}) %collective-permute-start.15) | collective-permute-done | bytes 49184 | tf_op jit(solution)/shard_map/ppermute | solution.py:297
  38.2 0.9 %shard_map.101 = (bf16[128,512]{1,0:T(8,128)(2,1)}, bf16[128,512]{1,0:T(8,128)(2,1)}, bf16[128,512]{1,0:T(8,128)(2,1)}) custom-call(bf16[192,128]{1,0:T(8,128)(2,1)S(1)} %get-tuple-element.61.rest_0_, bf16[192,128]{1,0:T(8,128)(2,1)S(1)} %collective-permute-done.12.rest_1_, bf16[192,128]{1,0:T(8,128)(2,1)S(1)} %collective-permute-done.13.rest_2_, ...), custom_call_target="tpu_custom_call" | custom-call | tf_op jit(solution)/shard_map/pallas_call | solution.py:407
  (31 shorter events, 2.0 us)
Async XLA Ops:
  2.0 9.9 %collective-permute-start = (bf16[272,128]{1,0:T(8,128)(2,1)S(1)}, bf16[272,128]{1,0:T(8,128)(2,1)S(1)}, u32[]{:S(2)}, u32[]{:S(2)}) collective-permute-start(bf16[272,128]{1,0:T(8,128)(2,1)S(1)} %get-tuple-element.37), channel_id=1, source_target_pairs={{0,8},{1,9},{2,10},{3,11},{8,0},{9,1},{10,2},{11,3},{4,12},{5,13},... | collective-permute-start | bytes 208904 | tf_op jit(solution)/shard_map/ppermute | solution.py:297
  5.0 8.5 %collective-permute-start.1 = (bf16[272,128]{1,0:T(8,128)(2,1)S(1)}, bf16[272,128]{1,0:T(8,128)(2,1)S(1)}, u32[]{:S(2)}, u32[]{:S(2)}) collective-permute-start(bf16[272,128]{1,0:T(8,128)(2,1)S(1)} %get-tuple-element.38), channel_id=1, source_target_pairs={{0,2},{1,3},{2,0},{3,1},{8,10},{9,11},{10,8},{11,9},{4,6},{5,7},{6... | collective-permute-start | bytes 208904 | tf_op jit(solution)/shard_map/ppermute | solution.py:297
  7.6 8.8 %collective-permute-start.2 = (bf16[272,128]{1,0:T(8,128)(2,1)S(1)}, bf16[272,128]{1,0:T(8,128)(2,1)S(1)}, u32[]{:S(2)}, u32[]{:S(2)}) collective-permute-start(bf16[272,128]{1,0:T(8,128)(2,1)S(1)} %get-tuple-element.39), channel_id=1, source_target_pairs={{0,11},{1,10},{2,9},{3,8},{8,3},{9,2},{10,1},{11,0},{4,15},{5,14},... | collective-permute-start | bytes 208904 | tf_op jit(solution)/shard_map/ppermute | solution.py:297
  8.9 7.6 %collective-permute-start.3 = (bf16[272,128]{1,0:T(8,128)(2,1)S(1)}, bf16[272,128]{1,0:T(8,128)(2,1)S(1)}, u32[]{:S(2)}, u32[]{:S(2)}) collective-permute-start(bf16[272,128]{1,0:T(8,128)(2,1)S(1)} %get-tuple-element.40), channel_id=1, source_target_pairs={{0,9},{1,8},{2,11},{3,10},{8,1},{9,0},{10,3},{11,2},{4,13},{5,12},... | collective-permute-start | bytes 208904 | tf_op jit(solution)/shard_map/ppermute | solution.py:297
  9.4 7.7 %collective-permute-start.4 = (bf16[272,128]{1,0:T(8,128)(2,1)S(1)}, bf16[272,128]{1,0:T(8,128)(2,1)S(1)}, u32[]{:S(2)}, u32[]{:S(2)}) collective-permute-start(bf16[272,128]{1,0:T(8,128)(2,1)S(1)} %get-tuple-element.41), channel_id=1, source_target_pairs={{0,1},{1,0},{2,3},{3,2},{8,9},{9,8},{10,11},{11,10},{4,5},{5,4},{6... | collective-permute-start | bytes 208904 | tf_op jit(solution)/shard_map/ppermute | solution.py:297
  11.9 8.3 %collective-permute-start.5 = (bf16[272,128]{1,0:T(8,128)(2,1)S(1)}, bf16[272,128]{1,0:T(8,128)(2,1)S(1)}, u32[]{:S(2)}, u32[]{:S(2)}) collective-permute-start(bf16[272,128]{1,0:T(8,128)(2,1)S(1)} %get-tuple-element.42), channel_id=1, source_target_pairs={{0,10},{1,11},{2,8},{3,9},{8,2},{9,3},{10,0},{11,1},{4,14},{5,15},... | collective-permute-start | bytes 208904 | tf_op jit(solution)/shard_map/ppermute | solution.py:297
  13.6 6.7 %collective-permute-start.6 = (bf16[272,128]{1,0:T(8,128)(2,1)S(1)}, bf16[272,128]{1,0:T(8,128)(2,1)S(1)}, u32[]{:S(2)}, u32[]{:S(2)}) collective-permute-start(bf16[272,128]{1,0:T(8,128)(2,1)S(1)} %get-tuple-element.43), channel_id=1, source_target_pairs={{0,3},{1,2},{2,1},{3,0},{8,11},{9,10},{10,9},{11,8},{4,7},{5,6},{6... | collective-permute-start | bytes 208904 | tf_op jit(solution)/shard_map/ppermute | solution.py:297
  16.4 1.3 %collective-permute-start.7 = (bf16[256,128]{1,0:T(8,128)(2,1)S(1)}, bf16[256,128]{1,0:T(8,128)(2,1)S(1)}, u32[]{:S(2)}, u32[]{:S(2)}) collective-permute-start(bf16[256,128]{1,0:T(8,128)(2,1)S(1)} %pad_maximum_fusion), channel_id=1, source_target_pairs={{0,4},{4,0},{1,5},{5,1},{2,6},{6,2},{3,7},{7,3},{8,12},{12,8},{9,1... | collective-permute-start | bytes 196616 | tf_op jit(solution)/shard_map/ppermute | solution.py:303
  16.5 1.4 %collective-permute-start.8 = (bf16[256,128]{1,0:T(8,128)(2,1)S(1)}, bf16[256,128]{1,0:T(8,128)(2,1)S(1)}, u32[]{:S(2)}, u32[]{:S(2)}) collective-permute-start(bf16[256,128]{1,0:T(8,128)(2,1)S(1)} %pad_maximum_fusion.1), channel_id=1, source_target_pairs={{0,4},{4,0},{1,5},{5,1},{2,6},{6,2},{3,7},{7,3},{8,12},{12,8},{9,1... | collective-permute-start | bytes 196616 | tf_op jit(solution)/shard_map/ppermute | solution.py:303
  17.1 1.3 %collective-permute-start.9 = (bf16[256,128]{1,0:T(8,128)(2,1)S(1)}, bf16[256,128]{1,0:T(8,128)(2,1)S(1)}, u32[]{:S(2)}, u32[]{:S(2)}) collective-permute-start(bf16[256,128]{1,0:T(8,128)(2,1)S(1)} %pad_maximum_fusion.2), channel_id=1, source_target_pairs={{0,4},{4,0},{1,5},{5,1},{2,6},{6,2},{3,7},{7,3},{8,12},{12,8},{9,1... | collective-permute-start | bytes 196616 | tf_op jit(solution)/shard_map/ppermute | solution.py:303
  20.2 1.3 %collective-permute-start.10 = (bf16[256,128]{1,0:T(8,128)(2,1)S(1)}, bf16[256,128]{1,0:T(8,128)(2,1)S(1)}, u32[]{:S(2)}, u32[]{:S(2)}) collective-permute-start(bf16[256,128]{1,0:T(8,128)(2,1)S(1)} %shard_map.96), channel_id=1, source_target_pairs={{0,4},{4,0},{1,5},{5,1},{2,6},{6,2},{3,7},{7,3},{8,12},{12,8},{9,1... | collective-permute-start | bytes 196616 | tf_op jit(solution)/shard_map/ppermute | solution.py:303
  23.0 1.6 %collective-permute-start.11 = (bf16[8,128,128]{2,1,0:T(8,128)(2,1)S(1)}, bf16[8,128,128]{2,1,0:T(8,128)(2,1)S(1)}, u32[]{:S(2)}, u32[]{:S(2)}) collective-permute-start(bf16[8,128,128]{2,1,0:T(8,128)(2,1)S(1)} %get-tuple-element.59), channel_id=1, source_target_pairs={{0,4},{4,0},{1,5},{5,1},{2,6},{6,2},{3,7},{7,3},{8,12},{12,8},{9,1... | collective-permute-start | bytes 786440 | tf_op jit(solution)/shard_map/ppermute | solution.py:310
  24.6 7.8 %collective-permute-start.12 = (bf16[192,128]{1,0:T(8,128)(2,1)S(1)}, bf16[192,128]{1,0:T(8,128)(2,1)S(1)}, u32[]{:S(2)}, u32[]{:S(2)}) collective-permute-start(bf16[192,128]{1,0:T(8,128)(2,1)S(1)} %get-tuple-element.62), channel_id=1, source_target_pairs={{0,3},{1,2},{2,1},{3,0},{8,11},{9,10},{10,9},{11,8},{4,7},{5,6},{6... | collective-permute-start | bytes 147464 | tf_op jit(solution)/shard_map/ppermute | solution.py:297
  27.0 7.1 %collective-permute-start.13 = (bf16[192,128]{1,0:T(8,128)(2,1)S(1)}, bf16[192,128]{1,0:T(8,128)(2,1)S(1)}, u32[]{:S(2)}, u32[]{:S(2)}) collective-permute-start(bf16[192,128]{1,0:T(8,128)(2,1)S(1)} %get-tuple-element.63), channel_id=1, source_target_pairs={{0,2},{1,3},{2,0},{3,1},{8,10},{9,11},{10,8},{11,9},{4,6},{5,7},{6... | collective-permute-start | bytes 147464 | tf_op jit(solution)/shard_map/ppermute | solution.py:297
  27.4 8.4 %collective-permute-start.14 = (bf16[192,128]{1,0:T(8,128)(2,1)S(1)}, bf16[192,128]{1,0:T(8,128)(2,1)S(1)}, u32[]{:S(2)}, u32[]{:S(2)}) collective-permute-start(bf16[192,128]{1,0:T(8,128)(2,1)S(1)} %get-tuple-element.64), channel_id=1, source_target_pairs={{0,10},{1,11},{2,8},{3,9},{8,2},{9,3},{10,0},{11,1},{4,14},{5,15},... | collective-permute-start | bytes 147464 | tf_op jit(solution)/shard_map/ppermute | solution.py:297
  31.0 6.9 %collective-permute-start.15 = (bf16[192,128]{1,0:T(8,128)(2,1)S(1)}, bf16[192,128]{1,0:T(8,128)(2,1)S(1)}, u32[]{:S(2)}, u32[]{:S(2)}) collective-permute-start(bf16[192,128]{1,0:T(8,128)(2,1)S(1)} %get-tuple-element.65), channel_id=1, source_target_pairs={{0,11},{1,10},{2,9},{3,8},{8,3},{9,2},{10,1},{11,0},{4,15},{5,14},... | collective-permute-start | bytes 147464 | tf_op jit(solution)/shard_map/ppermute | solution.py:297
  32.3 5.6 %collective-permute-start.16 = (bf16[192,128]{1,0:T(8,128)(2,1)S(1)}, bf16[192,128]{1,0:T(8,128)(2,1)S(1)}, u32[]{:S(2)}, u32[]{:S(2)}) collective-permute-start(bf16[192,128]{1,0:T(8,128)(2,1)S(1)} %get-tuple-element.66), channel_id=1, source_target_pairs={{0,9},{1,8},{2,11},{3,10},{8,1},{9,0},{10,3},{11,2},{4,13},{5,12},... | collective-permute-start | bytes 147464 | tf_op jit(solution)/shard_map/ppermute | solution.py:297
  32.5 5.5 %collective-permute-start.17 = (bf16[192,128]{1,0:T(8,128)(2,1)S(1)}, bf16[192,128]{1,0:T(8,128)(2,1)S(1)}, u32[]{:S(2)}, u32[]{:S(2)}) collective-permute-start(bf16[192,128]{1,0:T(8,128)(2,1)S(1)} %get-tuple-element.67), channel_id=1, source_target_pairs={{0,8},{1,9},{2,10},{3,11},{8,0},{9,1},{10,2},{11,3},{4,12},{5,13},... | collective-permute-start | bytes 147464 | tf_op jit(solution)/shard_map/ppermute | solution.py:297
  34.1 4.1 %collective-permute-start.18 = (bf16[192,128]{1,0:T(8,128)(2,1)S(1)}, bf16[192,128]{1,0:T(8,128)(2,1)S(1)}, u32[]{:S(2)}, u32[]{:S(2)}) collective-permute-start(bf16[192,128]{1,0:T(8,128)(2,1)S(1)} %get-tuple-element.68), channel_id=1, source_target_pairs={{0,1},{1,0},{2,3},{3,2},{8,9},{9,8},{10,11},{11,10},{4,5},{5,4},{6... | collective-permute-start | bytes 147464 | tf_op jit(solution)/shard_map/ppermute | solution.py:297

commit v6 on v5

--- a/solution.py
+++ b/solution.py
@@ -32,7 +32,7 @@
     home = max(0, contact_count - (shares - 1) * HEADS)
     late = len(LATE) * (shares - 1 if home >= len(LATE) else shares)
     away = contact_count - home
-    return max(0, away - late), away, away + home // 2, contact_count
+    return max(0, away - late), away, away + home // 4, contact_count
 
 
 def number():
@@ -210,11 +210,14 @@
 def first_kernel(sizes, *rest):
     rows = rest[:HEADS]
     kv, kt, weights, total, dq = rest[HEADS + 5 :]
-    _, start, end, _ = contact_plan(sizes)
+    first, start, end, _ = contact_plan(sizes)
     lists = lists_of(rows)
     for s, row in zip(LATE, rows[len(EARLY) :]):
         fill_own(kv, kt, weights, s, row)
-    jobs = [(rows[n], weights.at[s], [lists[n, i] for i in range(start, end)]) for n, s in enumerate(EARLY + LATE)]
+    jobs = []
+    for n, s in enumerate(EARLY + LATE):
+        places = list(range(start, end)) + list(range(first if s in LATE else 0))
+        jobs.append((rows[n], weights.at[s], [lists[n, i] for i in places]))
     for s, part in zip(EARLY + LATE, run(jobs, kv, kt, total)):
         dq[s] += part
 
@@ -225,10 +228,7 @@
     start, end, _, _ = contact_plan(sizes)
     lists = lists_of(rows)
     fill_other(kv, kt, LATE, other_ref)
-    jobs = []
-    for n, s in enumerate(EARLY + LATE):
-        first = start if s in EARLY else 0
-        jobs.append((rows[n], weights.at[s], [lists[n, i] for i in range(first, end)]))
+    jobs = [(rows[n], weights.at[s], [lists[n, i] for i in range(start, end)]) for n, s in enumerate(EARLY + LATE)]
     for s, part in zip(EARLY + LATE, run(jobs, kv, kt, total)):
         dq[s] += part
     final = final_scale()
@@ -380,14 +380,14 @@
         lambda *refs: first_kernel(sizes, *refs),
         held,
         [VMEM] * (HEADS + 5),
-        tiles=HEADS * (plan[2] - plan[1]) + 12,
+        tiles=HEADS * (plan[2] - plan[1]) + len(LATE) * plan[0],
         aliases={HEADS + n: n for n in range(5)},
     )(*early, *late, kv, kt, weights, total, dq)
     kv, kt, total, dq, theirs = call(
         lambda *refs: second_kernel(sizes, *refs),
         [held[0], held[1], held[3], held[4], ((count - HEADS, BLOCK, LANES), bf16)],
         [VMEM] * (HEADS + 6),
-        tiles=HEADS * (plan[1] - plan[0]) + len(LATE) * plan[0],
+        tiles=HEADS * (plan[1] - plan[0]),
         aliases={HEADS + 1: 0, HEADS + 2: 1, HEADS + 4: 2, HEADS + 5: 3},
     )(*early, *late, other, kv, kt, weights, total, dq)
     arrived = sum_shares(theirs, shares, share)

time: 39.3 us -> 39.1 us (level)
  waiting for transfers between devices: 4.93 us -> 4.3 us
    pallas_call x1, Pallas kernels: 1.38 us -> 0.91 us  [body(): call(lambda *refs: second_kernel(sizes, *refs), [held[0], held[1], held[3...]
    pallas_call x1, Pallas kernels: 0.94 us -> 1.41 us  [body(): call(lambda *refs: third_kernel(sizes, *refs), [((HEADS, BLOCK, LANES), f...]
    ppermute x1, waiting for transfers between devices: 0.42 us -> 0.01 us  [sum_shares(): return lax.ppermute(theirs, 'share', [(0, 1), (1, 0)])]
  transfers between devices with their start and end apart: 19 -> 19, of which waited for: 8 -> 6; matrix products, arithmetic and copies ran while one was open for 0% -> 0% of each run, Pallas kernels for 9% -> 11%
where the time goes in v6:
time: 39.1 us; the launch traced here: 38.9 us
  starting transfers between devices  26.2 us (67%)
  Pallas kernels  7.62 us (19%)
  waiting for transfers between devices  4.3 us (11%)
  between operations  0.78 us (2%)
    ppermute x14, starting transfers between devices, exchange(): moved[s] = lax.ppermute(parts[s], ('across', 'col'), pairs)  24.8 us
    ppermute x14, waiting for transfers between devices, exchange(): moved[s] = lax.ppermute(parts[s], ('across', 'col'), pairs)  3.07 us
    pallas_call x1, Pallas kernels, body(): call(lambda *refs: early_kernel(sizes, *refs), held, [VMEM] * (len(EARLY)...  1.79 us
    pallas_call x1, Pallas kernels, body(): call(lambda *refs: third_kernel(sizes, *refs), [((HEADS, BLOCK, LANES), f...  1.41 us
    pallas_call x1, Pallas kernels, body(): call(lambda *refs: pack_kernel(sizes, *refs), [((length, LANES), bf16)] *...  1.39 us
    ppermute x4, waiting for transfers between devices, gather_keys(): return lax.ppermute(own, 'share', [(0, 1), (1, 0)])  1.22 us
    pallas_call x1, Pallas kernels, body(): call(lambda *refs: first_kernel(sizes, *refs), held, [VMEM] * (HEADS + 5)...  1.16 us
    ppermute x4, starting transfers between devices, gather_keys(): return lax.ppermute(own, 'share', [(0, 1), (1, 0)])  0.94 us
  transfers between devices with their start and end apart: 19, of which 6 were waited for; matrix products, arithmetic and copies ran while one was open for 0% of the time, Pallas kernels for 11%

profile of v6, /device:TPU:0, one launch (start us, length us, event | category | flops | bytes accessed | tf_op | source)
XLA Modules:
  0.0 38.9 jit_solution(16184401168504117750)
XLA Ops:
  0.6 1.4 %shard_map.94 = (bf16[272,128]{1,0:T(8,128)(2,1)S(1)}, bf16[272,128]{1,0:T(8,128)(2,1)S(1)}, bf16[272,128]{1,0:T(8,128)(2,1)S(1)}, bf16[272,128]{1,0:T(8,128)(2,...) custom-call(s32[4,12]{1,0:T(4,128)} %refs_0_.1, ...), custom_call_target="tpu_custom_call" | custom-call | tf_op jit(solution)/shard_map/pallas_call | solution.py:348
  2.0 3.0 %collective-permute-start = (bf16[272,128]{1,0:T(8,128)(2,1)S(1)}, bf16[272,128]{1,0:T(8,128)(2,1)S(1)}, u32[]{:S(2)}, u32[]{:S(2)}) collective-permute-start(bf16[272,128]{1,0:T(8,128)(2,1)S(1)} %get-tuple-element.37), channel_id=1, source_target_pairs={{0,8},{1,9},{2,10},{3,11},{8,0},{9,1},{10,2},{11,3},{4,12},{5,13},... | collective-permute-start | bytes 208904 | tf_op jit(solution)/shard_map/ppermute | solution.py:297
  5.0 2.6 %collective-permute-start.1 = (bf16[272,128]{1,0:T(8,128)(2,1)S(1)}, bf16[272,128]{1,0:T(8,128)(2,1)S(1)}, u32[]{:S(2)}, u32[]{:S(2)}) collective-permute-start(bf16[272,128]{1,0:T(8,128)(2,1)S(1)} %get-tuple-element.38), channel_id=1, source_target_pairs={{0,2},{1,3},{2,0},{3,1},{8,10},{9,11},{10,8},{11,9},{4,6},{5,7},{6... | collective-permute-start | bytes 208904 | tf_op jit(solution)/shard_map/ppermute | solution.py:297
  7.6 1.3 %collective-permute-start.2 = (bf16[272,128]{1,0:T(8,128)(2,1)S(1)}, bf16[272,128]{1,0:T(8,128)(2,1)S(1)}, u32[]{:S(2)}, u32[]{:S(2)}) collective-permute-start(bf16[272,128]{1,0:T(8,128)(2,1)S(1)} %get-tuple-element.39), channel_id=1, source_target_pairs={{0,11},{1,10},{2,9},{3,8},{8,3},{9,2},{10,1},{11,0},{4,15},{5,14},... | collective-permute-start | bytes 208904 | tf_op jit(solution)/shard_map/ppermute | solution.py:297
  8.9 0.5 %collective-permute-start.3 = (bf16[272,128]{1,0:T(8,128)(2,1)S(1)}, bf16[272,128]{1,0:T(8,128)(2,1)S(1)}, u32[]{:S(2)}, u32[]{:S(2)}) collective-permute-start(bf16[272,128]{1,0:T(8,128)(2,1)S(1)} %get-tuple-element.40), channel_id=1, source_target_pairs={{0,9},{1,8},{2,11},{3,10},{8,1},{9,0},{10,3},{11,2},{4,13},{5,12},... | collective-permute-start | bytes 208904 | tf_op jit(solution)/shard_map/ppermute | solution.py:297
  9.4 2.5 %collective-permute-start.4 = (bf16[272,128]{1,0:T(8,128)(2,1)S(1)}, bf16[272,128]{1,0:T(8,128)(2,1)S(1)}, u32[]{:S(2)}, u32[]{:S(2)}) collective-permute-start(bf16[272,128]{1,0:T(8,128)(2,1)S(1)} %get-tuple-element.41), channel_id=1, source_target_pairs={{0,1},{1,0},{2,3},{3,2},{8,9},{9,8},{10,11},{11,10},{4,5},{5,4},{6... | collective-permute-start | bytes 208904 | tf_op jit(solution)/shard_map/ppermute | solution.py:297
  11.9 1.7 %collective-permute-start.5 = (bf16[272,128]{1,0:T(8,128)(2,1)S(1)}, bf16[272,128]{1,0:T(8,128)(2,1)S(1)}, u32[]{:S(2)}, u32[]{:S(2)}) collective-permute-start(bf16[272,128]{1,0:T(8,128)(2,1)S(1)} %get-tuple-element.42), channel_id=1, source_target_pairs={{0,10},{1,11},{2,8},{3,9},{8,2},{9,3},{10,0},{11,1},{4,14},{5,15},... | collective-permute-start | bytes 208904 | tf_op jit(solution)/shard_map/ppermute | solution.py:297
  13.6 2.8 %collective-permute-start.6 = (bf16[272,128]{1,0:T(8,128)(2,1)S(1)}, bf16[272,128]{1,0:T(8,128)(2,1)S(1)}, u32[]{:S(2)}, u32[]{:S(2)}) collective-permute-start(bf16[272,128]{1,0:T(8,128)(2,1)S(1)} %get-tuple-element.43), channel_id=1, source_target_pairs={{0,3},{1,2},{2,1},{3,0},{8,11},{9,10},{10,9},{11,8},{4,7},{5,6},{6... | collective-permute-start | bytes 208904 | tf_op jit(solution)/shard_map/ppermute | solution.py:297
  16.5 0.5 %collective-permute-start.8 = (bf16[256,128]{1,0:T(8,128)(2,1)S(1)}, bf16[256,128]{1,0:T(8,128)(2,1)S(1)}, u32[]{:S(2)}, u32[]{:S(2)}) collective-permute-start(bf16[256,128]{1,0:T(8,128)(2,1)S(1)} %pad_maximum_fusion.1), channel_id=1, source_target_pairs={{0,4},{4,0},{1,5},{5,1},{2,6},{6,2},{3,7},{7,3},{8,12},{12,8},{9,1... | collective-permute-start | bytes 196616 | tf_op jit(solution)/shard_map/ppermute | solution.py:303
  17.2 0.5 %collective-permute-done.7.refs_6_ = bf16[256,128]{1,0:T(8,128)(2,1)S(1)} collective-permute-done((bf16[256,128]{1,0:T(8,128)(2,1)S(1)}, bf16[256,128]{1,0:T(8,128)(2,1)S(1)}, u32[]{:S(2)}, u32[]{:S(2)}) %collective-permute-start.7) | collective-permute-done | bytes 65568 | tf_op jit(solution)/shard_map/ppermute | solution.py:303
  18.0 0.4 %collective-permute-done.9.refs_8_ = bf16[256,128]{1,0:T(8,128)(2,1)S(1)} collective-permute-done((bf16[256,128]{1,0:T(8,128)(2,1)S(1)}, bf16[256,128]{1,0:T(8,128)(2,1)S(1)}, u32[]{:S(2)}, u32[]{:S(2)}) %collective-permute-start.9) | collective-permute-done | bytes 65568 | tf_op jit(solution)/shard_map/ppermute | solution.py:303
  18.4 1.8 %shard_map.95 = (bf16[16,128,128]{2,1,0:T(8,128)(2,1)S(1)}, bf16[16,64,128]{2,1,0:T(8,128)(2,1)S(1)}, bf16[8,256,128]{2,1,0:T(8,128)(2,1)S(1)}, f32[16,128,128]{2,1,0:T(8,128)S(1)}, f32[8,64,128]{2,1,0:T(8,128)S(1)}) custom-call(bf16[272,128]{1,0:T(8,128)(2,1)S(1)} %get-tuple-element.36.refs_0_, bf16[272,128]{1,0:T(8,128)(2,1)S(1)} %collective-permute-done.refs_1_, ...), custom_call_target="tpu_custom_call" | custom-call | tf_op jit(solution)/shard_map/pallas_call | solution.py:372
  20.5 1.2 %shard_map.97 = (bf16[16,128,128]{2,1,0:T(8,128)(2,1)S(1)}, bf16[16,64,128]{2,1,0:T(8,128)(2,1)S(1)}, bf16[8,256,128]{2,1,0:T(8,128)(2,1)S(1)}, f32[16,128,128]{2,1,0:T(8,128)S(1)}, f32[8,64,128]{2,1,0:T(8,128)S(1)}) custom-call(bf16[272,128]{1,0:T(8,128)(2,1)S(1)} %get-tuple-element.3, ...), custom_call_target="tpu_custom_call", output_to_operand_aliasing={{0}: (8, {}), {1}: (9, {}), {2}: (10, {}), {3}: (11, {}), {... | custom-call | flops 209715200 | bytes 327680 | tf_op jit(solution)/shard_map/pallas_call | solution.py:379
  21.6 0.9 %shard_map.98 = (bf16[16,128,128]{2,1,0:T(8,128)(2,1)S(1)}, bf16[16,64,128]{2,1,0:T(8,128)(2,1)S(1)}, f32[16,128,128]{2,1,0:T(8,128)S(1)}, f32[8,64,128]{2,1,0:T(8,128)S(1)}, bf16[8,128,128]{2,1,0:T(8,128)(2,1)S(1)}) custom-call(bf16[272,128]{1,0:T(8,128)(2,1)S(1)} %get-tuple-element.36.re, ...), custom_call_target="tpu_custom_call", output_to_operand_aliasing={{0}: (9, {}), {1}: (10, {}), {2}: (12, {}), {3}: (13, {})} | custom-call | flops 167772160 | bytes 262144 | tf_op jit(solution)/shard_map/pallas_call | solution.py:386
  23.0 1.4 %shard_map.99 = (f32[8,128,128]{2,1,0:T(8,128)S(1)}, bf16[8,64,128]{2,1,0:T(8,128)(2,1)S(1)}) custom-call(bf16[272,128]{1,0:T(8,128)(2,1)S(1)} %get-tuple-element.36.refs_0_, bf16[272,128]{1,0:T(8,128)(2,1)S(1)} %collective-permute-done.refs_1_, bf16[272,128]{1,0:T(8,128)(2,1)S(1)} %collective-permute-done.1.refs_2_, ...), custom_call_target="tpu_custom_call" | custom-call | flops 262144000 | bytes 409600 | tf_op jit(solution)/shard_map/pallas_call | solution.py:394
  24.5 2.3 %collective-permute-start.12 = (bf16[192,128]{1,0:T(8,128)(2,1)S(1)}, bf16[192,128]{1,0:T(8,128)(2,1)S(1)}, u32[]{:S(2)}, u32[]{:S(2)}) collective-permute-start(bf16[192,128]{1,0:T(8,128)(2,1)S(1)} %get-tuple-element.62), channel_id=1, source_target_pairs={{0,3},{1,2},{2,1},{3,0},{8,11},{9,10},{10,9},{11,8},{4,7},{5,6},{6... | collective-permute-start | bytes 147464 | tf_op jit(solution)/shard_map/ppermute | solution.py:297
  26.8 0.4 %collective-permute-start.13 = (bf16[192,128]{1,0:T(8,128)(2,1)S(1)}, bf16[192,128]{1,0:T(8,128)(2,1)S(1)}, u32[]{:S(2)}, u32[]{:S(2)}) collective-permute-start(bf16[192,128]{1,0:T(8,128)(2,1)S(1)} %get-tuple-element.63), channel_id=1, source_target_pairs={{0,2},{1,3},{2,0},{3,1},{8,10},{9,11},{10,8},{11,9},{4,6},{5,7},{6... | collective-permute-start | bytes 147464 | tf_op jit(solution)/shard_map/ppermute | solution.py:297
  27.3 3.6 %collective-permute-start.14 = (bf16[192,128]{1,0:T(8,128)(2,1)S(1)}, bf16[192,128]{1,0:T(8,128)(2,1)S(1)}, u32[]{:S(2)}, u32[]{:S(2)}) collective-permute-start(bf16[192,128]{1,0:T(8,128)(2,1)S(1)} %get-tuple-element.64), channel_id=1, source_target_pairs={{0,10},{1,11},{2,8},{3,9},{8,2},{9,3},{10,0},{11,1},{4,14},{5,15},... | collective-permute-start | bytes 147464 | tf_op jit(solution)/shard_map/ppermute | solution.py:297
  30.8 1.3 %collective-permute-start.15 = (bf16[192,128]{1,0:T(8,128)(2,1)S(1)}, bf16[192,128]{1,0:T(8,128)(2,1)S(1)}, u32[]{:S(2)}, u32[]{:S(2)}) collective-permute-start(bf16[192,128]{1,0:T(8,128)(2,1)S(1)} %get-tuple-element.65), channel_id=1, source_target_pairs={{0,11},{1,10},{2,9},{3,8},{8,3},{9,2},{10,1},{11,0},{4,15},{5,14},... | collective-permute-start | bytes 147464 | tf_op jit(solution)/shard_map/ppermute | solution.py:297
  32.3 0.9 %collective-permute-start.17 = (bf16[192,128]{1,0:T(8,128)(2,1)S(1)}, bf16[192,128]{1,0:T(8,128)(2,1)S(1)}, u32[]{:S(2)}, u32[]{:S(2)}) collective-permute-start(bf16[192,128]{1,0:T(8,128)(2,1)S(1)} %get-tuple-element.67), channel_id=1, source_target_pairs={{0,8},{1,9},{2,10},{3,11},{8,0},{9,1},{10,2},{11,3},{4,12},{5,13},... | collective-permute-start | bytes 147464 | tf_op jit(solution)/shard_map/ppermute | solution.py:297
  33.2 0.7 %collective-permute-done.13.rest_2_ = bf16[192,128]{1,0:T(8,128)(2,1)S(1)} collective-permute-done((bf16[192,128]{1,0:T(8,128)(2,1)S(1)}, bf16[192,128]{1,0:T(8,128)(2,1)S(1)}, u32[]{:S(2)}, u32[]{:S(2)}) %collective-permute-start.13) | collective-permute-done | bytes 49184 | tf_op jit(solution)/shard_map/ppermute | solution.py:297
  33.9 1.8 %collective-permute-start.18 = (bf16[192,128]{1,0:T(8,128)(2,1)S(1)}, bf16[192,128]{1,0:T(8,128)(2,1)S(1)}, u32[]{:S(2)}, u32[]{:S(2)}) collective-permute-start(bf16[192,128]{1,0:T(8,128)(2,1)S(1)} %get-tuple-element.68), channel_id=1, source_target_pairs={{0,1},{1,0},{2,3},{3,2},{8,9},{9,8},{10,11},{11,10},{4,5},{5,4},{6... | collective-permute-start | bytes 147464 | tf_op jit(solution)/shard_map/ppermute | solution.py:297
  35.7 2.0 %collective-permute-done.15.rest_4_ = bf16[192,128]{1,0:T(8,128)(2,1)S(1)} collective-permute-done((bf16[192,128]{1,0:T(8,128)(2,1)S(1)}, bf16[192,128]{1,0:T(8,128)(2,1)S(1)}, u32[]{:S(2)}, u32[]{:S(2)}) %collective-permute-start.15) | collective-permute-done | bytes 49184 | tf_op jit(solution)/shard_map/ppermute | solution.py:297
  38.0 0.9 %shard_map.101 = (bf16[128,512]{1,0:T(8,128)(2,1)}, bf16[128,512]{1,0:T(8,128)(2,1)}, bf16[128,512]{1,0:T(8,128)(2,1)}) custom-call(bf16[192,128]{1,0:T(8,128)(2,1)S(1)} %get-tuple-element.61.rest_0_, bf16[192,128]{1,0:T(8,128)(2,1)S(1)} %collective-permute-done.12.rest_1_, bf16[192,128]{1,0:T(8,128)(2,1)S(1)} %collective-permute-done.13.rest_2_, ...), custom_call_target="tpu_custom_call" | custom-call | tf_op jit(solution)/shard_map/pallas_call | solution.py:407
  (31 shorter events, 1.6 us)
Async XLA Ops:
  2.0 9.9 %collective-permute-start = (bf16[272,128]{1,0:T(8,128)(2,1)S(1)}, bf16[272,128]{1,0:T(8,128)(2,1)S(1)}, u32[]{:S(2)}, u32[]{:S(2)}) collective-permute-start(bf16[272,128]{1,0:T(8,128)(2,1)S(1)} %get-tuple-element.37), channel_id=1, source_target_pairs={{0,8},{1,9},{2,10},{3,11},{8,0},{9,1},{10,2},{11,3},{4,12},{5,13},... | collective-permute-start | bytes 208904 | tf_op jit(solution)/shard_map/ppermute | solution.py:297
  5.0 8.5 %collective-permute-start.1 = (bf16[272,128]{1,0:T(8,128)(2,1)S(1)}, bf16[272,128]{1,0:T(8,128)(2,1)S(1)}, u32[]{:S(2)}, u32[]{:S(2)}) collective-permute-start(bf16[272,128]{1,0:T(8,128)(2,1)S(1)} %get-tuple-element.38), channel_id=1, source_target_pairs={{0,2},{1,3},{2,0},{3,1},{8,10},{9,11},{10,8},{11,9},{4,6},{5,7},{6... | collective-permute-start | bytes 208904 | tf_op jit(solution)/shard_map/ppermute | solution.py:297
  7.6 8.8 %collective-permute-start.2 = (bf16[272,128]{1,0:T(8,128)(2,1)S(1)}, bf16[272,128]{1,0:T(8,128)(2,1)S(1)}, u32[]{:S(2)}, u32[]{:S(2)}) collective-permute-start(bf16[272,128]{1,0:T(8,128)(2,1)S(1)} %get-tuple-element.39), channel_id=1, source_target_pairs={{0,11},{1,10},{2,9},{3,8},{8,3},{9,2},{10,1},{11,0},{4,15},{5,14},... | collective-permute-start | bytes 208904 | tf_op jit(solution)/shard_map/ppermute | solution.py:297
  8.9 7.6 %collective-permute-start.3 = (bf16[272,128]{1,0:T(8,128)(2,1)S(1)}, bf16[272,128]{1,0:T(8,128)(2,1)S(1)}, u32[]{:S(2)}, u32[]{:S(2)}) collective-permute-start(bf16[272,128]{1,0:T(8,128)(2,1)S(1)} %get-tuple-element.40), channel_id=1, source_target_pairs={{0,9},{1,8},{2,11},{3,10},{8,1},{9,0},{10,3},{11,2},{4,13},{5,12},... | collective-permute-start | bytes 208904 | tf_op jit(solution)/shard_map/ppermute | solution.py:297
  9.4 7.7 %collective-permute-start.4 = (bf16[272,128]{1,0:T(8,128)(2,1)S(1)}, bf16[272,128]{1,0:T(8,128)(2,1)S(1)}, u32[]{:S(2)}, u32[]{:S(2)}) collective-permute-start(bf16[272,128]{1,0:T(8,128)(2,1)S(1)} %get-tuple-element.41), channel_id=1, source_target_pairs={{0,1},{1,0},{2,3},{3,2},{8,9},{9,8},{10,11},{11,10},{4,5},{5,4},{6... | collective-permute-start | bytes 208904 | tf_op jit(solution)/shard_map/ppermute | solution.py:297
  11.9 8.3 %collective-permute-start.5 = (bf16[272,128]{1,0:T(8,128)(2,1)S(1)}, bf16[272,128]{1,0:T(8,128)(2,1)S(1)}, u32[]{:S(2)}, u32[]{:S(2)}) collective-permute-start(bf16[272,128]{1,0:T(8,128)(2,1)S(1)} %get-tuple-element.42), channel_id=1, source_target_pairs={{0,10},{1,11},{2,8},{3,9},{8,2},{9,3},{10,0},{11,1},{4,14},{5,15},... | collective-permute-start | bytes 208904 | tf_op jit(solution)/shard_map/ppermute | solution.py:297
  13.6 6.7 %collective-permute-start.6 = (bf16[272,128]{1,0:T(8,128)(2,1)S(1)}, bf16[272,128]{1,0:T(8,128)(2,1)S(1)}, u32[]{:S(2)}, u32[]{:S(2)}) collective-permute-start(bf16[272,128]{1,0:T(8,128)(2,1)S(1)} %get-tuple-element.43), channel_id=1, source_target_pairs={{0,3},{1,2},{2,1},{3,0},{8,11},{9,10},{10,9},{11,8},{4,7},{5,6},{6... | collective-permute-start | bytes 208904 | tf_op jit(solution)/shard_map/ppermute | solution.py:297
  16.4 1.3 %collective-permute-start.7 = (bf16[256,128]{1,0:T(8,128)(2,1)S(1)}, bf16[256,128]{1,0:T(8,128)(2,1)S(1)}, u32[]{:S(2)}, u32[]{:S(2)}) collective-permute-start(bf16[256,128]{1,0:T(8,128)(2,1)S(1)} %pad_maximum_fusion), channel_id=1, source_target_pairs={{0,4},{4,0},{1,5},{5,1},{2,6},{6,2},{3,7},{7,3},{8,12},{12,8},{9,1... | collective-permute-start | bytes 196616 | tf_op jit(solution)/shard_map/ppermute | solution.py:303
  16.5 1.4 %collective-permute-start.8 = (bf16[256,128]{1,0:T(8,128)(2,1)S(1)}, bf16[256,128]{1,0:T(8,128)(2,1)S(1)}, u32[]{:S(2)}, u32[]{:S(2)}) collective-permute-start(bf16[256,128]{1,0:T(8,128)(2,1)S(1)} %pad_maximum_fusion.1), channel_id=1, source_target_pairs={{0,4},{4,0},{1,5},{5,1},{2,6},{6,2},{3,7},{7,3},{8,12},{12,8},{9,1... | collective-permute-start | bytes 196616 | tf_op jit(solution)/shard_map/ppermute | solution.py:303
  17.1 1.3 %collective-permute-start.9 = (bf16[256,128]{1,0:T(8,128)(2,1)S(1)}, bf16[256,128]{1,0:T(8,128)(2,1)S(1)}, u32[]{:S(2)}, u32[]{:S(2)}) collective-permute-start(bf16[256,128]{1,0:T(8,128)(2,1)S(1)} %pad_maximum_fusion.2), channel_id=1, source_target_pairs={{0,4},{4,0},{1,5},{5,1},{2,6},{6,2},{3,7},{7,3},{8,12},{12,8},{9,1... | collective-permute-start | bytes 196616 | tf_op jit(solution)/shard_map/ppermute | solution.py:303
  20.2 1.4 %collective-permute-start.10 = (bf16[256,128]{1,0:T(8,128)(2,1)S(1)}, bf16[256,128]{1,0:T(8,128)(2,1)S(1)}, u32[]{:S(2)}, u32[]{:S(2)}) collective-permute-start(bf16[256,128]{1,0:T(8,128)(2,1)S(1)} %shard_map.96), channel_id=1, source_target_pairs={{0,4},{4,0},{1,5},{5,1},{2,6},{6,2},{3,7},{7,3},{8,12},{12,8},{9,1... | collective-permute-start | bytes 196616 | tf_op jit(solution)/shard_map/ppermute | solution.py:303
  22.6 1.8 %collective-permute-start.11 = (bf16[8,128,128]{2,1,0:T(8,128)(2,1)S(1)}, bf16[8,128,128]{2,1,0:T(8,128)(2,1)S(1)}, u32[]{:S(2)}, u32[]{:S(2)}) collective-permute-start(bf16[8,128,128]{2,1,0:T(8,128)(2,1)S(1)} %get-tuple-element.59), channel_id=1, source_target_pairs={{0,4},{4,0},{1,5},{5,1},{2,6},{6,2},{3,7},{7,3},{8,12},{12,8},{9,1... | collective-permute-start | bytes 786440 | tf_op jit(solution)/shard_map/ppermute | solution.py:310
  24.5 7.8 %collective-permute-start.12 = (bf16[192,128]{1,0:T(8,128)(2,1)S(1)}, bf16[192,128]{1,0:T(8,128)(2,1)S(1)}, u32[]{:S(2)}, u32[]{:S(2)}) collective-permute-start(bf16[192,128]{1,0:T(8,128)(2,1)S(1)} %get-tuple-element.62), channel_id=1, source_target_pairs={{0,3},{1,2},{2,1},{3,0},{8,11},{9,10},{10,9},{11,8},{4,7},{5,6},{6... | collective-permute-start | bytes 147464 | tf_op jit(solution)/shard_map/ppermute | solution.py:297
  26.8 7.1 %collective-permute-start.13 = (bf16[192,128]{1,0:T(8,128)(2,1)S(1)}, bf16[192,128]{1,0:T(8,128)(2,1)S(1)}, u32[]{:S(2)}, u32[]{:S(2)}) collective-permute-start(bf16[192,128]{1,0:T(8,128)(2,1)S(1)} %get-tuple-element.63), channel_id=1, source_target_pairs={{0,2},{1,3},{2,0},{3,1},{8,10},{9,11},{10,8},{11,9},{4,6},{5,7},{6... | collective-permute-start | bytes 147464 | tf_op jit(solution)/shard_map/ppermute | solution.py:297
  27.3 8.4 %collective-permute-start.14 = (bf16[192,128]{1,0:T(8,128)(2,1)S(1)}, bf16[192,128]{1,0:T(8,128)(2,1)S(1)}, u32[]{:S(2)}, u32[]{:S(2)}) collective-permute-start(bf16[192,128]{1,0:T(8,128)(2,1)S(1)} %get-tuple-element.64), channel_id=1, source_target_pairs={{0,10},{1,11},{2,8},{3,9},{8,2},{9,3},{10,0},{11,1},{4,14},{5,15},... | collective-permute-start | bytes 147464 | tf_op jit(solution)/shard_map/ppermute | solution.py:297
  30.8 6.9 %collective-permute-start.15 = (bf16[192,128]{1,0:T(8,128)(2,1)S(1)}, bf16[192,128]{1,0:T(8,128)(2,1)S(1)}, u32[]{:S(2)}, u32[]{:S(2)}) collective-permute-start(bf16[192,128]{1,0:T(8,128)(2,1)S(1)} %get-tuple-element.65), channel_id=1, source_target_pairs={{0,11},{1,10},{2,9},{3,8},{8,3},{9,2},{10,1},{11,0},{4,15},{5,14},... | collective-permute-start | bytes 147464 | tf_op jit(solution)/shard_map/ppermute | solution.py:297
  32.2 5.6 %collective-permute-start.16 = (bf16[192,128]{1,0:T(8,128)(2,1)S(1)}, bf16[192,128]{1,0:T(8,128)(2,1)S(1)}, u32[]{:S(2)}, u32[]{:S(2)}) collective-permute-start(bf16[192,128]{1,0:T(8,128)(2,1)S(1)} %get-tuple-element.66), channel_id=1, source_target_pairs={{0,9},{1,8},{2,11},{3,10},{8,1},{9,0},{10,3},{11,2},{4,13},{5,12},... | collective-permute-start | bytes 147464 | tf_op jit(solution)/shard_map/ppermute | solution.py:297
  32.3 5.4 %collective-permute-start.17 = (bf16[192,128]{1,0:T(8,128)(2,1)S(1)}, bf16[192,128]{1,0:T(8,128)(2,1)S(1)}, u32[]{:S(2)}, u32[]{:S(2)}) collective-permute-start(bf16[192,128]{1,0:T(8,128)(2,1)S(1)} %get-tuple-element.67), channel_id=1, source_target_pairs={{0,8},{1,9},{2,10},{3,11},{8,0},{9,1},{10,2},{11,3},{4,12},{5,13},... | collective-permute-start | bytes 147464 | tf_op jit(solution)/shard_map/ppermute | solution.py:297
  33.9 4.1 %collective-permute-start.18 = (bf16[192,128]{1,0:T(8,128)(2,1)S(1)}, bf16[192,128]{1,0:T(8,128)(2,1)S(1)}, u32[]{:S(2)}, u32[]{:S(2)}) collective-permute-start(bf16[192,128]{1,0:T(8,128)(2,1)S(1)} %get-tuple-element.68), channel_id=1, source_target_pairs={{0,1},{1,0},{2,3},{3,2},{8,9},{9,8},{10,11},{11,10},{4,5},{5,4},{6... | collective-permute-start | bytes 147464 | tf_op jit(solution)/shard_map/ppermute | solution.py:297
